TPU v7x, 32 devices: a whole 2x2x4 slice. The times are simulated.
32 devices in a mesh: row: 8 (over y, x, core), col: 4 (over z).
Axes of the slice: x: 2, y: 2, z: 4, core: 2. Of those that a mesh axis runs over, the one named last changes fastest.
Arguments:
- features: bfloat16 [64, 64, 512], P('row', 'col'), may hold values from -6 to 6
- conv_first: bfloat16 [3, 3, 512, 512], replicated, may hold values from -0.25 to 0.25
- conv_second: bfloat16 [3, 3, 512, 512], replicated, may hold values from -0.09375 to 0.09375
- conv_last: bfloat16 [3, 3, 512, 16], replicated, may hold values from -0.25 to 0.25
- noise: bfloat16 [1024, 64], P(('row', 'col')), may hold values from -6 to 6
- prior_patches: bfloat16 [1024, 3, 64], P(('row', 'col')), may hold values from -6 to 6
- step_index: int32 [4], replicated, may hold values from 0 to 3
- mod_table: float32 [4, 3, 3072], replicated, may hold values from -3 to 3
- embed_weight: bfloat16 [64, 3072], replicated, may hold values from -0.75 to 0.75
- qkv_weight: bfloat16 [3072, 9216], P(None, 'col')
- q_gain: float32 [128], replicated, may hold values from 0.5 to 5
- k_gain: float32 [128], replicated, may hold values from 0.5 to 5
- out_weight: bfloat16 [3072, 3072], P('col'), may hold values from -0.109375 to 0.109375
Outputs:
- block_out: bfloat16 [1024, 4, 3072], P(('row', 'col'))
All inputs are finite; a program needn't handle non-finite values.
Results may differ from a plain program's by a relative error of at most 0.017.
Values may be sent and summed in bfloat16 or wider, within the bound.
No kernel may reach another device: no remote copies, remote signals or barrier semaphores. Data moves between devices by JAX's collectives and lax.ppermute only.
A program may use at most 192 MiB of HBM per device.

v0:
```python
import math

import jax
import jax.numpy as jnp
from jax import lax
from jax.sharding import PartitionSpec as P

norm_eps = 1e-06
latent_shift = 0.1159
latent_scale = 0.3611
far_negative = -1e30


def padded(cells, sides, width):
    for axis, dim in sides:
        count = lax.axis_size(axis)
        ends = count - 1
        head = lax.slice_in_dim(cells, 0, width, axis=dim)
        tail = lax.slice_in_dim(cells, cells.shape[dim] - width, cells.shape[dim], axis=dim)
        cells = jnp.concatenate(
            [
                lax.ppermute(tail, axis, [(i, (i + 1) % count) for i in range(ends)]),
                cells,
                lax.ppermute(head, axis, [((i + 1) % count, i) for i in range(ends)]),
            ],
            axis=dim,
        )
    return cells


def conv_valid(field, kernel):
    out = lax.conv_general_dilated(
        field[None],
        kernel,
        (1, 1),
        "VALID",
        dimension_numbers=("NHWC", "HWIO", "NHWC"),
        preferred_element_type=jnp.float32,
    )
    return out[0]


def swish(field):
    return jax.nn.silu(field.astype(jnp.float32)).astype(jnp.bfloat16)


def encode(features, conv_first, conv_second, conv_last):
    act0 = swish(features)
    edged = padded(act0, (("row", 0), ("col", 1)), 1)
    inner = conv_valid(edged, conv_first).astype(jnp.bfloat16)
    act1 = swish(inner)
    edged = padded(act1, (("row", 0), ("col", 1)), 1)
    block = (features.astype(jnp.float32) + conv_valid(edged, conv_second)).astype(jnp.bfloat16)
    wider = padded(swish(block), (("row", 0), ("col", 1)), 1)
    return (conv_valid(wider, conv_last) - latent_shift) * latent_scale


def rms_scale(values, gain):
    return values * lax.rsqrt(jnp.mean(values * values, axis=-1, keepdims=True) + norm_eps) * gain


def on_device(
    features,
    conv_first,
    conv_second,
    conv_last,
    noise,
    prior_patches,
    step_index,
    mod_table,
    embed_weight,
    qkv_weight,
    q_gain,
    k_gain,
    out_weight,
):
    latent = encode(features, conv_first, conv_second, conv_last)
    tile_rows, tile_cols, lat_channels = latent.shape
    tok_here = tile_rows // 2 * (tile_cols // 2)
    patch = (
        latent.reshape(tile_rows // 2, 2, tile_cols // 2, 2, lat_channels)
        .transpose(0, 2, 1, 3, 4)
        .reshape(tok_here, 4 * lat_channels)
    )
    step_total = mod_table.shape[0]
    sigma = (step_total - step_index.astype(jnp.float32)) / (step_total + 1.0)
    fresh = ((1.0 - sigma[0]) * patch + sigma[0] * noise.astype(jnp.float32)).astype(jnp.bfloat16)
    patches = jnp.concatenate([fresh[:, None, :], prior_patches], axis=1)
    picker = (step_index[:, None] == jnp.arange(step_total, dtype=jnp.int32)[None, :]).astype(
        jnp.float32
    )
    mods = jnp.einsum("sk,kcd->scd", picker, mod_table, precision=lax.Precision.HIGHEST)
    head_dim = q_gain.shape[0]
    local_heads = qkv_weight.shape[1] // (3 * head_dim)
    slots = patches.shape[1]
    own = jnp.einsum(
        "tsc,cd->tsd", patches, embed_weight, preferred_element_type=jnp.float32
    ).astype(jnp.bfloat16)
    hidden = own.astype(jnp.float32)
    mean = jnp.mean(hidden, axis=-1, keepdims=True)
    centred = hidden - mean
    variance = jnp.mean(centred * centred, axis=-1, keepdims=True)
    normed = centred * lax.rsqrt(variance + norm_eps)
    rows = lax.all_gather(
        ((1.0 + mods[None, :, 1, :]) * normed + mods[None, :, 0, :]).astype(jnp.bfloat16),
        "col",
        axis=0,
        tiled=True,
    )
    count = rows.shape[0]
    mixed = jnp.einsum("tsd,de->tse", rows, qkv_weight, preferred_element_type=jnp.float32)
    mixed = mixed.reshape(count, slots, local_heads, 3, head_dim)
    prepare_queries = rms_scale(mixed[:, :, :, 0], q_gain).astype(jnp.bfloat16)
    keys = rms_scale(mixed[:, :, :, 1], k_gain).astype(jnp.bfloat16)
    values = mixed[:, :, :, 2].astype(jnp.bfloat16)
    ready = jnp.stack([prepare_queries, keys, values], axis=3).reshape(
        count, slots, local_heads * 3 * head_dim
    )
    group_rows = ready.shape[0]
    ready = ready.reshape(group_rows, slots, local_heads, 3, head_dim)
    queries = ready[:, :, :, 0]
    keys = ready[:, :, :, 1].reshape(group_rows, slots, local_heads * head_dim)
    values = ready[:, :, :, 2].reshape(group_rows, slots, local_heads * head_dim)
    inverse_root = 1.0 / math.sqrt(head_dim)
    start_best = jnp.full((slots, local_heads, group_rows), far_negative, jnp.float32)
    start_total = jnp.zeros((slots, local_heads, group_rows), jnp.float32)
    start_accum = jnp.zeros((slots, local_heads, group_rows, head_dim), jnp.float32)
    piece = (
        lax.all_gather(keys, "row", axis=0, tiled=True),
        lax.all_gather(values, "row", axis=0, tiled=True),
    )
    total = start_total
    accum = start_accum
    count = piece[0].shape[0]
    far_keys = piece[0].reshape(count, slots, local_heads, head_dim)
    far_values = piece[1].reshape(count, slots, local_heads, head_dim)
    new_best = []
    new_total = []
    new_accum = []
    for slot in range(slots):
        scores = (
            jnp.einsum(
                "qhd,khd->hqk",
                queries[:, slot],
                far_keys[:, slot],
                preferred_element_type=jnp.float32,
            )
            * inverse_root
        )
        top = jnp.maximum(start_best[slot], jnp.max(scores, axis=-1))
        fade = jnp.exp(start_best[slot] - top)
        expo = jnp.exp(scores - top[:, :, None])
        new_best.append(top)
        new_total.append(total[slot] * fade + jnp.sum(expo, axis=-1))
        gathered = jnp.einsum(
            "hqk,khd->hqd",
            expo.astype(jnp.bfloat16),
            far_values[:, slot],
            preferred_element_type=jnp.float32,
        )
        new_accum.append(accum[slot] * fade[:, :, None] + gathered)
    total = jnp.stack(new_total)
    accum = jnp.stack(new_accum)
    attended = (accum / total[:, :, :, None]).astype(jnp.bfloat16)
    attended = attended.transpose(2, 0, 1, 3).reshape(group_rows, slots, local_heads * head_dim)
    rows = lax.slice_in_dim(attended, 0, tok_here * lax.axis_size("col"), axis=0)
    projected = lax.psum_scatter(
        jnp.einsum("tse,ed->tsd", rows, out_weight, preferred_element_type=jnp.float32),
        "col",
        scatter_dimension=0,
        tiled=True,
    )
    return (own.astype(jnp.float32) + mods[None, :, 2, :] * projected).astype(jnp.bfloat16)


def solution(mesh):
    placed = (
        P("row", "col", None),
        P(),
        P(),
        P(),
        P(("row", "col"), None),
        P(("row", "col"), None, None),
        P(),
        P(),
        P(),
        P(None, "col"),
        P(),
        P(),
        P("col", None),
    )
    return jax.shard_map(
        on_device,
        mesh=mesh,
        in_specs=placed,
        out_specs=P(("row", "col"), None, None),
        check_vma=False,
    )
```

profile of v0, /device:TPU:0, one launch (start us, length us, event | category | flops | bytes accessed | tf_op | source)
XLA Modules:
  0.0 378.9 jit_solution(1029843280191258922)
XLA Ops:
  7.7 1.3 collective-permute-start.1
  9.0 3.0 collective-permute-start
  12.9 1.3 collective-permute-start.3
  14.2 5.6 %collective-permute-start.2 = (bf16[10,1,512]{2,0,1:T(8,128)(2,1)S(1)}, bf16[10,1,512]{2,0,1:T(8,128)(2,1)S(1)}, u32[]{:S(2)}, u32[]{:S(2)}) collective-permute-start(bf16[10,1,512]{2,0,1:T(8,128)(2,1)S(1)} %get-tuple-element.12), channel_id=1, source_target_pairs={{0,1},{1,2},{2,3},{4,5},{5,6},{6,7},{8,9},{9,10},{10,11},{12,13},{... | collective-permute-start | bytes 30728 | tf_op jit(solution)/shard_map/ppermute | solution.py:22
  19.7 1.4 collective-permute-done.2
  21.6 3.6 fusion.63
  25.4 1.3 collective-permute-start.5
  26.7 3.1 collective-permute-start.4
  32.0 4.8 %collective-permute-start.6 = (bf16[10,1,512]{2,0,1:T(8,128)(2,1)S(1)}, bf16[10,1,512]{2,0,1:T(8,128)(2,1)S(1)}, u32[]{:S(2)}, u32[]{:S(2)}) collective-permute-start(bf16[10,1,512]{2,0,1:T(8,128)(2,1)S(1)} %get-tuple-element.10), channel_id=1, source_target_pairs={{0,1},{1,2},{2,3},{4,5},{5,6},{6,7},{8,9},{9,10},{10,11},{12,13},{... | collective-permute-start | bytes 30728 | tf_op jit(solution)/shard_map/ppermute | solution.py:22
  41.5 5.4 %collective-permute-start.8 = (bf16[1,16,512]{2,0,1:T(2,128)(2,1)S(1)}, bf16[1,16,512]{2,0,1:T(2,128)(2,1)S(1)}, u32[]{:S(2)}, u32[]{:S(2)}) collective-permute-start(bf16[1,16,512]{2,0,1:T(2,128)(2,1)S(1)} %get-tuple-element.17), channel_id=1, source_target_pairs={{0,4},{4,8},{8,12},{12,16},{16,20},{20,24},{24,28},{1,5},{5,9},{9,... | collective-permute-start | bytes 49160 | tf_op jit(solution)/shard_map/ppermute | solution.py:22
  49.0 4.5 %collective-permute-start.10 = (bf16[10,1,512]{2,0,1:T(8,128)(2,1)S(1)}, bf16[10,1,512]{2,0,1:T(8,128)(2,1)S(1)}, u32[]{:S(2)}, u32[]{:S(2)}) collective-permute-start(bf16[10,1,512]{2,0,1:T(8,128)(2,1)S(1)} %get-tuple-element.8), channel_id=1, source_target_pairs={{0,1},{1,2},{2,3},{4,5},{5,6},{6,7},{8,9},{9,10},{10,11},{12,13},{... | collective-permute-start | bytes 30728 | tf_op jit(solution)/shard_map/ppermute | solution.py:22
  53.6 1.4 collective-permute-done.10
  58.4 73.3 %all-gather.4.cloned.1.call-done = bf16[128,4,3072]{2,0,1:T(8,128)(2,1)} async-done(((bf16[32,4,3072]{2,0,1:T(8,128)(2,1)}), bf16[128,4,3072]{2,0,1:T(8,128)(2,1)}) %all-gather.4.cloned.1.call-update) | async-done | bytes 3145744 | tf_op jit(solution)/shard_map/all_gather | solution.py:104
  131.7 11.3 %fusion = f32[128,4,2304]{0,2,1:T(8,128)S(1)} fusion(bf16[128,4,3072]{2,0,1:T(8,128)(2,1)} %all-gather.4.cloned.1.call-done, bf16[3072,2304]{1,0:T(8,128)(2,1)} %param.22), kind=kOutput, calls=%fused_computation | convolution fusion | flops 7247757312 | bytes 22020096 | tf_op jit(solution)/shard_map/tsd,de->tse/dot_general | solution.py:111
  143.0 1.7 fusion.127
  146.9 2.4 slice.217
  149.5 1.9 copy.53
  151.9 1.4 fusion.30
  153.3 39.0 %all-gather.6.cloned.1.call-done = bf16[1024,4,768]{0,2,1:T(8,128)(2,1)} async-done(((bf16[128,4,768]{0,2,1:T(8,128)(2,1)}), bf16[1024,4,768]{0,2,1:T(8,128)(2,1)}) %all-gather.6.cloned.1.call-update) | async-done | bytes 6291472 | tf_op jit(solution)/shard_map/all_gather | solution.py:129
  192.3 2.3 multiply_reduce_fusion
  194.6 3.2 multiply_reduce_fusion.1
  199.6 2.3 multiply_reduce_fusion.2
  201.8 2.2 multiply_reduce_fusion.3
  204.1 36.8 %all-gather.8.cloned.1.call-done = bf16[1024,4,768]{0,2,1:T(8,128)(2,1)} async-done(((bf16[128,4,768]{0,2,1:T(8,128)(2,1)}), bf16[1024,4,768]{0,2,1:T(8,128)(2,1)}) %all-gather.8.cloned.1.call-update) | async-done | bytes 6291472 | tf_op jit(solution)/shard_map/all_gather | solution.py:130
  240.9 3.4 fusion.60
  244.4 2.5 fusion.54
  248.4 2.4 fusion.48
  250.9 2.5 fusion.42
  253.7 4.6 %fusion.2 = f32[128,4,3072]{2,0,1:T(8,128)} fusion(bf16[128,4,768]{0,2,1:T(8,128)(2,1)S(1)} %bitcast.190, bf16[768,3072]{1,0:T(8,128)(2,1)S(1)} %bitcast.186), kind=kOutput, calls=%fused_computation.2 | convolution fusion | flops 2415919104 | bytes 11796480 | tf_op jit(solution)/shard_map/tse,ed->tsd/dot_general | solution.py:168
  258.3 110.9 %reduce-scatter.2.cloned.1.call-done = f32[32,4,3072]{2,0,1:T(8,128)} async-done(((f32[128,4,3072]{2,0,1:T(8,128)}), f32[32,4,3072]{2,0,1:T(8,128)}) %reduce-scatter.2.cloned.1.call-update) | async-done | bytes 1572880 | tf_op jit(solution)/shard_map/reduce_scatter | solution.py:167
  369.2 1.6 add_convert_fusion
  370.8 1.5 copy.41
  (130 shorter events, 20.8 us)
Async XLA Ops:
  6.5 49.7 %copy-start = (bf16[64,3072]{1,0:T(8,128)(2,1)S(1)}, bf16[64,3072]{1,0:T(8,128)(2,1)}, u32[]{:S(2)}) copy-start(bf16[64,3072]{1,0:T(8,128)(2,1)} %param.21) | copy-start | bytes 1179652
  6.5 125.2 %all-gather.4.cloned.1.call-start = ((), (), s32[]{:S(2)}) async-start(), calls=%async_computation.1 | async-start | bytes 3932160 | tf_op jit(solution)/shard_map/all_gather | solution.py:104
  7.7 4.3 %collective-permute-start.1 = (bf16[1,16,512]{2,0,1:T(2,128)(2,1)S(1)}, bf16[1,16,512]{2,0,1:T(2,128)(2,1)S(1)}, u32[]{:S(2)}, u32[]{:S(2)}) collective-permute-start(bf16[1,16,512]{2,0,1:T(2,128)(2,1)S(1)} %get-tuple-element.22), channel_id=1, source_target_pairs={{4,0},{8,4},{12,8},{16,12},{20,16},{24,20},{28,24},{5,1},{9,5},{13... | collective-permute-start | bytes 49160 | tf_op jit(solution)/shard_map/ppermute | solution.py:24
  9.0 3.9 %collective-permute-start = (bf16[1,16,512]{2,0,1:T(2,128)(2,1)S(1)}, bf16[1,16,512]{2,0,1:T(2,128)(2,1)S(1)}, u32[]{:S(2)}, u32[]{:S(2)}) collective-permute-start(bf16[1,16,512]{2,0,1:T(2,128)(2,1)S(1)} %get-tuple-element.21), channel_id=1, source_target_pairs={{0,4},{4,8},{8,12},{12,16},{16,20},{20,24},{24,28},{1,5},{5,9},{9,... | collective-permute-start | bytes 49160 | tf_op jit(solution)/shard_map/ppermute | solution.py:22
  12.9 6.9 %collective-permute-start.3 = (bf16[10,1,512]{2,0,1:T(8,128)(2,1)S(1)}, bf16[10,1,512]{2,0,1:T(8,128)(2,1)S(1)}, u32[]{:S(2)}, u32[]{:S(2)}) collective-permute-start(bf16[10,1,512]{2,0,1:T(8,128)(2,1)S(1)} %get-tuple-element.13), channel_id=1, source_target_pairs={{1,0},{2,1},{3,2},{5,4},{6,5},{7,6},{9,8},{10,9},{11,10},{13,12},{... | collective-permute-start | bytes 30728 | tf_op jit(solution)/shard_map/ppermute | solution.py:24
  14.2 7.0 %collective-permute-start.2 = (bf16[10,1,512]{2,0,1:T(8,128)(2,1)S(1)}, bf16[10,1,512]{2,0,1:T(8,128)(2,1)S(1)}, u32[]{:S(2)}, u32[]{:S(2)}) collective-permute-start(bf16[10,1,512]{2,0,1:T(8,128)(2,1)S(1)} %get-tuple-element.12), channel_id=1, source_target_pairs={{0,1},{1,2},{2,3},{4,5},{5,6},{6,7},{8,9},{9,10},{10,11},{12,13},{... | collective-permute-start | bytes 30728 | tf_op jit(solution)/shard_map/ppermute | solution.py:22
  21.5 17.0 %slice-start.4 = ((s8[4718592]{0:T(1024)(128)(4,1)}), s8[4194304]{0:T(1024)(128)(4,1)S(1)}, s32[]{:S(2)}) async-start(s8[4718592]{0:T(1024)(128)(4,1)} %bitcast.204), calls=%async_computation.9 | async-start | bytes 8388608
  21.5 15.2 %copy-start.11 = (f32[4,3,3072]{2,0,1:T(4,128)S(1)}, f32[4,3,3072]{2,0,1:T(4,128)}, u32[]{:S(2)}) copy-start(f32[4,3,3072]{2,0,1:T(4,128)} %param.20) | copy-start | bytes 442372
  21.6 15.2 %copy-start.14 = (s32[4]{0:T(128)S(1)}, s32[4]{0:T(128)}, u32[]{:S(2)}) copy-start(s32[4]{0:T(128)} %param.19) | copy-start | bytes 52
  21.6 17.0 %slice-start.5 = ((s8[4718592]{0:T(1024)(128)(4,1)}), s8[524288]{0:T(1024)(128)(4,1)S(1)}, s32[]{:S(2)}) async-start(s8[4718592]{0:T(1024)(128)(4,1)} %bitcast.204), calls=%async_computation.10 | async-start | bytes 1048576
  25.2 13.4 %copy-start.18 = (pred[8,3]{0,1:T(4,128)(4,1)S(1)}, pred[8,3]{0,1:T(4,128)(4,1)}, u32[]{:S(2)}) copy-start(pred[8,3]{0,1:T(4,128)(4,1)} %constant.50) | copy-start | bytes 76
  25.4 4.4 %collective-permute-start.5 = (bf16[1,16,512]{2,0,1:T(2,128)(2,1)S(1)}, bf16[1,16,512]{2,0,1:T(2,128)(2,1)S(1)}, u32[]{:S(2)}, u32[]{:S(2)}) collective-permute-start(bf16[1,16,512]{2,0,1:T(2,128)(2,1)S(1)} %get-tuple-element.20), channel_id=1, source_target_pairs={{4,0},{8,4},{12,8},{16,12},{20,16},{24,20},{28,24},{5,1},{9,5},{13... | collective-permute-start | bytes 49160 | tf_op jit(solution)/shard_map/ppermute | solution.py:24
  26.7 3.9 %collective-permute-start.4 = (bf16[1,16,512]{2,0,1:T(2,128)(2,1)S(1)}, bf16[1,16,512]{2,0,1:T(2,128)(2,1)S(1)}, u32[]{:S(2)}, u32[]{:S(2)}) collective-permute-start(bf16[1,16,512]{2,0,1:T(2,128)(2,1)S(1)} %get-tuple-element.19), channel_id=1, source_target_pairs={{0,4},{4,8},{8,12},{12,16},{16,20},{20,24},{24,28},{1,5},{5,9},{9,... | collective-permute-start | bytes 49160 | tf_op jit(solution)/shard_map/ppermute | solution.py:22
  30.7 6.4 %collective-permute-start.7 = (bf16[10,1,512]{2,0,1:T(8,128)(2,1)S(1)}, bf16[10,1,512]{2,0,1:T(8,128)(2,1)S(1)}, u32[]{:S(2)}, u32[]{:S(2)}) collective-permute-start(bf16[10,1,512]{2,0,1:T(8,128)(2,1)S(1)} %get-tuple-element.11), channel_id=1, source_target_pairs={{1,0},{2,1},{3,2},{5,4},{6,5},{7,6},{9,8},{10,9},{11,10},{13,12},{... | collective-permute-start | bytes 30728 | tf_op jit(solution)/shard_map/ppermute | solution.py:24
  32.0 6.2 %collective-permute-start.6 = (bf16[10,1,512]{2,0,1:T(8,128)(2,1)S(1)}, bf16[10,1,512]{2,0,1:T(8,128)(2,1)S(1)}, u32[]{:S(2)}, u32[]{:S(2)}) collective-permute-start(bf16[10,1,512]{2,0,1:T(8,128)(2,1)S(1)} %get-tuple-element.10), channel_id=1, source_target_pairs={{0,1},{1,2},{2,3},{4,5},{5,6},{6,7},{8,9},{9,10},{10,11},{12,13},{... | collective-permute-start | bytes 30728 | tf_op jit(solution)/shard_map/ppermute | solution.py:22
  39.7 15.6 %copy-start.17 = (bf16[3,3,512,16]{2,3,1,0:T(8,128)(2,1)S(1)}, bf16[3,3,512,16]{2,3,1,0:T(8,128)(2,1)}, u32[]{:S(2)}) copy-start(bf16[3,3,512,16]{2,3,1,0:T(8,128)(2,1)} %param.16) | copy-start | bytes 442372
  40.0 16.2 %copy-start.13 = (bf16[32,64]{1,0:T(8,128)(2,1)S(1)}, bf16[32,64]{1,0:T(8,128)(2,1)}, u32[]{:S(2)}) copy-start(bf16[32,64]{1,0:T(8,128)(2,1)} %param.17) | copy-start | bytes 12292
  40.0 16.3 %copy-start.12 = (bf16[32,3,64]{2,0,1:T(8,128)(2,1)S(1)}, bf16[32,3,64]{2,0,1:T(8,128)(2,1)}, u32[]{:S(2)}) copy-start(bf16[32,3,64]{2,0,1:T(8,128)(2,1)} %param.18) | copy-start | bytes 36868
  40.2 7.3 %collective-permute-start.9 = (bf16[1,16,512]{2,0,1:T(2,128)(2,1)S(1)}, bf16[1,16,512]{2,0,1:T(2,128)(2,1)S(1)}, u32[]{:S(2)}, u32[]{:S(2)}) collective-permute-start(bf16[1,16,512]{2,0,1:T(2,128)(2,1)S(1)} %get-tuple-element.18), channel_id=1, source_target_pairs={{4,0},{8,4},{12,8},{16,12},{20,16},{24,20},{28,24},{5,1},{9,5},{13... | collective-permute-start | bytes 49160 | tf_op jit(solution)/shard_map/ppermute | solution.py:24
  41.5 6.2 %collective-permute-start.8 = (bf16[1,16,512]{2,0,1:T(2,128)(2,1)S(1)}, bf16[1,16,512]{2,0,1:T(2,128)(2,1)S(1)}, u32[]{:S(2)}, u32[]{:S(2)}) collective-permute-start(bf16[1,16,512]{2,0,1:T(2,128)(2,1)S(1)} %get-tuple-element.17), channel_id=1, source_target_pairs={{0,4},{4,8},{8,12},{12,16},{16,20},{20,24},{24,28},{1,5},{5,9},{9,... | collective-permute-start | bytes 49160 | tf_op jit(solution)/shard_map/ppermute | solution.py:22
  47.7 5.9 %collective-permute-start.11 = (bf16[10,1,512]{2,0,1:T(8,128)(2,1)S(1)}, bf16[10,1,512]{2,0,1:T(8,128)(2,1)S(1)}, u32[]{:S(2)}, u32[]{:S(2)}) collective-permute-start(bf16[10,1,512]{2,0,1:T(8,128)(2,1)S(1)} %get-tuple-element.9), channel_id=1, source_target_pairs={{1,0},{2,1},{3,2},{5,4},{6,5},{7,6},{9,8},{10,9},{11,10},{13,12},{... | collective-permute-start | bytes 30728 | tf_op jit(solution)/shard_map/ppermute | solution.py:24
  49.0 6.0 %collective-permute-start.10 = (bf16[10,1,512]{2,0,1:T(8,128)(2,1)S(1)}, bf16[10,1,512]{2,0,1:T(8,128)(2,1)S(1)}, u32[]{:S(2)}, u32[]{:S(2)}) collective-permute-start(bf16[10,1,512]{2,0,1:T(8,128)(2,1)S(1)} %get-tuple-element.8), channel_id=1, source_target_pairs={{0,1},{1,2},{2,3},{4,5},{5,6},{6,7},{8,9},{9,10},{10,11},{12,13},{... | collective-permute-start | bytes 30728 | tf_op jit(solution)/shard_map/ppermute | solution.py:22
  58.3 134.0 %all-gather.6.cloned.1.call-start = ((), (), s32[]{:S(2)}) async-start(), calls=%async_computation.2 | async-start | bytes 7077888 | tf_op jit(solution)/shard_map/all_gather | solution.py:129
  146.8 94.1 %all-gather.8.cloned.1.call-start = ((), (), s32[]{:S(2)}) async-start(), calls=%async_computation.3 | async-start | bytes 7077888 | tf_op jit(solution)/shard_map/all_gather | solution.py:130
  149.3 219.9 %reduce-scatter.2.cloned.1.call-start = ((), (), s32[]{:S(2)}) async-start(), calls=%async_computation.4 | async-start | bytes 7864320 | tf_op jit(solution)/shard_map/reduce_scatter | solution.py:167
  153.3 41.3 %copy-start.8 = (bf16[128,4,6,128]{3,0,2,1:T(8,128)(2,1)S(1)}, bf16[128,4,6,128]{3,0,2,1:T(8,128)(2,1)}, u32[]{:S(2)}) copy-start(bf16[128,4,6,128]{3,0,2,1:T(8,128)(2,1)} %fusion.30) | copy-start | bytes 2359300
  192.3 7.2 %slice-start = ((s8[6291456]{0:T(1024)(128)(4,1)}), s8[4194304]{0:T(1024)(128)(4,1)S(1)}, s32[]{:S(2)}) async-start(s8[6291456]{0:T(1024)(128)(4,1)} %bitcast.181), calls=%async_computation.5 | async-start | bytes 8388608
  194.6 4.0 %copy-start.4 = (f32[6,128,1024]{2,1,0:T(8,128)}, f32[6,128,1024]{2,1,0:T(8,128)S(1)}, u32[]{:S(2)}) copy-start(f32[6,128,1024]{2,1,0:T(8,128)S(1)} %get-tuple-element.34) | copy-start | bytes 9437188
  194.6 4.9 %slice-start.1 = ((s8[6291456]{0:T(1024)(128)(4,1)}), s8[2097152]{0:T(1024)(128)(4,1)S(1)}, s32[]{:S(2)}) async-start(s8[6291456]{0:T(1024)(128)(4,1)} %bitcast.181), calls=%async_computation.6 | async-start | bytes 4194304
  248.4 5.2 %slice-start.2 = ((s8[4718592]{0:T(1024)(128)(4,1)}), s8[524288]{0:T(1024)(128)(4,1)S(1)}, s32[]{:S(2)}) async-start(s8[4718592]{0:T(1024)(128)(4,1)} %bitcast.185), calls=%async_computation.7 | async-start | bytes 1048576
  258.3 110.9 %copy-start.10 = (f32[4,3072]{1,0:T(4,128)S(1)}, f32[4,3072]{1,0:T(4,128)}, u32[]{:S(2)}) copy-start(f32[4,3072]{1,0:T(4,128)} %get-tuple-element.14) | copy-start | bytes 147460
  258.3 114.0 %copy-start.1 = (bf16[64,3072]{1,0:T(8,128)(2,1)S(1)}, bf16[64,3072]{1,0:T(8,128)(2,1)}, u32[]{:S(2)}) copy-start(bf16[64,3072]{1,0:T(8,128)(2,1)} %param.21) | copy-start | bytes 1179652
  (9 other events, 22.5 us)
Sparse Core Ops, SparseCore 0:
  58.4 73.2 all-gather.3
  146.9 45.3 all-gather.5
  194.2 46.6 all-gather.7
  258.4 110.7 reduce-scatter.1
where the time goes:
time: 379 us
  waiting for transfers between devices  266 us (70%)
  matrix products  43 us (11%)
  starting transfers between devices  34.4 us (9%)
  between operations  14 us (4%)
  other arithmetic  13.3 us (4%)
  local copies, waits for them, and re-layouts  8.3 us (2%)
    reduce_scatter x1, waiting for transfers between devices, on_device(): lax.psum_scatter(jnp.einsum('tse,ed->tsd', rows, out_weight, preferred_el...  111 us
    all_gather x1, waiting for transfers between devices, on_device(): lax.all_gather(((1.0 + mods[None, :, 1, :]) * normed + mods[None, :, 0, :...  73.3 us
    all_gather x1, waiting for transfers between devices, on_device(): lax.all_gather(keys, 'row', axis=0, tiled=True)  39 us
    all_gather x1, waiting for transfers between devices, on_device(): lax.all_gather(values, 'row', axis=0, tiled=True)  36.8 us
    ppermute x6, starting transfers between devices, padded(): lax.ppermute(tail, axis, [(i, (i + 1) % count) for i in range(ends)])  26.4 us
    dot_general x1, matrix products, on_device(): jnp.einsum('tsd,de->tse', rows, qkv_weight, preferred_element_type=jnp.fl...  11.3 us
    dot_general x4, matrix products, on_device(): jnp.einsum('hqk,khd->hqd', expo.astype(jnp.bfloat16), far_values[:, slot]...  10.9 us
    dot_general x4, matrix products, on_device(): jnp.einsum('qhd,khd->hqk', queries[:, slot], far_keys[:, slot], preferred...  10 us
  transfers between devices with their start and end apart: 16, of which 10 were waited for; matrix products, arithmetic and copies ran while one was open for 5% of the time, Pallas kernels for 0%

commit v1 on v0

v1 whole, which is shorter than its diff:
```python
import functools
import math

import jax
import jax.numpy as jnp
from jax import lax
from jax.experimental import pallas as pl
from jax.experimental.pallas import tpu as pltpu
from jax.sharding import PartitionSpec as P

norm_eps = 1e-06
latent_shift = 0.1159
latent_scale = 0.3611
bf16 = jnp.bfloat16
f32 = jnp.float32


def swish(field):
    return jax.nn.silu(field.astype(f32)).astype(bf16)


def conv_valid(field, kernel):
    out = lax.conv_general_dilated(
        field[None],
        kernel,
        (1, 1),
        "VALID",
        dimension_numbers=("NHWC", "HWIO", "NHWC"),
        preferred_element_type=f32,
    )
    return out[0]


def padded(cells, axis, dim, width):
    count = lax.axis_size(axis)
    head = lax.slice_in_dim(cells, 0, width, axis=dim)
    tail = lax.slice_in_dim(cells, cells.shape[dim] - width, cells.shape[dim], axis=dim)
    before = lax.ppermute(tail, axis, [(i, i + 1) for i in range(count - 1)])
    after = lax.ppermute(head, axis, [(i + 1, i) for i in range(count - 1)])
    return jnp.concatenate([before, cells, after], axis=dim)


def inside(rows, cols, tile_rows, tile_cols, reach):
    at_row = lax.axis_index("row") * tile_rows - reach + jnp.arange(rows)
    at_col = lax.axis_index("col") * tile_cols - reach + jnp.arange(cols)
    ok_row = (at_row >= 0) & (at_row < lax.axis_size("row") * tile_rows)
    ok_col = (at_col >= 0) & (at_col < lax.axis_size("col") * tile_cols)
    return (ok_row[:, None] & ok_col[None, :])[:, :, None]


def encode(wide, conv_first, conv_second, conv_last, tile_rows, tile_cols):
    zero = jnp.zeros((), bf16)
    inner = conv_valid(swish(wide), conv_first).astype(bf16)
    mask = inside(inner.shape[0], inner.shape[1], tile_rows, tile_cols, 2)
    act1 = jnp.where(mask, swish(inner), zero)
    block = (wide[2:-2, 2:-2].astype(f32) + conv_valid(act1, conv_second)).astype(bf16)
    mask = inside(block.shape[0], block.shape[1], tile_rows, tile_cols, 1)
    act2 = jnp.where(mask, swish(block), zero)
    return (conv_valid(act2, conv_last) - latent_shift) * latent_scale


def fold_kernel(e_ref, scale_ref, shift_ref, w_ref, out_ref, lhs_ref):
    slots = scale_ref.shape[0]
    width = e_ref.shape[0]

    @pl.when(pl.program_id(0) == 0)
    def _():
        e = e_ref[...].astype(f32)
        e = e - jnp.mean(e, axis=1, keepdims=True)
        for s in range(slots):
            lhs_ref[s * width : (s + 1) * width, :] = (e * (1.0 + scale_ref[s : s + 1, :])).astype(
                bf16
            )
        lhs_ref[slots * width :, :] = shift_ref[...]

    r = jnp.dot(lhs_ref[...], w_ref[...], preferred_element_type=f32)
    base = slots * width
    for s in range(slots):
        out_ref[0, s, 0:width, :] = r[s * width : (s + 1) * width]
        bias = r[base + s : base + s + 1] + r[base + slots + s : base + slots + s + 1]
        out_ref[0, s, width:, :] = jnp.broadcast_to(bias, (8, bias.shape[1]))


def fold(embed_weight, scale, shift, qkv_weight, head_dim):
    width, depth = embed_weight.shape
    slots = scale.shape[0]
    cols = 3 * head_dim
    heads = qkv_weight.shape[1] // cols
    rows = slots * width + shift.shape[0]
    return pl.pallas_call(
        fold_kernel,
        grid=(heads,),
        in_specs=[
            pl.BlockSpec((width, depth), lambda h: (0, 0)),
            pl.BlockSpec((slots, depth), lambda h: (0, 0)),
            pl.BlockSpec(shift.shape, lambda h: (0, 0)),
            pl.BlockSpec((depth, cols), lambda h: (0, h)),
        ],
        out_specs=pl.BlockSpec((1, slots, width + 8, cols), lambda h: (h, 0, 0, 0)),
        out_shape=jax.ShapeDtypeStruct((heads, slots, width + 8, cols), f32),
        scratch_shapes=[pltpu.VMEM((rows, depth), bf16)],
        compiler_params=pltpu.CompilerParams(vmem_limit_bytes=24 * 2**20),
        cost_estimate=pl.CostEstimate(
            flops=2 * rows * depth * heads * cols,
            bytes_accessed=depth * heads * cols * 2,
            transcendentals=0,
        ),
    )(embed_weight, scale, shift, qkv_weight)


def widen(p, gram_ref):
    pf = p.astype(f32)
    pg = jnp.dot(p, gram_ref[0], preferred_element_type=f32)
    pg = pg + jnp.dot(p, gram_ref[1], preferred_element_type=f32)
    var = jnp.sum(pg * pf, axis=1, keepdims=True)
    pn = pf * lax.rsqrt(jnp.maximum(var, 0.0) + norm_eps)
    hi = pn.astype(bf16)
    lo = (pn - hi.astype(f32)).astype(bf16)
    lane = lax.broadcasted_iota(jnp.int32, p.shape, 1)
    ones = jnp.where(lane < 2, 1.0, 0.0).astype(bf16)
    return jnp.concatenate([hi, lo, hi, ones], axis=1)


def attend_kernel(
    hp, head_dim, key_ref, query_ref, gram_ref, m_ref, gain_ref, wo_ref, keep_ref, send_ref,
    kaug_ref, qaug_ref, acc_ref,
):
    step = pl.program_id(0)
    width = key_ref.shape[-1]

    @pl.when(step == 0)
    def _():
        kaug_ref[...] = widen(key_ref[...].reshape(-1, width), gram_ref)
        qaug_ref[...] = widen(query_ref[...].reshape(-1, width), gram_ref)

    kaug = kaug_ref[...]
    qaug = qaug_ref[...]
    outs = []
    for j in range(hp):
        m = m_ref[j, 0:width, :]
        bias = m_ref[j, width : width + 1, :]
        mhi = m.astype(bf16)
        mlo = (m - mhi.astype(f32)).astype(bf16)
        bhi = bias.astype(bf16).astype(f32)
        blo = bias - bhi
        at = lax.broadcasted_iota(jnp.int32, m.shape, 0)
        low = jnp.where(at == 0, bhi, jnp.where(at == 1, blo, 0.0)).astype(bf16)
        maug = jnp.concatenate([mhi, mhi, mlo, low], axis=0)
        xq = jnp.dot(qaug, maug[:, :head_dim], preferred_element_type=f32)
        xkv = jnp.dot(kaug, maug[:, head_dim:], preferred_element_type=f32)
        xk = xkv[:, :head_dim]
        v = xkv[:, head_dim:].astype(bf16)
        k = (
            xk * lax.rsqrt(jnp.mean(xk * xk, axis=1, keepdims=True) + norm_eps)
        ).astype(bf16)
        q = (
            xq * lax.rsqrt(jnp.mean(xq * xq, axis=1, keepdims=True) + norm_eps) * gain_ref[...]
        ).astype(bf16)
        s = lax.dot_general(q, k, (((1,), (1,)), ((), ())), preferred_element_type=f32)
        e = jnp.exp2(s - jnp.max(s, axis=1, keepdims=True))
        total = jnp.sum(e, axis=1, keepdims=True)
        o = jnp.dot(e.astype(bf16), v, preferred_element_type=f32)
        outs.append((o / total).astype(bf16))
    att = outs[0] if hp == 1 else jnp.concatenate(outs, axis=1)
    part = jnp.dot(att, wo_ref[...], preferred_element_type=f32)

    @pl.when(step == 0)
    def _():
        acc_ref[...] = part

    @pl.when(step > 0)
    def _():
        acc_ref[...] += part

    @pl.when(step == pl.num_programs(0) - 1)
    def _():
        tok = keep_ref.shape[1]
        for i in range(keep_ref.shape[0]):
            keep_ref[i] = acc_ref[2 * i * tok : (2 * i + 1) * tok, :]
            send_ref[i] = acc_ref[(2 * i + 1) * tok : (2 * i + 2) * tok, :].astype(bf16)


def attend(keys, queries, at, gram, folded, slot, gain, out_weight):
    nr, nc, _, tok, width = keys.shape
    heads, _, mrows, cols = folded.shape
    head_dim = cols // 3
    depth = out_weight.shape[1]
    hp = 2 if heads % 2 == 0 else 1
    nk, nq = nr * nc * tok, nc * tok
    half = nc // 2
    return pl.pallas_call(
        functools.partial(attend_kernel, hp, head_dim),
        grid=(heads // hp,),
        in_specs=[
            pl.BlockSpec((nr, nc, None, tok, width), lambda h: (0, 0, at, 0, 0)),
            pl.BlockSpec((nc, None, tok, width), lambda h: (0, at, 0, 0)),
            pl.BlockSpec((2, width, width), lambda h: (0, 0, 0)),
            pl.BlockSpec((hp, None, mrows, cols), lambda h: (h, slot, 0, 0)),
            pl.BlockSpec((1, head_dim), lambda h: (0, 0)),
            pl.BlockSpec((hp * head_dim, depth), lambda h: (h, 0)),
        ],
        out_specs=[
            pl.BlockSpec((half, tok, depth), lambda h: (0, 0, 0)),
            pl.BlockSpec((half, tok, depth), lambda h: (0, 0, 0)),
        ],
        out_shape=[
            jax.ShapeDtypeStruct((half, tok, depth), f32),
            jax.ShapeDtypeStruct((half, tok, depth), bf16),
        ],
        scratch_shapes=[
            pltpu.VMEM((nk, 4 * width), bf16),
            pltpu.VMEM((nq, 4 * width), bf16),
            pltpu.VMEM((nq, depth), f32),
        ],
        compiler_params=pltpu.CompilerParams(vmem_limit_bytes=40 * 2**20),
        cost_estimate=pl.CostEstimate(
            flops=2 * heads * (nk * 256 * 256 + 2 * nq * nk * head_dim * 2 + nq * head_dim * depth),
            bytes_accessed=heads * head_dim * depth * 2 + nq * depth * 3,
            transcendentals=heads * nq * nk,
        ),
    )(keys, queries, gram, folded, gain, out_weight)


def exchange(value, axis, bit):
    count = lax.axis_size(axis)
    return lax.ppermute(value, axis, [(i, i ^ bit) for i in range(count)])


def gather_tokens(own):
    nc = lax.axis_size("col")
    queries = jnp.stack([own] + [exchange(own, "col", k) for k in range(1, nc)])
    return queries, lax.all_gather(queries, "row", axis=0, tiled=False)


def settle(keep, send):
    bit = 1
    while True:
        total = keep + exchange(send, "col", bit).astype(f32)
        if total.shape[0] == 1:
            return total[0]
        keep, send = total[0::2], total[1::2].astype(bf16)
        bit *= 2


def on_device(
    features,
    conv_first,
    conv_second,
    conv_last,
    noise,
    prior_patches,
    step_index,
    mod_table,
    embed_weight,
    qkv_weight,
    q_gain,
    k_gain,
    out_weight,
):
    tile_rows, tile_cols, _ = features.shape
    wide = padded(padded(features, "row", 0, 3), "col", 1, 3)
    prior = prior_patches.transpose(1, 0, 2)
    prior_queries, prior_keys = gather_tokens(prior)

    step_total = mod_table.shape[0]
    mods = sum(
        jnp.where((step_index == k)[:, None, None], mod_table[k][None], 0.0)
        for k in range(step_total)
    )
    slots = step_index.shape[0]
    shift = mods[:, 0, :]
    shift_hi = shift.astype(bf16)
    shift_lo = (shift - shift_hi.astype(f32)).astype(bf16)
    spare = -(2 * slots) % 16
    shift2 = jnp.concatenate(
        [shift_hi, shift_lo, jnp.zeros((spare, shift.shape[1]), bf16)], axis=0
    )
    head_dim = q_gain.shape[0]
    folded = fold(embed_weight, mods[:, 1, :], shift2, qkv_weight, head_dim)
    centred = embed_weight.astype(f32)
    centred = centred - jnp.mean(centred, axis=1, keepdims=True)
    gram = (
        jnp.einsum("ad,bd->ab", centred, centred, precision=lax.Precision.HIGHEST)
        / embed_weight.shape[1]
    )
    gram_hi = gram.astype(bf16)
    gram2 = jnp.stack([gram_hi, (gram - gram_hi.astype(f32)).astype(bf16)])
    gain = (q_gain * k_gain * (math.log2(math.e) / math.sqrt(head_dim)))[None]

    sums = {}
    for slot in range(1, slots):
        keep, send = attend(
            prior_keys, prior_queries, slot - 1, gram2, folded, slot, gain, out_weight
        )
        sums[slot] = settle(keep, send)

    latent = encode(wide, conv_first, conv_second, conv_last, tile_rows, tile_cols)
    channels = latent.shape[-1]
    tok = tile_rows // 2 * (tile_cols // 2)
    patch = (
        latent.reshape(tile_rows // 2, 2, tile_cols // 2, 2, channels)
        .transpose(0, 2, 1, 3, 4)
        .reshape(tok, 4 * channels)
    )
    sigma = (step_total - step_index.astype(f32)) / (step_total + 1.0)
    fresh = ((1.0 - sigma[0]) * patch + sigma[0] * noise.astype(f32)).astype(bf16)
    fresh_queries, fresh_keys = gather_tokens(fresh[None])
    keep, send = attend(fresh_keys, fresh_queries, 0, gram2, folded, 0, gain, out_weight)
    sums[0] = settle(keep, send)

    patches = jnp.concatenate([fresh[None], prior], axis=0)
    own = jnp.einsum(
        "stc,cd->std", patches, embed_weight, preferred_element_type=f32
    ).astype(bf16)
    outs = [
        (own[s].astype(f32) + mods[s, 2][None, :] * sums[s]).astype(bf16) for s in range(slots)
    ]
    return jnp.stack(outs, axis=1)


def solution(mesh):
    placed = (
        P("row", "col", None),
        P(),
        P(),
        P(),
        P(("row", "col"), None),
        P(("row", "col"), None, None),
        P(),
        P(),
        P(),
        P(None, "col"),
        P(),
        P(),
        P("col", None),
    )
    return jax.shard_map(
        on_device,
        mesh=mesh,
        in_specs=placed,
        out_specs=P(("row", "col"), None, None),
        check_vma=False,
    )
```

time: 379 us -> 167 us (0.44)
  waiting for transfers between devices: 266 us -> 36.7 us
  Pallas kernels: 0 us -> 40.3 us
  matrix products: 43 us -> 17.3 us
  blocking collectives: 0 us -> 22.9 us
  between operations: 14 us -> 0.65 us
  starting transfers between devices: 34.4 us -> 25.9 us
  local copies, waits for them, and re-layouts: 8.3 us -> 15.8 us
  other arithmetic: 13.3 us -> 7.03 us
    all_gather x3 -> x0, waiting for transfers between devices: 149 us -> none  [the longest x1 73.3 us: on_device(): lax.all_gather(((1.0 + mods[None, :, 1, :]) * normed + mods[None, :, 0, :...]
    reduce_scatter x1 -> x0, waiting for transfers between devices: 111 us -> none  [on_device(): lax.psum_scatter(jnp.einsum('tse,ed->tsd', rows, out_weight, preferred_el...]
    pallas_call x0 -> x5, Pallas kernels: none -> 40.3 us  [the longest x4 32.1 us: attend(): pl.pallas_call(functools.partial(attend_kernel, hp, head_dim), grid=(head...]
    dot_general x12 -> x2, matrix products: 37.7 us -> 2.4 us  [the longest x1 2.05 us: on_device(): jnp.einsum('ad,bd->ab', centred, centred, precision=lax.Precision.HIGHEST)]
    ppermute x12 -> x18, waiting for transfers between devices: 5.71 us -> 36.7 us  [the longest x14 36.6 us: exchange(): return lax.ppermute(value, axis, [(i, i ^ bit) for i in range(count)])]
    all_gather x0 -> x2, blocking collectives: none -> 22.9 us  [gather_tokens(): return (queries, lax.all_gather(queries, 'row', axis=0, tiled=False))]
    conv_general_dilated x3, matrix products: 5.3 us -> 14.9 us  [conv_valid(): lax.conv_general_dilated(field[None], kernel, (1, 1), 'VALID', dimension_...]
    unnamed x51 -> x44, local copies, waits for them, and re-layouts: 3.11 us -> 11.7 us
  transfers between devices with their start and end apart: 16 -> 18, of which waited for: 10 -> 6; matrix products, arithmetic and copies ran while one was open for 5% -> 16% of each run, Pallas kernels for 0% -> 24%
where the time goes in v1:
time: 167 us
  Pallas kernels  40.3 us (24%)
  waiting for transfers between devices  36.7 us (22%)
  starting transfers between devices  25.9 us (16%)
  blocking collectives  22.9 us (14%)
  matrix products  17.3 us (10%)
  local copies, waits for them, and re-layouts  15.8 us (9%)
  other arithmetic  7.03 us (4%)
    ppermute x14, waiting for transfers between devices, exchange(): return lax.ppermute(value, axis, [(i, i ^ bit) for i in range(count)])  36.6 us
    pallas_call x4, Pallas kernels, attend(): pl.pallas_call(functools.partial(attend_kernel, hp, head_dim), grid=(head...  32.1 us
    all_gather x2, blocking collectives, gather_tokens(): return (queries, lax.all_gather(queries, 'row', axis=0, tiled=False))  22.9 us
    ppermute x14, starting transfers between devices, exchange(): return lax.ppermute(value, axis, [(i, i ^ bit) for i in range(count)])  18.9 us
    conv_general_dilated x3, matrix products, conv_valid(): lax.conv_general_dilated(field[None], kernel, (1, 1), 'VALID', dimension_...  14.9 us
    unnamed x44, local copies, waits for them, and re-layouts  11.7 us
    pallas_call x1, Pallas kernels, fold(): pl.pallas_call(fold_kernel, grid=(heads,), in_specs=[pl.BlockSpec((width,...  8.19 us
    ppermute x2, starting transfers between devices, padded(): before = lax.ppermute(tail, axis, [(i, i + 1) for i in range(count - 1)])  4.13 us
  transfers between devices with their start and end apart: 18, of which 6 were waited for; matrix products, arithmetic and copies ran while one was open for 16% of the time, Pallas kernels for 24%

profile of v1, /device:TPU:0, one launch (start us, length us, event | category | flops | bytes accessed | tf_op | source)
XLA Modules:
  0.0 166.5 jit_solution(11685079150012457019)
XLA Ops:
  0.0 3.0 %collective-permute-start.9 = (bf16[3,32,64]{2,1,0:T(8,128)(2,1)}, bf16[3,32,64]{2,1,0:T(8,128)(2,1)S(1)}, u32[]{:S(2)}, u32[]{:S(2)}) collective-permute-start(bf16[3,32,64]{2,1,0:T(8,128)(2,1)} %bitcast.127), channel_id=1, source_target_pairs={{0,1},{1,0},{2,3},{3,2},{4,5},{5,4},{6,7},{7,6},{8,9},{9,8},{10,11... | collective-permute-start | bytes 36872 | tf_op jit(solution)/shard_map/ppermute | solution.py:226
  3.0 2.6 %collective-permute-start.10 = (bf16[3,32,64]{2,1,0:T(8,128)(2,1)}, bf16[3,32,64]{2,1,0:T(8,128)(2,1)S(1)}, u32[]{:S(2)}, u32[]{:S(2)}) collective-permute-start(bf16[3,32,64]{2,1,0:T(8,128)(2,1)} %bitcast.128), channel_id=1, source_target_pairs={{0,2},{1,3},{2,0},{3,1},{4,6},{5,7},{6,4},{7,5},{8,10},{9,11},{10,... | collective-permute-start | bytes 36872 | tf_op jit(solution)/shard_map/ppermute | solution.py:226
  6.5 1.3 collective-permute-start
  7.7 1.3 collective-permute-start.1
  9.0 1.4 fusion.48
  12.1 1.1 convert_reduce_fusion
  13.2 2.1 %convert_bitcast_fusion = (bf16[1,64,64]{2,1,0:T(8,128)(2,1)S(1)}, bf16[1,64,64]{2,1,0:T(8,128)(2,1)S(1)}) fusion(bf16[64,3072]{1,0:T(8,128)(2,1)} %e_ref.1, f32[64]{0:T(128)S(1)} %broadcast_multiply_fusion), kind=kOutput, calls=%fused_computation.93 | convolution fusion | flops 151408640 | bytes 409856 | tf_op jit(solution)/shard_map/ad,bd->ab/dot_general | solution.py:283
  16.4 5.0 %copy-done.3 = bf16[3072,2304]{1,0:T(8,128)(2,1)S(1)} copy-done((bf16[3072,2304]{1,0:T(8,128)(2,1)S(1)}, bf16[3072,2304]{1,0:T(8,128)(2,1)}, u32[]{:S(2)}) %copy-start.3) | copy-done | bytes 14155800
  22.4 8.2 %shard_map.127.m_ref = f32[6,4,72,384]{3,2,1,0:T(8,128)S(1)} custom-call(bf16[64,3072]{1,0:T(8,128)(2,1)S(1)} %copy-done.4, f32[4,3072]{1,0:T(4,128)S(1)} %slice_bitcast_fusion.5.scale_ref, bf16[16,3072]{1,0:T(8,128)(2,1)S(1)} %maximum_maximum_fusion.shift_ref, bf16[3072,2304]{1,0:T(8,128)(2,1)S(1)} %copy-done.3), custom_call_target="tpu_custom_call" | custom-call | flops 3850371072 | bytes 14155776 | tf_op jit(solution)/shard_map/pallas_call | solution.py:90
  30.7 14.5 %all-gather.1 = bf16[32,3,32,64]{3,2,1,0:T(8,128)(2,1)S(1)} all-gather(bf16[4,3,32,64]{3,2,1,0:T(8,128)(2,1)S(1)} %pad_maximum_fusion.3.query_ref), channel_id=3, replica_groups=mesh['row'=8,'col'=4] {'row'}, dimensions={0}, use_global_device_ids=true | all-gather | bytes 442368 | tf_op jit(solution)/shard_map/all_gather | solution.py:232
  45.2 2.3 %copy-done.1 = bf16[768,3072]{1,0:T(8,128)(2,1)S(1)} copy-done((bf16[768,3072]{1,0:T(8,128)(2,1)S(1)}, bf16[768,3072]{1,0:T(8,128)(2,1)}, u32[]{:S(2)}) %copy-start.1) | copy-done | bytes 4718616
  47.5 8.6 %shard_map.129 = (f32[2,32,3072]{2,1,0:T(8,128)S(1)}, bf16[2,32,3072]{2,1,0:T(8,128)(2,1)}) custom-call(bf16[8,4,3,32,64]{4,3,2,1,0:T(8,128)(2,1)S(1)} %bitcast.119, bf16[4,3,32,64]{3,2,1,0:T(8,128)(2,1)S(1)} %pad_maximum_fusion.3.query_ref, bf16[2,64,64]{2,1,0:T(8,128)(2,1)S(1)} %pad_maximum_fusion.5.gram_ref, f32[6,4,72,384]{3,2,1,0:T(8,128)S(1)} %shard_map.127.m_ref, ...), custom_call_target="tpu_custom_call" | custom-call | flops 2214592512 | bytes 5898240 | tf_op jit(solution)/shard_map/pallas_call | solution.py:191
  57.0 7.9 %shard_map.130 = (f32[2,32,3072]{2,1,0:T(8,128)S(1)}, bf16[2,32,3072]{2,1,0:T(8,128)(2,1)S(1)}) custom-call(bf16[8,4,3,32,64]{4,3,2,1,0:T(8,128)(2,1)S(1)} %bitcast.120, bf16[4,3,32,64]{3,2,1,0:T(8,128)(2,1)S(1)} %pad_maximum_fusion.3.query_ref, bf16[2,64,64]{2,1,0:T(8,128)(2,1)S(1)} %pad_maximum_fusion.5.gram_ref, f32[6,4,72,384]{3,2,1,0:T(8,128)S(1)} %shard_map.127.m_ref, ...), custom_call_target="tpu_custom_call" | custom-call | flops 2214592512 | bytes 5898240 | tf_op jit(solution)/shard_map/pallas_call | solution.py:191
  65.1 2.9 %collective-permute-start.2 = (bf16[14,3,512]{2,1,0:T(4,128)(2,1)S(1)}, bf16[14,3,512]{2,1,0:T(4,128)(2,1)S(1)}, u32[]{:S(2)}, u32[]{:S(2)}) collective-permute-start(bf16[14,3,512]{2,1,0:T(4,128)(2,1)S(1)} %get-tuple-element.27), channel_id=1, source_target_pairs={{0,1},{1,2},{2,3},{4,5},{5,6},{6,7},{8,9},{9,10},{10,11},{12,13},{... | collective-permute-start | bytes 129032 | tf_op jit(solution)/shard_map/ppermute | solution.py:38
  67.9 1.6 collective-permute-start.3
  69.6 7.9 %shard_map.131 = (f32[2,32,3072]{2,1,0:T(8,128)S(1)}, bf16[2,32,3072]{2,1,0:T(8,128)(2,1)S(1)}) custom-call(bf16[8,4,3,32,64]{4,3,2,1,0:T(8,128)(2,1)S(1)} %bitcast.121, bf16[4,3,32,64]{3,2,1,0:T(8,128)(2,1)S(1)} %pad_maximum_fusion.3.query_ref, bf16[2,64,64]{2,1,0:T(8,128)(2,1)S(1)} %pad_maximum_fusion.5.gram_ref, f32[6,4,72,384]{3,2,1,0:T(8,128)S(1)} %shard_map.127.m_ref, ...), custom_call_target="tpu_custom_call" | custom-call | flops 2214592512 | bytes 5898240 | tf_op jit(solution)/shard_map/pallas_call | solution.py:191
  77.4 2.7 %collective-permute-start.12 = (bf16[2,32,3072]{2,1,0:T(8,128)(2,1)}, bf16[2,32,3072]{2,1,0:T(8,128)(2,1)}, u32[]{:S(2)}, u32[]{:S(2)}) collective-permute-start(bf16[2,32,3072]{2,1,0:T(8,128)(2,1)} %get-tuple-element.16), channel_id=1, source_target_pairs={{0,1},{1,0},{2,3},{3,2},{4,5},{5,4},{6,7},{7,6},{8,9},{9,8},{10,11... | collective-permute-start | bytes 1179656 | tf_op jit(solution)/shard_map/ppermute | solution.py:226
  80.6 7.0 %fusion = f32[1,12,20,512]{3,0,2,1:T(1,128)S(1)} fusion(bf16[3,3,512,512]{3,2,1,0:T(8,128)(2,1)S(1)} %bitcast.147, bf16[1,14,22,512]{3,2,1,0:T(8,128)(2,1)S(1)} %fusion.5), kind=kOutput, calls=%fused_computation.2 | convolution fusion | flops 1132707840 | bytes 5525504 | tf_op jit(solution)/shard_map/conv_general_dilated | solution.py:23
  87.7 6.8 %fusion.11 = f32[1,10,18,512]{3,0,2,1:T(1,128)S(1)} fusion(bf16[3,3,512,512]{3,2,1,0:T(8,128)(2,1)S(1)} %bitcast.149, pred[12,20]{1,0:T(8,128)(4,1)S(1)} %broadcast_and_fusion, f32[1,12,20,512]{3,0,2,1:T(1,128)S(1)} %fusion), kind=kOutput, calls=%fused_computation.28 | convolution fusion | flops 850083840 | bytes 5578992 | tf_op jit(solution)/shard_map/conv_general_dilated | solution.py:23
  96.0 2.0 %collective-permute-start.4 = (bf16[1,32,64]{2,1,0:T(8,128)(2,1)S(1)}, bf16[1,32,64]{2,1,0:T(8,128)(2,1)S(1)}, u32[]{:S(2)}, u32[]{:S(2)}) collective-permute-start(bf16[1,32,64]{2,1,0:T(8,128)(2,1)S(1)} %fusion.54), channel_id=1, source_target_pairs={{0,1},{1,0},{2,3},{3,2},{4,5},{5,4},{6,7},{7,6},{8,9},{9,8},{10,11... | collective-permute-start | bytes 12296 | tf_op jit(solution)/shard_map/ppermute | solution.py:226
  98.0 3.5 %collective-permute-start.5 = (bf16[1,32,64]{2,1,0:T(8,128)(2,1)S(1)}, bf16[1,32,64]{2,1,0:T(8,128)(2,1)S(1)}, u32[]{:S(2)}, u32[]{:S(2)}) collective-permute-start(bf16[1,32,64]{2,1,0:T(8,128)(2,1)S(1)} %fusion.54), channel_id=1, source_target_pairs={{0,2},{1,3},{2,0},{3,1},{4,6},{5,7},{6,4},{7,5},{8,10},{9,11},{10,... | collective-permute-start | bytes 12296 | tf_op jit(solution)/shard_map/ppermute | solution.py:226
  103.1 4.0 %collective-permute-done.6 = bf16[1,32,64]{2,1,0:T(8,128)(2,1)S(1)} collective-permute-done((bf16[1,32,64]{2,1,0:T(8,128)(2,1)S(1)}, bf16[1,32,64]{2,1,0:T(8,128)(2,1)S(1)}, u32[]{:S(2)}, u32[]{:S(2)}) %collective-permute-start.6) | collective-permute-done | bytes 4128 | tf_op jit(solution)/shard_map/ppermute | solution.py:226
  107.1 8.4 %all-gather = bf16[32,1,32,64]{3,2,1,0:T(8,128)(2,1)S(1)} all-gather(bf16[4,1,32,64]{3,2,1,0:T(8,128)(2,1)S(1)} %pad_maximum_fusion.4.query_ref), channel_id=2, replica_groups=mesh['row'=8,'col'=4] {'row'}, dimensions={0}, use_global_device_ids=true | all-gather | bytes 147456 | tf_op jit(solution)/shard_map/all_gather | solution.py:232
  115.5 2.3 %copy-done.2 = bf16[768,3072]{1,0:T(8,128)(2,1)S(1)} copy-done((bf16[768,3072]{1,0:T(8,128)(2,1)S(1)}, bf16[768,3072]{1,0:T(8,128)(2,1)}, u32[]{:S(2)}) %copy-start.2) | copy-done | bytes 4718616
  117.8 7.8 %shard_map.128 = (f32[2,32,3072]{2,1,0:T(8,128)S(1)}, bf16[2,32,3072]{2,1,0:T(8,128)(2,1)S(1)}) custom-call(bf16[8,4,1,32,64]{4,3,2,1,0:T(8,128)(2,1)S(1)} %bitcast.122, bf16[4,1,32,64]{3,2,1,0:T(8,128)(2,1)S(1)} %pad_maximum_fusion.4.query_ref, bf16[2,64,64]{2,1,0:T(8,128)(2,1)S(1)} %pad_maximum_fusion.5.gram_ref, f32[6,4,72,384]{3,2,1,0:T(8,128)S(1)} %shard_map.127.m_ref, ...), custom_call_target="tpu_custom_call" | custom-call | flops 2214592512 | bytes 5898240 | tf_op jit(solution)/shard_map/pallas_call | solution.py:191
  125.8 1.1 convert_add_fusion.2
  128.8 2.3 %collective-permute-start.15 = (bf16[1,32,3072]{2,1,0:T(8,128)(2,1)S(1)}, bf16[1,32,3072]{2,1,0:T(8,128)(2,1)S(1)}, u32[]{:S(2)}, u32[]{:S(2)}) collective-permute-start(bf16[1,32,3072]{2,1,0:T(8,128)(2,1)S(1)} %slice.204), channel_id=1, source_target_pairs={{0,2},{1,3},{2,0},{3,1},{4,6},{5,7},{6,4},{7,5},{8,10},{9,11},{10,... | collective-permute-start | bytes 589832 | tf_op jit(solution)/shard_map/ppermute | solution.py:226
  131.9 10.0 %collective-permute-done.7 = bf16[2,32,3072]{2,1,0:T(8,128)(2,1)S(1)} collective-permute-done((bf16[2,32,3072]{2,1,0:T(8,128)(2,1)S(1)}, bf16[2,32,3072]{2,1,0:T(8,128)(2,1)S(1)}, u32[]{:S(2)}, u32[]{:S(2)}) %collective-permute-start.7) | collective-permute-done | bytes 393248 | tf_op jit(solution)/shard_map/ppermute | solution.py:226
  142.9 13.9 %collective-permute-done.15 = bf16[1,32,3072]{2,1,0:T(8,128)(2,1)S(1)} collective-permute-done((bf16[1,32,3072]{2,1,0:T(8,128)(2,1)S(1)}, bf16[1,32,3072]{2,1,0:T(8,128)(2,1)S(1)}, u32[]{:S(2)}, u32[]{:S(2)}) %collective-permute-start.15) | collective-permute-done | bytes 196640 | tf_op jit(solution)/shard_map/ppermute | solution.py:226
  156.7 4.2 %collective-permute-done.17 = bf16[1,32,3072]{2,1,0:T(8,128)(2,1)S(1)} collective-permute-done((bf16[1,32,3072]{2,1,0:T(8,128)(2,1)S(1)}, bf16[1,32,3072]{2,1,0:T(8,128)(2,1)S(1)}, u32[]{:S(2)}, u32[]{:S(2)}) %collective-permute-start.17) | collective-permute-done | bytes 196640 | tf_op jit(solution)/shard_map/ppermute | solution.py:226
  160.9 3.6 %collective-permute-done.8 = bf16[1,32,3072]{2,1,0:T(8,128)(2,1)S(1)} collective-permute-done((bf16[1,32,3072]{2,1,0:T(8,128)(2,1)S(1)}, bf16[1,32,3072]{2,1,0:T(8,128)(2,1)S(1)}, u32[]{:S(2)}, u32[]{:S(2)}) %collective-permute-start.8) | collective-permute-done | bytes 196640 | tf_op jit(solution)/shard_map/ppermute | solution.py:226
  165.0 1.5 copy.27
  (104 shorter events, 13.2 us)
Async XLA Ops:
  0.0 94.7 %copy-start = (bf16[3,3,512,16]{2,3,1,0:T(8,128)(2,1)S(1)}, bf16[3,3,512,16]{2,3,1,0:T(8,128)(2,1)}, u32[]{:S(2)}) copy-start(bf16[3,3,512,16]{2,3,1,0:T(8,128)(2,1)} %param.16) | copy-start | bytes 442372
  0.0 30.6 %collective-permute-start.9 = (bf16[3,32,64]{2,1,0:T(8,128)(2,1)}, bf16[3,32,64]{2,1,0:T(8,128)(2,1)S(1)}, u32[]{:S(2)}, u32[]{:S(2)}) collective-permute-start(bf16[3,32,64]{2,1,0:T(8,128)(2,1)} %bitcast.127), channel_id=1, source_target_pairs={{0,1},{1,0},{2,3},{3,2},{4,5},{5,4},{6,7},{7,6},{8,9},{9,8},{10,11... | collective-permute-start | bytes 36872 | tf_op jit(solution)/shard_map/ppermute | solution.py:226
  3.0 27.6 %collective-permute-start.10 = (bf16[3,32,64]{2,1,0:T(8,128)(2,1)}, bf16[3,32,64]{2,1,0:T(8,128)(2,1)S(1)}, u32[]{:S(2)}, u32[]{:S(2)}) collective-permute-start(bf16[3,32,64]{2,1,0:T(8,128)(2,1)} %bitcast.128), channel_id=1, source_target_pairs={{0,2},{1,3},{2,0},{3,1},{4,6},{5,7},{6,4},{7,5},{8,10},{9,11},{10,... | collective-permute-start | bytes 36872 | tf_op jit(solution)/shard_map/ppermute | solution.py:226
  5.6 25.0 %collective-permute-start.11 = (bf16[3,32,64]{2,1,0:T(8,128)(2,1)}, bf16[3,32,64]{2,1,0:T(8,128)(2,1)S(1)}, u32[]{:S(2)}, u32[]{:S(2)}) collective-permute-start(bf16[3,32,64]{2,1,0:T(8,128)(2,1)} %bitcast.129), channel_id=1, source_target_pairs={{0,3},{1,2},{2,1},{3,0},{4,7},{5,6},{6,5},{7,4},{8,11},{9,10},{10,... | collective-permute-start | bytes 36872 | tf_op jit(solution)/shard_map/ppermute | solution.py:226
  6.5 58.5 %collective-permute-start = (bf16[3,16,512]{2,1,0:T(8,128)(2,1)S(1)}, bf16[3,16,512]{2,1,0:T(8,128)(2,1)S(1)}, u32[]{:S(2)}, u32[]{:S(2)}) collective-permute-start(bf16[3,16,512]{2,1,0:T(8,128)(2,1)S(1)} %get-tuple-element.38), channel_id=1, source_target_pairs={{0,4},{4,8},{8,12},{12,16},{16,20},{20,24},{24,28},{1,5},{5,9},{9,... | collective-permute-start | bytes 147464 | tf_op jit(solution)/shard_map/ppermute | solution.py:38
  7.7 57.2 %collective-permute-start.1 = (bf16[3,16,512]{2,1,0:T(8,128)(2,1)S(1)}, bf16[3,16,512]{2,1,0:T(8,128)(2,1)S(1)}, u32[]{:S(2)}, u32[]{:S(2)}) collective-permute-start(bf16[3,16,512]{2,1,0:T(8,128)(2,1)S(1)} %get-tuple-element.37), channel_id=1, source_target_pairs={{4,0},{8,4},{12,8},{16,12},{20,16},{24,20},{28,24},{5,1},{9,5},{13... | collective-permute-start | bytes 147464 | tf_op jit(solution)/shard_map/ppermute | solution.py:39
  22.4 8.3 %copy-start.14 = (bf16[32,3,64]{2,0,1:T(8,128)(2,1)S(1)}, bf16[32,3,64]{2,0,1:T(8,128)(2,1)}, u32[]{:S(2)}) copy-start(bf16[32,3,64]{2,0,1:T(8,128)(2,1)} %param.18) | copy-start | bytes 36868
  57.0 7.9 %copy-start.13 = (bf16[8,16,512]{2,1,0:T(8,128)(2,1)S(1)}, bf16[8,16,512]{2,1,0:T(8,128)(2,1)}, u32[]{:S(2)}) copy-start(bf16[8,16,512]{2,1,0:T(8,128)(2,1)} %param.13) | copy-start | bytes 393220
  64.9 15.6 %copy-start.6 = (f32[2,32,3072]{2,1,0:T(8,128)}, f32[2,32,3072]{2,1,0:T(8,128)S(1)}, u32[]{:S(2)}) copy-start(f32[2,32,3072]{2,1,0:T(8,128)S(1)} %get-tuple-element.17) | copy-start | bytes 2359300
  65.0 15.6 %slice-start = ((s8[4718592]{0:T(1024)(128)(4,1)}), s8[4194304]{0:T(1024)(128)(4,1)S(1)}, s32[]{:S(2)}) async-start(s8[4718592]{0:T(1024)(128)(4,1)} %bitcast.146), calls=%async_computation | async-start | bytes 8388608
  65.1 15.2 %collective-permute-start.2 = (bf16[14,3,512]{2,1,0:T(4,128)(2,1)S(1)}, bf16[14,3,512]{2,1,0:T(4,128)(2,1)S(1)}, u32[]{:S(2)}, u32[]{:S(2)}) collective-permute-start(bf16[14,3,512]{2,1,0:T(4,128)(2,1)S(1)} %get-tuple-element.27), channel_id=1, source_target_pairs={{0,1},{1,2},{2,3},{4,5},{5,6},{6,7},{8,9},{9,10},{10,11},{12,13},{... | collective-permute-start | bytes 129032 | tf_op jit(solution)/shard_map/ppermute | solution.py:38
  67.9 12.6 %slice-start.1 = ((s8[4718592]{0:T(1024)(128)(4,1)}), s8[524288]{0:T(1024)(128)(4,1)S(1)}, s32[]{:S(2)}) async-start(s8[4718592]{0:T(1024)(128)(4,1)} %bitcast.146), calls=%async_computation.1 | async-start | bytes 1048576
  67.9 12.3 %collective-permute-start.3 = (bf16[14,3,512]{2,1,0:T(4,128)(2,1)S(1)}, bf16[14,3,512]{2,1,0:T(4,128)(2,1)S(1)}, u32[]{:S(2)}, u32[]{:S(2)}) collective-permute-start(bf16[14,3,512]{2,1,0:T(4,128)(2,1)S(1)} %get-tuple-element.28), channel_id=1, source_target_pairs={{1,0},{2,1},{3,2},{5,4},{6,5},{7,6},{9,8},{10,9},{11,10},{13,12},{... | collective-permute-start | bytes 129032 | tf_op jit(solution)/shard_map/ppermute | solution.py:39
  69.5 18.1 %slice-start.2 = ((s8[4718592]{0:T(1024)(128)(4,1)}), s8[4194304]{0:T(1024)(128)(4,1)S(1)}, s32[]{:S(2)}) async-start(s8[4718592]{0:T(1024)(128)(4,1)} %bitcast.148), calls=%async_computation.2 | async-start | bytes 8388608
  77.4 10.2 %copy-start.10 = (f32[2,32,3072]{2,1,0:T(8,128)}, f32[2,32,3072]{2,1,0:T(8,128)S(1)}, u32[]{:S(2)}) copy-start(f32[2,32,3072]{2,1,0:T(8,128)S(1)} %get-tuple-element.19) | copy-start | bytes 2359300
  77.4 10.2 %copy-start.12 = (bf16[2,32,3072]{2,1,0:T(8,128)(2,1)}, bf16[2,32,3072]{2,1,0:T(8,128)(2,1)S(1)}, u32[]{:S(2)}) copy-start(bf16[2,32,3072]{2,1,0:T(8,128)(2,1)S(1)} %get-tuple-element.20) | copy-start | bytes 1179652
  77.4 48.3 %collective-permute-start.12 = (bf16[2,32,3072]{2,1,0:T(8,128)(2,1)}, bf16[2,32,3072]{2,1,0:T(8,128)(2,1)}, u32[]{:S(2)}, u32[]{:S(2)}) collective-permute-start(bf16[2,32,3072]{2,1,0:T(8,128)(2,1)} %get-tuple-element.16), channel_id=1, source_target_pairs={{0,1},{1,0},{2,3},{3,2},{4,5},{5,4},{6,7},{7,6},{8,9},{9,8},{10,11... | collective-permute-start | bytes 1179656 | tf_op jit(solution)/shard_map/ppermute | solution.py:226
  80.2 47.5 %collective-permute-start.14 = (bf16[2,32,3072]{2,1,0:T(8,128)(2,1)S(1)}, bf16[2,32,3072]{2,1,0:T(8,128)(2,1)}, u32[]{:S(2)}, u32[]{:S(2)}) collective-permute-start(bf16[2,32,3072]{2,1,0:T(8,128)(2,1)S(1)} %get-tuple-element.18), channel_id=1, source_target_pairs={{0,1},{1,0},{2,3},{3,2},{4,5},{5,4},{6,7},{7,6},{8,9},{9,8},{10,11... | collective-permute-start | bytes 1179656 | tf_op jit(solution)/shard_map/ppermute | solution.py:226
  80.6 7.1 %slice-start.3 = ((s8[4718592]{0:T(1024)(128)(4,1)}), s8[524288]{0:T(1024)(128)(4,1)S(1)}, s32[]{:S(2)}) async-start(s8[4718592]{0:T(1024)(128)(4,1)} %bitcast.148), calls=%async_computation.3 | async-start | bytes 1048576
  96.0 5.6 %collective-permute-start.4 = (bf16[1,32,64]{2,1,0:T(8,128)(2,1)S(1)}, bf16[1,32,64]{2,1,0:T(8,128)(2,1)S(1)}, u32[]{:S(2)}, u32[]{:S(2)}) collective-permute-start(bf16[1,32,64]{2,1,0:T(8,128)(2,1)S(1)} %fusion.54), channel_id=1, source_target_pairs={{0,1},{1,0},{2,3},{3,2},{4,5},{5,4},{6,7},{7,6},{8,9},{9,8},{10,11... | collective-permute-start | bytes 12296 | tf_op jit(solution)/shard_map/ppermute | solution.py:226
  98.0 5.1 %collective-permute-start.5 = (bf16[1,32,64]{2,1,0:T(8,128)(2,1)S(1)}, bf16[1,32,64]{2,1,0:T(8,128)(2,1)S(1)}, u32[]{:S(2)}, u32[]{:S(2)}) collective-permute-start(bf16[1,32,64]{2,1,0:T(8,128)(2,1)S(1)} %fusion.54), channel_id=1, source_target_pairs={{0,2},{1,3},{2,0},{3,1},{4,6},{5,7},{6,4},{7,5},{8,10},{9,11},{10,... | collective-permute-start | bytes 12296 | tf_op jit(solution)/shard_map/ppermute | solution.py:226
  101.5 5.6 %collective-permute-start.6 = (bf16[1,32,64]{2,1,0:T(8,128)(2,1)S(1)}, bf16[1,32,64]{2,1,0:T(8,128)(2,1)S(1)}, u32[]{:S(2)}, u32[]{:S(2)}) collective-permute-start(bf16[1,32,64]{2,1,0:T(8,128)(2,1)S(1)} %fusion.54), channel_id=1, source_target_pairs={{0,3},{1,2},{2,1},{3,0},{4,7},{5,6},{6,5},{7,4},{8,11},{9,10},{10,... | collective-permute-start | bytes 12296 | tf_op jit(solution)/shard_map/ppermute | solution.py:226
  101.6 29.5 %collective-permute-start.16 = (bf16[2,32,3072]{2,1,0:T(8,128)(2,1)}, bf16[2,32,3072]{2,1,0:T(8,128)(2,1)S(1)}, u32[]{:S(2)}, u32[]{:S(2)}) collective-permute-start(bf16[2,32,3072]{2,1,0:T(8,128)(2,1)} %copy-done.12), channel_id=1, source_target_pairs={{0,1},{1,0},{2,3},{3,2},{4,5},{5,4},{6,7},{7,6},{8,9},{9,8},{10,11... | collective-permute-start | bytes 1179656 | tf_op jit(solution)/shard_map/ppermute | solution.py:226
  117.8 7.9 %copy-start.9 = (f32[2,32,3072]{2,1,0:T(8,128)S(1)}, f32[2,32,3072]{2,1,0:T(8,128)}, u32[]{:S(2)}) copy-start(f32[2,32,3072]{2,1,0:T(8,128)} %copy-done.8) | copy-start | bytes 2359300
  117.8 9.8 %copy-start.7 = (f32[2,32,3072]{2,1,0:T(8,128)S(1)}, f32[2,32,3072]{2,1,0:T(8,128)}, u32[]{:S(2)}) copy-start(f32[2,32,3072]{2,1,0:T(8,128)} %copy-done.6) | copy-start | bytes 2359300
  117.8 13.3 %copy-start.11 = (f32[2,32,3072]{2,1,0:T(8,128)S(1)}, f32[2,32,3072]{2,1,0:T(8,128)}, u32[]{:S(2)}) copy-start(f32[2,32,3072]{2,1,0:T(8,128)} %copy-done.10) | copy-start | bytes 2359300
  125.7 16.3 %collective-permute-start.7 = (bf16[2,32,3072]{2,1,0:T(8,128)(2,1)S(1)}, bf16[2,32,3072]{2,1,0:T(8,128)(2,1)S(1)}, u32[]{:S(2)}, u32[]{:S(2)}) collective-permute-start(bf16[2,32,3072]{2,1,0:T(8,128)(2,1)S(1)} %get-tuple-element.14), channel_id=1, source_target_pairs={{0,1},{1,0},{2,3},{3,2},{4,5},{5,4},{6,7},{7,6},{8,9},{9,8},{10,11... | collective-permute-start | bytes 1179656 | tf_op jit(solution)/shard_map/ppermute | solution.py:226
  125.8 16.7 %copy-start.5 = (bf16[64,3072]{1,0:T(8,128)(2,1)S(1)}, bf16[64,3072]{1,0:T(8,128)(2,1)}, u32[]{:S(2)}) copy-start(bf16[64,3072]{1,0:T(8,128)(2,1)} %e_ref.1) | copy-start | bytes 1179652
  126.9 15.9 %collective-permute-start.13 = (bf16[1,32,3072]{2,1,0:T(8,128)(2,1)S(1)}, bf16[1,32,3072]{2,1,0:T(8,128)(2,1)S(1)}, u32[]{:S(2)}, u32[]{:S(2)}) collective-permute-start(bf16[1,32,3072]{2,1,0:T(8,128)(2,1)S(1)} %slice.205), channel_id=1, source_target_pairs={{0,2},{1,3},{2,0},{3,1},{4,6},{5,7},{6,4},{7,5},{8,10},{9,11},{10,... | collective-permute-start | bytes 589832 | tf_op jit(solution)/shard_map/ppermute | solution.py:226
  128.8 27.9 %collective-permute-start.15 = (bf16[1,32,3072]{2,1,0:T(8,128)(2,1)S(1)}, bf16[1,32,3072]{2,1,0:T(8,128)(2,1)S(1)}, u32[]{:S(2)}, u32[]{:S(2)}) collective-permute-start(bf16[1,32,3072]{2,1,0:T(8,128)(2,1)S(1)} %slice.204), channel_id=1, source_target_pairs={{0,2},{1,3},{2,0},{3,1},{4,6},{5,7},{6,4},{7,5},{8,10},{9,11},{10,... | collective-permute-start | bytes 589832 | tf_op jit(solution)/shard_map/ppermute | solution.py:226
  131.2 29.7 %collective-permute-start.17 = (bf16[1,32,3072]{2,1,0:T(8,128)(2,1)S(1)}, bf16[1,32,3072]{2,1,0:T(8,128)(2,1)S(1)}, u32[]{:S(2)}, u32[]{:S(2)}) collective-permute-start(bf16[1,32,3072]{2,1,0:T(8,128)(2,1)S(1)} %slice.203), channel_id=1, source_target_pairs={{0,2},{1,3},{2,0},{3,1},{4,6},{5,7},{6,4},{7,5},{8,10},{9,11},{10,... | collective-permute-start | bytes 589832 | tf_op jit(solution)/shard_map/ppermute | solution.py:226
  142.0 22.5 %collective-permute-start.8 = (bf16[1,32,3072]{2,1,0:T(8,128)(2,1)S(1)}, bf16[1,32,3072]{2,1,0:T(8,128)(2,1)S(1)}, u32[]{:S(2)}, u32[]{:S(2)}) collective-permute-start(bf16[1,32,3072]{2,1,0:T(8,128)(2,1)S(1)} %slice.206), channel_id=1, source_target_pairs={{0,2},{1,3},{2,0},{3,1},{4,6},{5,7},{6,4},{7,5},{8,10},{9,11},{10,... | collective-permute-start | bytes 589832 | tf_op jit(solution)/shard_map/ppermute | solution.py:226
  (6 other events, 12.8 us)

commit v2 on v1

v2 whole, which is shorter than its diff:
```python
import functools
import math

import jax
import jax.numpy as jnp
from jax import lax
from jax.experimental import pallas as pl
from jax.experimental.pallas import tpu as pltpu
from jax.sharding import PartitionSpec as P

norm_eps = 1e-06
latent_shift = 0.1159
latent_scale = 0.3611
bf16 = jnp.bfloat16
f32 = jnp.float32


def swish(field):
    return (field / (1.0 + jnp.exp(-field))).astype(bf16)


def shifted(dst_ref, act):
    cols, rows, _ = act.shape
    dst_ref[0, 0:cols] = pltpu.roll(act, 1, 1).astype(bf16)
    dst_ref[1, 0:cols] = act.astype(bf16)
    dst_ref[2, 0:cols] = pltpu.roll(act, rows - 1, 1).astype(bf16)


def encode_kernel(
    place_ref, left_ref, mid_ref, right_ref, f0_ref, f1_ref, f2_ref, s0_ref, s1_ref, s2_ref,
    last_ref, out_ref, x_ref, s_ref, acc_ref,
):
    step = pl.program_id(0)
    wide, rows, channels = x_ref.shape
    tile_cols, tile_rows, _ = out_ref.shape
    first_ref = (f0_ref, f1_ref, f2_ref)
    second_ref = (s0_ref, s1_ref, s2_ref)

    def masked(act, reach):
        shape = act.shape
        col = lax.broadcasted_iota(jnp.int32, shape, 0) + (place_ref[1] - reach)
        row = lax.broadcasted_iota(jnp.int32, shape, 1)
        row = jnp.where(row < tile_rows + 3, row, row - rows) + place_ref[0]
        ok = (row >= 0) & (row < place_ref[2]) & (col >= 0) & (col < place_ref[3])
        return jnp.where(ok, act, 0.0)

    def taps(w_ref, dy, cols):
        total = None
        for dx in range(3):
            lhs = s_ref[dy, dx : dx + cols].reshape(cols * rows, channels)
            part = jnp.dot(lhs, w_ref[dx][...], preferred_element_type=f32)
            total = part if total is None else total + part
        return total.reshape(cols, rows, total.shape[-1])

    @pl.when(step == 0)
    def _():
        x_ref[0:3] = left_ref[...].astype(f32)
        x_ref[3 : 3 + tile_cols] = mid_ref[...].astype(f32)
        x_ref[3 + tile_cols :] = right_ref[...].astype(f32)
        shifted(s_ref, swish(x_ref[...]).astype(f32))
        acc_ref[...] = taps(first_ref, 0, wide - 2)

    for dy in (1, 2):

        @pl.when(step == dy)
        def _():
            acc_ref[...] += taps(first_ref, dy, wide - 2)

    @pl.when(step == 2)
    def _():
        inner = acc_ref[...].astype(bf16).astype(f32)
        shifted(s_ref, masked(swish(inner).astype(f32), 2))

    @pl.when(step == 3)
    def _():
        acc_ref[0 : wide - 4] = x_ref[2 : wide - 2] + taps(second_ref, 0, wide - 4)

    for dy in (1, 2):

        @pl.when(step == 3 + dy)
        def _():
            acc_ref[0 : wide - 4] += taps(second_ref, dy, wide - 4)

    @pl.when(step == 5)
    def _():
        block = acc_ref[0 : wide - 4].astype(bf16).astype(f32)
        shifted(s_ref, masked(swish(block).astype(f32), 1))
        latent = None
        for dy in range(3):
            for dx in range(3):
                lhs = s_ref[dy, dx : dx + wide - 6].reshape(-1, channels)
                part = lax.dot_general(
                    lhs, last_ref[dy, dx], (((1,), (1,)), ((), ())), preferred_element_type=f32
                )
                latent = part if latent is None else latent + part
        latent = ((latent - latent_shift) * latent_scale).reshape(tile_cols, rows, -1)
        out_ref[...] = latent[:, :tile_rows]


def edges(features):
    nr = lax.axis_size("row")
    turned = features.transpose(1, 0, 2)
    tile_cols, tile_rows, channels = turned.shape
    above = lax.ppermute(turned[:, -3:], "row", [(i, i + 1) for i in range(nr - 1)])
    below = lax.ppermute(turned[:, :3], "row", [(i + 1, i) for i in range(nr - 1)])
    spare = -(tile_rows + 6) % 16
    gap = jnp.zeros((tile_cols, spare, channels), bf16)
    return jnp.concatenate([turned, below, gap, above], axis=1)


def sides(mid):
    nc = lax.axis_size("col")
    left = lax.ppermute(mid[-3:], "col", [(i, i + 1) for i in range(nc - 1)])
    right = lax.ppermute(mid[:3], "col", [(i + 1, i) for i in range(nc - 1)])
    return left, right


def encode(left, mid, right, tile_rows, conv_first, conv_second, conv_last):
    nr, nc = lax.axis_size("row"), lax.axis_size("col")
    tile_cols, rows, channels = mid.shape
    wide = tile_cols + 6
    place = jnp.stack(
        [
            lax.axis_index("row") * tile_rows,
            lax.axis_index("col") * tile_cols,
            nr * tile_rows,
            nc * tile_cols,
        ]
    ).astype(jnp.int32)
    hidden = conv_first.shape[3]
    latents = conv_last.shape[3]
    last = conv_last.transpose(0, 1, 3, 2)

    def whole(array):
        return pl.BlockSpec(array.shape, lambda i: (0,) * array.ndim)

    return pl.pallas_call(
        encode_kernel,
        grid=(6,),
        in_specs=[
            pl.BlockSpec(memory_space=pltpu.SMEM),
            whole(left),
            whole(mid),
            whole(right),
            *[
                pl.BlockSpec(
                    (None, None, channels, hidden), lambda i, x=x: (jnp.minimum(i, 2), x, 0, 0)
                )
                for x in range(3)
            ],
            *[
                pl.BlockSpec(
                    (None, None, hidden, channels), lambda i, x=x: (jnp.clip(i - 3, 0, 2), x, 0, 0)
                )
                for x in range(3)
            ],
            whole(last),
        ],
        out_specs=pl.BlockSpec((tile_cols, tile_rows, latents), lambda i: (0, 0, 0)),
        out_shape=jax.ShapeDtypeStruct((tile_cols, tile_rows, latents), f32),
        scratch_shapes=[
            pltpu.VMEM((wide, rows, channels), f32),
            pltpu.VMEM((3, wide, rows, channels), bf16),
            pltpu.VMEM((wide - 2, rows, channels), f32),
        ],
        compiler_params=pltpu.CompilerParams(vmem_limit_bytes=40 * 2**20),
        cost_estimate=pl.CostEstimate(
            flops=2 * 9 * wide * rows * channels * (2 * hidden + latents),
            bytes_accessed=9 * channels * 2 * (2 * hidden + 128),
            transcendentals=3 * wide * rows * channels,
        ),
    )(place, left, mid, right, *[conv_first] * 3, *[conv_second] * 3, last)


def widen(p, gram_ref):
    pf = p.astype(f32)
    pg = jnp.dot(p, gram_ref[0], preferred_element_type=f32)
    pg = pg + jnp.dot(p, gram_ref[1], preferred_element_type=f32)
    var = jnp.sum(pg * pf, axis=1, keepdims=True)
    pn = pf * lax.rsqrt(jnp.maximum(var, 0.0) + norm_eps)
    hi = pn.astype(bf16)
    lo = (pn - hi.astype(f32)).astype(bf16)
    lane = lax.broadcasted_iota(jnp.int32, p.shape, 1)
    ones = jnp.where(lane < 2, 1.0, 0.0).astype(bf16)
    return jnp.concatenate([hi, lo, hi, ones], axis=1)


def attend_kernel(
    hp, head_dim, slot, slots, key_ref, query_ref, gram_ref, m_ref, bias_ref, gain_ref,
    wo_ref, keep_ref, send_ref, kaug_ref, qaug_ref, acc_ref,
):
    step = pl.program_id(0)
    width = key_ref.shape[-1]

    @pl.when(step == 0)
    def _():
        kaug_ref[...] = widen(key_ref[...].reshape(-1, width), gram_ref)
        qaug_ref[...] = widen(query_ref[...].reshape(-1, width), gram_ref)

    kaug = kaug_ref[...]
    qaug = qaug_ref[...]
    outs = []
    for j in range(hp):
        cols = slice(j * 3 * head_dim, (j + 1) * 3 * head_dim)
        m = m_ref[:, cols]
        bias = bias_ref[slot : slot + 1, cols] + bias_ref[slots + slot : slots + slot + 1, cols]
        mhi = m.astype(bf16)
        mlo = (m - mhi.astype(f32)).astype(bf16)
        bhi = bias.astype(bf16).astype(f32)
        blo = bias - bhi
        at = lax.broadcasted_iota(jnp.int32, m.shape, 0)
        low = jnp.where(at == 0, bhi, jnp.where(at == 1, blo, 0.0)).astype(bf16)
        maug = jnp.concatenate([mhi, mhi, mlo, low], axis=0)
        xq = jnp.dot(qaug, maug[:, :head_dim], preferred_element_type=f32)
        xkv = jnp.dot(kaug, maug[:, head_dim:], preferred_element_type=f32)
        xk = xkv[:, :head_dim]
        v = xkv[:, head_dim:].astype(bf16)
        k = (
            xk * lax.rsqrt(jnp.mean(xk * xk, axis=1, keepdims=True) + norm_eps)
        ).astype(bf16)
        q = (
            xq * lax.rsqrt(jnp.mean(xq * xq, axis=1, keepdims=True) + norm_eps) * gain_ref[...]
        ).astype(bf16)
        s = lax.dot_general(q, k, (((1,), (1,)), ((), ())), preferred_element_type=f32)
        e = jnp.exp2(s - jnp.max(s, axis=1, keepdims=True))
        total = jnp.sum(e, axis=1, keepdims=True)
        o = jnp.dot(e.astype(bf16), v, preferred_element_type=f32)
        outs.append((o / total).astype(bf16))
    att = outs[0] if hp == 1 else jnp.concatenate(outs, axis=1)
    part = jnp.dot(att, wo_ref[...], preferred_element_type=f32)

    @pl.when(step == 0)
    def _():
        acc_ref[...] = part

    @pl.when(step > 0)
    def _():
        acc_ref[...] += part

    @pl.when(step == pl.num_programs(0) - 1)
    def _():
        tok = keep_ref.shape[1]
        for i in range(keep_ref.shape[0]):
            keep_ref[i] = acc_ref[2 * i * tok : (2 * i + 1) * tok, :]
            send_ref[i] = acc_ref[(2 * i + 1) * tok : (2 * i + 2) * tok, :].astype(bf16)


def attend(keys, queries, slot, at, gram, folded, gain, out_weight):
    nr, nc, _, tok, width = keys.shape
    slots = folded.shape[0] // width
    head_dim = gain.shape[1]
    heads = folded.shape[1] // (3 * head_dim)
    depth = out_weight.shape[1]
    hp = heads_per_step(heads)
    nk, nq = nr * nc * tok, nc * tok
    half = nc // 2
    spare = folded.shape[0] - slots * width
    out_spec = pl.BlockSpec((half, tok, depth), lambda h: (0, 0, 0))
    return pl.pallas_call(
        functools.partial(attend_kernel, hp, head_dim, slot, slots),
        grid=(heads // hp,),
        in_specs=[
            pl.BlockSpec((nr, nc, None, tok, width), lambda h: (0, 0, at, 0, 0)),
            pl.BlockSpec((nc, None, tok, width), lambda h: (0, at, 0, 0)),
            pl.BlockSpec((2, width, width), lambda h: (0, 0, 0)),
            pl.BlockSpec((width, hp * 3 * head_dim), lambda h: (slot, h)),
            pl.BlockSpec((spare, hp * 3 * head_dim), lambda h: (slots * width // spare, h)),
            pl.BlockSpec((1, head_dim), lambda h: (0, 0)),
            pl.BlockSpec((hp * head_dim, depth), lambda h: (h, 0)),
        ],
        out_specs=[out_spec, out_spec],
        out_shape=[
            jax.ShapeDtypeStruct((half, tok, depth), f32),
            jax.ShapeDtypeStruct((half, tok, depth), bf16),
        ],
        scratch_shapes=[
            pltpu.VMEM((nk, 4 * width), bf16),
            pltpu.VMEM((nq, 4 * width), bf16),
            pltpu.VMEM((nq, depth), f32),
        ],
        compiler_params=pltpu.CompilerParams(vmem_limit_bytes=40 * 2**20),
        cost_estimate=pl.CostEstimate(
            flops=2 * heads * (nk * 256 * 256 + 2 * nq * nk * head_dim * 2 + nq * head_dim * depth),
            bytes_accessed=heads * head_dim * depth * 2 + nq * depth * 3,
            transcendentals=heads * nq * nk,
        ),
    )(keys, queries, gram, folded, folded, gain, out_weight)


def heads_per_step(heads):
    return max(k for k in (1, 2, 3) if heads % k == 0)


def exchange(value, axis, bit):
    count = lax.axis_size(axis)
    return lax.ppermute(value, axis, [(i, i ^ bit) for i in range(count)])


def spread(value, axis, bits):
    masks = [0]
    for bit in bits:
        masks += [mask | bit for mask in masks]
    return jnp.stack([value] + [exchange(value, axis, mask) for mask in masks[1:]])


def bits_of(axis):
    return [1 << i for i in range(lax.axis_size(axis).bit_length() - 1)]


def finish_row(keys, shape):
    rest = bits_of("row")[1:]
    while rest:
        keys = spread(keys, "row", rest[:2]).reshape(-1, *shape)
        rest = rest[2:]
    return keys


def fold_inputs(embed_weight, scale, shift):
    centred = embed_weight.astype(f32)
    centred = centred - jnp.mean(centred, axis=1, keepdims=True)
    width, depth = embed_weight.shape
    slots = scale.shape[0]
    scaled = ((1.0 + scale)[:, None, :] * centred[None]).astype(bf16).reshape(slots * width, depth)
    shift_hi = shift.astype(bf16)
    shift_lo = (shift - shift_hi.astype(f32)).astype(bf16)
    spare = -(2 * slots) % 16
    lhs = jnp.concatenate([scaled, shift_hi, shift_lo, jnp.zeros((spare, depth), bf16)], axis=0)
    gram = jnp.einsum("ad,bd->ab", centred, centred, precision=lax.Precision.HIGHEST) / depth
    gram_hi = gram.astype(bf16)
    return lhs, jnp.stack([gram_hi, (gram - gram_hi.astype(f32)).astype(bf16)])


def on_device(
    features,
    conv_first,
    conv_second,
    conv_last,
    noise,
    prior_patches,
    step_index,
    mod_table,
    embed_weight,
    qkv_weight,
    q_gain,
    k_gain,
    out_weight,
):
    tie = lax.optimization_barrier
    tile_rows, tile_cols, _ = features.shape
    slots = step_index.shape[0]
    prior = prior_patches.transpose(1, 0, 2)
    queries = spread(prior, "col", bits_of("col"))
    mid = edges(features)
    left, right = sides(mid)

    step_total = mod_table.shape[0]
    mods = sum(
        jnp.where((step_index == k)[:, None, None], mod_table[k][None], 0.0)
        for k in range(step_total)
    )
    head_dim = q_gain.shape[0]
    lhs, gram = fold_inputs(embed_weight, mods[:, 1, :], mods[:, 0, :])
    gain = (q_gain * k_gain * (math.log2(math.e) / math.sqrt(head_dim)))[None]
    pair = spread(queries, "row", bits_of("row")[:1])
    pair, lhs = tie((pair, lhs))
    keys = finish_row(pair, queries.shape)
    folded = jnp.dot(lhs, qkv_weight, preferred_element_type=f32)

    def attended(slot, keys, queries, at):
        return attend(keys, queries, slot, at, gram, folded, gain, out_weight)

    parts, sums = {}, {}

    def first(slot):
        keep, send = parts[slot]
        total = keep + exchange(send, "col", 1).astype(f32)
        parts[slot] = (total[0::2], total[1::2].astype(bf16))

    def rest(slot):
        keep, send = parts[slot]
        bit = 2
        while True:
            total = keep + exchange(send, "col", bit).astype(f32)
            if total.shape[0] == 1:
                break
            keep, send = total[0::2], total[1::2].astype(bf16)
            bit *= 2
        sums[slot] = total[0]

    parts[1] = attended(1, keys, queries, 0)
    mid, left, right, parts[1] = tie((mid, left, right, parts[1]))
    latent = encode(left, mid, right, tile_rows, conv_first, conv_second, conv_last)
    channels = latent.shape[-1]
    tok = tile_rows // 2 * (tile_cols // 2)
    patch = (
        latent.reshape(tile_cols // 2, 2, tile_rows // 2, 2, channels)
        .transpose(2, 0, 3, 1, 4)
        .reshape(tok, 4 * channels)
    )
    sigma = (step_total - step_index.astype(f32)) / (step_total + 1.0)
    fresh = ((1.0 - sigma[0]) * patch + sigma[0] * noise.astype(f32)).astype(bf16)
    first(1)
    fresh, queries, parts[1] = tie((fresh, queries, parts[1]))
    fresh_queries = spread(fresh[None], "col", bits_of("col"))
    parts[2] = attended(2, keys, queries, 1)
    fresh_pair = spread(fresh_queries, "row", bits_of("row")[:1])
    fresh_pair, queries, parts[2] = tie((fresh_pair, queries, parts[2]))
    fresh_keys = finish_row(fresh_pair, fresh_queries.shape)
    parts[3] = attended(3, keys, queries, 2)
    rest(1)
    first(2)
    sums[1], parts[2], parts[3] = tie((sums[1], parts[2], parts[3]))
    fresh_queries, parts[2], parts[3] = tie((fresh_queries, parts[2], parts[3]))
    parts[0] = attended(0, fresh_keys, fresh_queries, 0)
    rest(2)
    first(3)
    sums[2], parts[3], parts[0] = tie((sums[2], parts[3], parts[0]))
    first(0)
    rest(3)
    rest(0)

    patches = jnp.concatenate([fresh[None], prior], axis=0)
    own = jnp.einsum(
        "stc,cd->std", patches, embed_weight, preferred_element_type=f32
    ).astype(bf16)
    outs = [
        (own[s].astype(f32) + mods[s, 2][None, :] * sums[s]).astype(bf16) for s in range(slots)
    ]
    return jnp.stack(outs, axis=1)


def solution(mesh):
    placed = (
        P("row", "col", None),
        P(),
        P(),
        P(),
        P(("row", "col"), None),
        P(("row", "col"), None, None),
        P(),
        P(),
        P(),
        P(None, "col"),
        P(),
        P(),
        P("col", None),
    )
    return jax.shard_map(
        on_device,
        mesh=mesh,
        in_specs=placed,
        out_specs=P(("row", "col"), None, None),
        check_vma=False,
    )
```

time: 167 us -> 134 us (0.80)
  blocking collectives: 22.9 us -> 0 us
  starting transfers between devices: 25.9 us -> 37.2 us
  local copies, waits for them, and re-layouts: 15.8 us -> 7.81 us
  matrix products: 17.3 us -> 9.41 us
  Pallas kernels: 40.3 us -> 37.1 us
  waiting for transfers between devices: 36.7 us -> 33.9 us
    all_gather x2 -> x0, blocking collectives: 22.9 us -> none  [gather_tokens(): return (queries, lax.all_gather(queries, 'row', axis=0, tiled=False))]
    conv_general_dilated x3 -> x0, matrix products: 14.9 us -> none  [conv_valid(): lax.conv_general_dilated(field[None], kernel, (1, 1), 'VALID', dimension_...]
    ppermute x14 -> x22, starting transfers between devices: 18.9 us -> 29.8 us  [exchange(): return lax.ppermute(value, axis, [(i, i ^ bit) for i in range(count)])]
    unnamed x44 -> x45, local copies, waits for them, and re-layouts: 11.7 us -> 3.5 us
    dot_general x1 -> x2, matrix products: 2.05 us -> 9.06 us  [the longest x1 8.13 us: on_device(): folded = jnp.dot(lhs, qkv_weight, preferred_element_type=f32)]
    pallas_call x5, Pallas kernels: 40.3 us -> 37.1 us  [the longest x4 31.1 us: attend(): pl.pallas_call(functools.partial(attend_kernel, hp, head_dim, slot, slots...]
    ppermute x14 -> x22, waiting for transfers between devices: 36.6 us -> 33.9 us  [exchange(): return lax.ppermute(value, axis, [(i, i ^ bit) for i in range(count)])]
    concatenate x1 -> x2, other arithmetic: 0.08 us -> 1.81 us  [the longest x1 1.68 us: fold_inputs(): jnp.concatenate([scaled, shift_hi, shift_lo, jnp.zeros((spare, depth), bf...]
  transfers between devices with their start and end apart: 18 -> 26, of which waited for: 6 -> 8; matrix products, arithmetic and copies ran while one was open for 16% -> 14% of each run, Pallas kernels for 24% -> 28%
where the time goes in v2:
time: 134 us
  starting transfers between devices  37.2 us (28%)
  Pallas kernels  37.1 us (28%)
  waiting for transfers between devices  33.9 us (25%)
  matrix products  9.41 us (7%)
  local copies, waits for them, and re-layouts  7.81 us (6%)
  other arithmetic  7.75 us (6%)
    ppermute x22, waiting for transfers between devices, exchange(): return lax.ppermute(value, axis, [(i, i ^ bit) for i in range(count)])  33.9 us
    pallas_call x4, Pallas kernels, attend(): pl.pallas_call(functools.partial(attend_kernel, hp, head_dim, slot, slots...  31.1 us
    ppermute x22, starting transfers between devices, exchange(): return lax.ppermute(value, axis, [(i, i ^ bit) for i in range(count)])  29.8 us
    dot_general x1, matrix products, on_device(): folded = jnp.dot(lhs, qkv_weight, preferred_element_type=f32)  8.13 us
    pallas_call x1, Pallas kernels, encode(): pl.pallas_call(encode_kernel, grid=(6,), in_specs=[pl.BlockSpec(memory_sp...  6.02 us
    unnamed x45, local copies, waits for them, and re-layouts  3.5 us
    ppermute x1, starting transfers between devices, sides(): left = lax.ppermute(mid[-3:], 'col', [(i, i + 1) for i in range(nc - 1)])  3.41 us
  transfers between devices with their start and end apart: 26, of which 8 were waited for; matrix products, arithmetic and copies ran while one was open for 14% of the time, Pallas kernels for 28%

profile of v2, /device:TPU:0, one launch (start us, length us, event | category | flops | bytes accessed | tf_op | source)
XLA Modules:
  0.0 134.1 jit_solution(6850072669195803603)
XLA Ops:
  0.0 5.0 %collective-permute-start.6 = (bf16[3,32,64]{2,1,0:T(8,128)(2,1)}, bf16[3,32,64]{2,1,0:T(8,128)(2,1)S(1)}, u32[]{:S(2)}, u32[]{:S(2)}) collective-permute-start(bf16[3,32,64]{2,1,0:T(8,128)(2,1)} %bitcast.146), channel_id=1, source_target_pairs={{0,3},{1,2},{2,1},{3,0},{4,7},{5,6},{6,5},{7,4},{8,11},{9,10},{10,... | collective-permute-start | bytes 36872 | tf_op jit(solution)/shard_map/ppermute | solution.py:296
  6.7 1.3 collective-permute-start.1
  8.0 1.3 collective-permute-start
  9.4 1.4 %fusion.20 = (f32[1,3,3072]{2,0,1:T(1,128)S(1)}, f32[1,3,3072]{2,0,1:T(1,128)S(1)}, f32[1,3,3072]{2,0,1:T(1,128)S(1)}, f32[1,3,3072]{2,0,1:T(1,128)S(1)}) fusion(f32[4,3,3072]{2,0,1:T(4,128)} %param.20), kind=kLoop, calls=%fused_computation.77 | loop fusion | bytes 294912 | tf_op jit(solution)/shard_map/slice | solution.py:358
  11.8 1.1 convert_reduce_fusion
  12.9 1.1 convert_subtract_fusion
  15.5 1.7 %maximum_maximum_fusion = bf16[272,3072]{1,0:T(8,128)(2,1)} fusion(bf16[4,3072]{1,0:T(4,128)(2,1)S(1)} %fusion.10, bf16[4,3072]{1,0:T(4,128)(2,1)S(1)} %bitcast.144, bf16[256,3072]{1,0:T(8,128)(2,1)S(1)} %bitcast.131, bf16[272]{0:T(512)(128)(2,1)S(1)} %pad.25.clone), kind=kLoop, calls=%fused_computation.2 | loop fusion | flops 6684672 | bytes 3293728 | tf_op jit(solution)/shard_map/concatenate | solution.py:327
  17.4 3.1 %collective-permute-start.7 = (bf16[4,3,32,64]{3,2,1,0:T(8,128)(2,1)S(1)}, bf16[4,3,32,64]{3,2,1,0:T(8,128)(2,1)S(1)}, u32[]{:S(2)}, u32[]{:S(2)}) collective-permute-start(bf16[4,3,32,64]{3,2,1,0:T(8,128)(2,1)S(1)} %get-tuple-element.60.query_ref), channel_id=1, source_target_pairs={{0,4},{4,0},{8,12},{12,8},{16,20},{20,16},{24,28},{28,24},{1,5},{5... | collective-permute-start | bytes 147464 | tf_op jit(solution)/shard_map/ppermute | solution.py:296
  20.7 3.4 %collective-permute-start.2 = (bf16[3,16,512]{2,1,0:T(8,128)(2,1)S(1)}, bf16[3,16,512]{2,1,0:T(8,128)(2,1)S(1)}, u32[]{:S(2)}, u32[]{:S(2)}) collective-permute-start(bf16[3,16,512]{2,1,0:T(8,128)(2,1)S(1)} %get-tuple-element.86), channel_id=1, source_target_pairs={{0,1},{1,2},{2,3},{4,5},{5,6},{6,7},{8,9},{9,10},{10,11},{12,13},{... | collective-permute-start | bytes 147464 | tf_op jit(solution)/shard_map/ppermute | solution.py:113
  24.1 1.5 %collective-permute-start.3 = (bf16[3,16,512]{2,1,0:T(8,128)(2,1)S(1)}, bf16[3,16,512]{2,1,0:T(8,128)(2,1)S(1)}, u32[]{:S(2)}, u32[]{:S(2)}) collective-permute-start(bf16[3,16,512]{2,1,0:T(8,128)(2,1)S(1)} %get-tuple-element.85), channel_id=1, source_target_pairs={{1,0},{2,1},{3,2},{5,4},{6,5},{7,6},{9,8},{10,9},{11,10},{13,12},{... | collective-permute-start | bytes 147464 | tf_op jit(solution)/shard_map/ppermute | solution.py:114
  25.7 2.7 %collective-permute-start.10 = (bf16[2,4,3,32,64]{4,3,2,1,0:T(8,128)(2,1)S(1)}, bf16[2,4,3,32,64]{4,3,2,1,0:T(8,128)(2,1)S(1)}, u32[]{:S(2)}, u32[]{:S(2)}) collective-permute-start(bf16[2,4,3,32,64]{4,3,2,1,0:T(8,128)(2,1)S(1)} %pad_maximum_fusion.4), channel_id=1, source_target_pairs={{0,24},{4,28},{8,16},{12,20},{16,8},{20,12},{24,0},{28,4},{1,25},{... | collective-permute-start | bytes 294920 | tf_op jit(solution)/shard_map/ppermute | solution.py:296
  29.8 8.1 %fusion.22.m_ref.bias_ref = f32[272,2304]{1,0:T(8,128)S(1)} fusion(bf16[272,3072]{1,0:T(8,128)(2,1)} %maximum_maximum_fusion, bf16[3072,2304]{1,0:T(8,128)(2,1)} %param.22), kind=kOutput, calls=%fused_computation.79 | convolution fusion | flops 3850371072 | bytes 18333696 | tf_op jit(solution)/shard_map/dot_general | solution.py:367
  39.3 8.4 %shard_map.127 = (f32[2,32,3072]{2,1,0:T(8,128)S(1)}, bf16[2,32,3072]{2,1,0:T(8,128)(2,1)}) custom-call(bf16[8,4,3,32,64]{4,3,2,1,0:T(8,128)(2,1)S(1)} %bitcast.126, bf16[4,3,32,64]{3,2,1,0:T(8,128)(2,1)S(1)} %get-tuple-element.60.query_ref, bf16[2,64,64]{2,1,0:T(8,128)(2,1)S(1)} %pad_maximum_fusion.7.gram_ref, f32[272,2304]{1,0:T(8,128)S(1)} %fusion.22.m_ref.bias_ref, ...), custom_call_target="tpu_custom_call" | custom-call | flops 2214592512 | bytes 5898240 | tf_op jit(solution)/shard_map/pallas_call | solution.py:259
  47.7 2.4 %collective-permute-start.11 = (bf16[2,32,3072]{2,1,0:T(8,128)(2,1)}, bf16[2,32,3072]{2,1,0:T(8,128)(2,1)}, u32[]{:S(2)}, u32[]{:S(2)}) collective-permute-start(bf16[2,32,3072]{2,1,0:T(8,128)(2,1)} %get-tuple-element.51), channel_id=1, source_target_pairs={{0,1},{1,0},{2,3},{3,2},{4,5},{5,4},{6,7},{7,6},{8,9},{9,8},{10,11... | collective-permute-start | bytes 1179656 | tf_op jit(solution)/shard_map/ppermute | solution.py:296
  50.2 6.0 %shard_map.128 = f32[16,8,16]{2,1,0:T(8,128)S(1)} custom-call(s32[4]{0:T(128)S(1)} %pad_add_fusion.place_ref, bf16[3,16,512]{2,1,0:T(8,128)(2,1)S(1)} %collective-permute-done.2.left_ref, bf16[16,16,512]{2,1,0:T(8,128)(2,1)S(1)} %pad_maximum_fusion.2.mid_ref, bf16[3,16,512]{2,1,0:T(8,128)(2,1)S(1)} %collective-permute-done.3.right_ref, ...), custom_call_target="tpu_custom_call" | custom-call | flops 3373793280 | bytes 10616832 | tf_op jit(solution)/shard_map/pallas_call | solution.py:137
  56.4 2.4 %collective-permute-done.11 = bf16[2,32,3072]{2,1,0:T(8,128)(2,1)} collective-permute-done((bf16[2,32,3072]{2,1,0:T(8,128)(2,1)}, bf16[2,32,3072]{2,1,0:T(8,128)(2,1)}, u32[]{:S(2)}, u32[]{:S(2)}) %collective-permute-start.11) | collective-permute-done | bytes 393248 | tf_op jit(solution)/shard_map/ppermute | solution.py:296
  58.8 1.3 convert_add_fusion.3
  60.2 4.2 %collective-permute-start.14 = (bf16[1,32,64]{2,1,0:T(8,128)(2,1)S(1)}, bf16[1,32,64]{2,1,0:T(8,128)(2,1)S(1)}, u32[]{:S(2)}, u32[]{:S(2)}) collective-permute-start(bf16[1,32,64]{2,1,0:T(8,128)(2,1)S(1)} %bitcast.151), channel_id=1, source_target_pairs={{0,3},{1,2},{2,1},{3,0},{4,7},{5,6},{6,5},{7,4},{8,11},{9,10},{10,... | collective-permute-start | bytes 12296 | tf_op jit(solution)/shard_map/ppermute | solution.py:296
  65.0 2.3 %collective-permute-start.15 = (bf16[1,32,3072]{2,1,0:T(8,128)(2,1)S(1)}, bf16[1,32,3072]{2,1,0:T(8,128)(2,1)S(1)}, u32[]{:S(2)}, u32[]{:S(2)}) collective-permute-start(bf16[1,32,3072]{2,1,0:T(8,128)(2,1)S(1)} %slice.172), channel_id=1, source_target_pairs={{0,2},{1,3},{2,0},{3,1},{4,6},{5,7},{6,4},{7,5},{8,10},{9,11},{10,... | collective-permute-start | bytes 589832 | tf_op jit(solution)/shard_map/ppermute | solution.py:296
  67.3 2.3 %collective-permute-done.13 = bf16[1,32,64]{2,1,0:T(8,128)(2,1)S(1)} collective-permute-done((bf16[1,32,64]{2,1,0:T(8,128)(2,1)S(1)}, bf16[1,32,64]{2,1,0:T(8,128)(2,1)S(1)}, u32[]{:S(2)}, u32[]{:S(2)}) %collective-permute-start.13) | collective-permute-done | bytes 4128 | tf_op jit(solution)/shard_map/ppermute | solution.py:296
  69.7 2.3 %copy-done = bf16[768,3072]{1,0:T(8,128)(2,1)S(1)} copy-done((bf16[768,3072]{1,0:T(8,128)(2,1)S(1)}, bf16[768,3072]{1,0:T(8,128)(2,1)}, u32[]{:S(2)}) %copy-start) | copy-done | bytes 4718616
  72.0 7.6 %shard_map.129 = (f32[2,32,3072]{2,1,0:T(8,128)S(1)}, bf16[2,32,3072]{2,1,0:T(8,128)(2,1)S(1)}) custom-call(bf16[8,4,3,32,64]{4,3,2,1,0:T(8,128)(2,1)S(1)} %bitcast.127, bf16[4,3,32,64]{3,2,1,0:T(8,128)(2,1)S(1)} %get-tuple-element.60.query_ref, bf16[2,64,64]{2,1,0:T(8,128)(2,1)S(1)} %pad_maximum_fusion.7.gram_ref, f32[272,2304]{1,0:T(8,128)S(1)} %fusion.22.m_ref.bias_ref, ...), custom_call_target="tpu_custom_call" | custom-call | flops 2214592512 | bytes 5898240 | tf_op jit(solution)/shard_map/pallas_call | solution.py:259
  79.7 3.1 %collective-permute-start.22 = (bf16[2,4,1,32,64]{4,3,1,2,0:T(8,128)(2,1)S(1)}, bf16[2,4,1,32,64]{4,3,1,2,0:T(8,128)(2,1)S(1)}, u32[]{:S(2)}, u32[]{:S(2)}) collective-permute-start(bf16[2,4,1,32,64]{4,3,1,2,0:T(8,128)(2,1)S(1)} %pad_maximum_fusion.6), channel_id=1, source_target_pairs={{0,24},{4,28},{8,16},{12,20},{16,8},{20,12},{24,0},{28,4},{1,25},{... | collective-permute-start | bytes 98312 | tf_op jit(solution)/shard_map/ppermute | solution.py:296
  83.5 7.6 %shard_map.130 = (f32[2,32,3072]{2,1,0:T(8,128)S(1)}, bf16[2,32,3072]{2,1,0:T(8,128)(2,1)S(1)}) custom-call(bf16[8,4,3,32,64]{4,3,2,1,0:T(8,128)(2,1)S(1)} %bitcast.128, bf16[4,3,32,64]{3,2,1,0:T(8,128)(2,1)S(1)} %get-tuple-element.60.query_ref, bf16[2,64,64]{2,1,0:T(8,128)(2,1)S(1)} %pad_maximum_fusion.7.gram_ref, f32[272,2304]{1,0:T(8,128)S(1)} %fusion.22.m_ref.bias_ref, ...), custom_call_target="tpu_custom_call" | custom-call | flops 2214592512 | bytes 5898240 | tf_op jit(solution)/shard_map/pallas_call | solution.py:259
  91.3 3.2 %collective-permute-done.17 = bf16[2,32,3072]{2,1,0:T(8,128)(2,1)S(1)} collective-permute-done((bf16[2,32,3072]{2,1,0:T(8,128)(2,1)S(1)}, bf16[2,32,3072]{2,1,0:T(8,128)(2,1)S(1)}, u32[]{:S(2)}, u32[]{:S(2)}) %collective-permute-start.17) | collective-permute-done | bytes 393248 | tf_op jit(solution)/shard_map/ppermute | solution.py:296
  95.8 7.6 %shard_map.131 = (f32[2,32,3072]{2,1,0:T(8,128)S(1)}, bf16[2,32,3072]{2,1,0:T(8,128)(2,1)S(1)}) custom-call(bf16[8,4,1,32,64]{4,3,2,1,0:T(8,128)(2,1)S(1)} %bitcast.129, bf16[4,1,32,64]{3,2,1,0:T(8,128)(2,1)S(1)} %get-tuple-element.72.query_ref, bf16[2,64,64]{2,1,0:T(8,128)(2,1)S(1)} %pad_maximum_fusion.7.gram_ref, f32[272,2304]{1,0:T(8,128)S(1)} %fusion.22.m_ref.bias_ref, ...), custom_call_target="tpu_custom_call" | custom-call | flops 2214592512 | bytes 5898240 | tf_op jit(solution)/shard_map/pallas_call | solution.py:259
  103.3 2.4 %collective-permute-done.18 = bf16[1,32,3072]{2,1,0:T(8,128)(2,1)S(1)} collective-permute-done((bf16[1,32,3072]{2,1,0:T(8,128)(2,1)S(1)}, bf16[1,32,3072]{2,1,0:T(8,128)(2,1)S(1)}, u32[]{:S(2)}, u32[]{:S(2)}) %collective-permute-start.18) | collective-permute-done | bytes 196640 | tf_op jit(solution)/shard_map/ppermute | solution.py:296
  105.8 3.4 %collective-permute-done.19 = bf16[2,32,3072]{2,1,0:T(8,128)(2,1)S(1)} collective-permute-done((bf16[2,32,3072]{2,1,0:T(8,128)(2,1)S(1)}, bf16[2,32,3072]{2,1,0:T(8,128)(2,1)S(1)}, u32[]{:S(2)}, u32[]{:S(2)}) %collective-permute-start.19) | collective-permute-done | bytes 393248 | tf_op jit(solution)/shard_map/ppermute | solution.py:296
  111.0 1.8 %collective-permute-start.25 = (bf16[1,32,3072]{2,1,0:T(8,128)(2,1)S(1)}, bf16[1,32,3072]{2,1,0:T(8,128)(2,1)S(1)}, u32[]{:S(2)}, u32[]{:S(2)}) collective-permute-start(bf16[1,32,3072]{2,1,0:T(8,128)(2,1)S(1)} %slice.170), channel_id=1, source_target_pairs={{0,2},{1,3},{2,0},{3,1},{4,6},{5,7},{6,4},{7,5},{8,10},{9,11},{10,... | collective-permute-start | bytes 589832 | tf_op jit(solution)/shard_map/ppermute | solution.py:296
  112.8 9.5 %collective-permute-done.23 = bf16[2,32,3072]{2,1,0:T(8,128)(2,1)S(1)} collective-permute-done((bf16[2,32,3072]{2,1,0:T(8,128)(2,1)S(1)}, bf16[2,32,3072]{2,1,0:T(8,128)(2,1)S(1)}, u32[]{:S(2)}, u32[]{:S(2)}) %collective-permute-start.23) | collective-permute-done | bytes 393248 | tf_op jit(solution)/shard_map/ppermute | solution.py:296
  122.7 9.6 %collective-permute-done.24 = bf16[1,32,3072]{2,1,0:T(8,128)(2,1)S(1)} collective-permute-done((bf16[1,32,3072]{2,1,0:T(8,128)(2,1)S(1)}, bf16[1,32,3072]{2,1,0:T(8,128)(2,1)S(1)}, u32[]{:S(2)}, u32[]{:S(2)}) %collective-permute-start.24) | collective-permute-done | bytes 196640 | tf_op jit(solution)/shard_map/ppermute | solution.py:296
  132.6 1.5 %copy.25 = bf16[32,4,3072]{2,1,0:T(4,128)(2,1)} copy(bf16[32,4,3072]{2,0,1:T(8,128)(2,1)S(1)} %pad_maximum_fusion.1) | data formatting | bytes 1572864 | tf_op jit(solution)/shard_map/stack | solution.py:429
  (128 shorter events, 12.7 us)
Async XLA Ops:
  0.0 15.0 %copy-start.9 = (s32[4]{0:T(128)S(1)}, s32[4]{0:T(128)}, u32[]{:S(2)}) copy-start(s32[4]{0:T(128)} %param.19) | copy-start | bytes 52
  0.0 14.1 %copy-start.3 = (bf16[64,3072]{1,0:T(8,128)(2,1)S(1)}, bf16[64,3072]{1,0:T(8,128)(2,1)}, u32[]{:S(2)}) copy-start(bf16[64,3072]{1,0:T(8,128)(2,1)} %param.21) | copy-start | bytes 1179652
  0.0 17.4 %collective-permute-start.6 = (bf16[3,32,64]{2,1,0:T(8,128)(2,1)}, bf16[3,32,64]{2,1,0:T(8,128)(2,1)S(1)}, u32[]{:S(2)}, u32[]{:S(2)}) collective-permute-start(bf16[3,32,64]{2,1,0:T(8,128)(2,1)} %bitcast.146), channel_id=1, source_target_pairs={{0,3},{1,2},{2,1},{3,0},{4,7},{5,6},{6,5},{7,4},{8,11},{9,10},{10,... | collective-permute-start | bytes 36872 | tf_op jit(solution)/shard_map/ppermute | solution.py:296
  5.1 12.3 %collective-permute-start.5 = (bf16[3,32,64]{2,1,0:T(8,128)(2,1)}, bf16[3,32,64]{2,1,0:T(8,128)(2,1)S(1)}, u32[]{:S(2)}, u32[]{:S(2)}) collective-permute-start(bf16[3,32,64]{2,1,0:T(8,128)(2,1)} %bitcast.147), channel_id=1, source_target_pairs={{0,2},{1,3},{2,0},{3,1},{4,6},{5,7},{6,4},{7,5},{8,10},{9,11},{10,... | collective-permute-start | bytes 36872 | tf_op jit(solution)/shard_map/ppermute | solution.py:296
  5.1 12.3 %collective-permute-start.4 = (bf16[3,32,64]{2,1,0:T(8,128)(2,1)}, bf16[3,32,64]{2,1,0:T(8,128)(2,1)S(1)}, u32[]{:S(2)}, u32[]{:S(2)}) collective-permute-start(bf16[3,32,64]{2,1,0:T(8,128)(2,1)} %bitcast.148), channel_id=1, source_target_pairs={{0,1},{1,0},{2,3},{3,2},{4,5},{5,4},{6,7},{7,6},{8,9},{9,8},{10,11... | collective-permute-start | bytes 36872 | tf_op jit(solution)/shard_map/ppermute | solution.py:296
  6.7 13.8 %collective-permute-start.1 = (bf16[16,3,512]{2,1,0:T(4,128)(2,1)S(1)}, bf16[16,3,512]{2,1,0:T(4,128)(2,1)S(1)}, u32[]{:S(2)}, u32[]{:S(2)}) collective-permute-start(bf16[16,3,512]{2,1,0:T(4,128)(2,1)S(1)} %get-tuple-element.98), channel_id=1, source_target_pairs={{0,4},{4,8},{8,12},{12,16},{16,20},{20,24},{24,28},{1,5},{5,9},{9,... | collective-permute-start | bytes 147464 | tf_op jit(solution)/shard_map/ppermute | solution.py:104
  8.0 12.5 %collective-permute-start = (bf16[16,3,512]{2,1,0:T(4,128)(2,1)S(1)}, bf16[16,3,512]{2,1,0:T(4,128)(2,1)S(1)}, u32[]{:S(2)}, u32[]{:S(2)}) collective-permute-start(bf16[16,3,512]{2,1,0:T(4,128)(2,1)S(1)} %get-tuple-element.97), channel_id=1, source_target_pairs={{4,0},{8,4},{12,8},{16,12},{20,16},{24,20},{28,24},{5,1},{9,5},{13... | collective-permute-start | bytes 147464 | tf_op jit(solution)/shard_map/ppermute | solution.py:105
  17.4 8.1 %collective-permute-start.7 = (bf16[4,3,32,64]{3,2,1,0:T(8,128)(2,1)S(1)}, bf16[4,3,32,64]{3,2,1,0:T(8,128)(2,1)S(1)}, u32[]{:S(2)}, u32[]{:S(2)}) collective-permute-start(bf16[4,3,32,64]{3,2,1,0:T(8,128)(2,1)S(1)} %get-tuple-element.60.query_ref), channel_id=1, source_target_pairs={{0,4},{4,0},{8,12},{12,8},{16,20},{20,16},{24,28},{28,24},{1,5},{5... | collective-permute-start | bytes 147464 | tf_op jit(solution)/shard_map/ppermute | solution.py:296
  20.6 29.5 %slice-start.6 = ((s8[4718592]{0:T(1024)(128)(4,1)}), s8[4194304]{0:T(1024)(128)(4,1)S(1)}, s32[]{:S(2)}) async-start(s8[4718592]{0:T(1024)(128)(4,1)} %bitcast.124), calls=%async_computation.6 | async-start | bytes 8388608
  20.7 27.0 %collective-permute-start.2 = (bf16[3,16,512]{2,1,0:T(8,128)(2,1)S(1)}, bf16[3,16,512]{2,1,0:T(8,128)(2,1)S(1)}, u32[]{:S(2)}, u32[]{:S(2)}) collective-permute-start(bf16[3,16,512]{2,1,0:T(8,128)(2,1)S(1)} %get-tuple-element.86), channel_id=1, source_target_pairs={{0,1},{1,2},{2,3},{4,5},{5,6},{6,7},{8,9},{9,10},{10,11},{12,13},{... | collective-permute-start | bytes 147464 | tf_op jit(solution)/shard_map/ppermute | solution.py:113
  24.1 23.6 %collective-permute-start.3 = (bf16[3,16,512]{2,1,0:T(8,128)(2,1)S(1)}, bf16[3,16,512]{2,1,0:T(8,128)(2,1)S(1)}, u32[]{:S(2)}, u32[]{:S(2)}) collective-permute-start(bf16[3,16,512]{2,1,0:T(8,128)(2,1)S(1)} %get-tuple-element.85), channel_id=1, source_target_pairs={{1,0},{2,1},{3,2},{5,4},{6,5},{7,6},{9,8},{10,9},{11,10},{13,12},{... | collective-permute-start | bytes 147464 | tf_op jit(solution)/shard_map/ppermute | solution.py:114
  25.6 13.7 %slice-start = ((s8[4718592]{0:T(1024)(128)(4,1)}), s8[4194304]{0:T(1024)(128)(4,1)S(1)}, s32[]{:S(2)}) async-start(s8[4718592]{0:T(1024)(128)(4,1)} %bitcast.118), calls=%async_computation | async-start | bytes 8388608
  25.7 24.4 %slice-start.7 = ((s8[4718592]{0:T(1024)(128)(4,1)}), s8[524288]{0:T(1024)(128)(4,1)S(1)}, s32[]{:S(2)}) async-start(s8[4718592]{0:T(1024)(128)(4,1)} %bitcast.124), calls=%async_computation.7 | async-start | bytes 1048576
  25.7 12.2 %collective-permute-start.10 = (bf16[2,4,3,32,64]{4,3,2,1,0:T(8,128)(2,1)S(1)}, bf16[2,4,3,32,64]{4,3,2,1,0:T(8,128)(2,1)S(1)}, u32[]{:S(2)}, u32[]{:S(2)}) collective-permute-start(bf16[2,4,3,32,64]{4,3,2,1,0:T(8,128)(2,1)S(1)} %pad_maximum_fusion.4), channel_id=1, source_target_pairs={{0,24},{4,28},{8,16},{12,20},{16,8},{20,12},{24,0},{28,4},{1,25},{... | collective-permute-start | bytes 294920 | tf_op jit(solution)/shard_map/ppermute | solution.py:296
  28.4 9.6 %collective-permute-start.9 = (bf16[2,4,3,32,64]{4,3,2,1,0:T(8,128)(2,1)S(1)}, bf16[2,4,3,32,64]{4,3,2,1,0:T(8,128)(2,1)S(1)}, u32[]{:S(2)}, u32[]{:S(2)}) collective-permute-start(bf16[2,4,3,32,64]{4,3,2,1,0:T(8,128)(2,1)S(1)} %pad_maximum_fusion.4), channel_id=1, source_target_pairs={{0,16},{4,20},{8,24},{12,28},{16,0},{20,4},{24,8},{28,12},{1,17},{... | collective-permute-start | bytes 294920 | tf_op jit(solution)/shard_map/ppermute | solution.py:296
  28.9 10.2 %collective-permute-start.8 = (bf16[2,4,3,32,64]{4,3,2,1,0:T(8,128)(2,1)S(1)}, bf16[2,4,3,32,64]{4,3,2,1,0:T(8,128)(2,1)S(1)}, u32[]{:S(2)}, u32[]{:S(2)}) collective-permute-start(bf16[2,4,3,32,64]{4,3,2,1,0:T(8,128)(2,1)S(1)} %pad_maximum_fusion.4), channel_id=1, source_target_pairs={{0,8},{4,12},{8,0},{12,4},{16,24},{20,28},{24,16},{28,20},{1,9},{5... | collective-permute-start | bytes 294920 | tf_op jit(solution)/shard_map/ppermute | solution.py:296
  47.7 11.1 %collective-permute-start.11 = (bf16[2,32,3072]{2,1,0:T(8,128)(2,1)}, bf16[2,32,3072]{2,1,0:T(8,128)(2,1)}, u32[]{:S(2)}, u32[]{:S(2)}) collective-permute-start(bf16[2,32,3072]{2,1,0:T(8,128)(2,1)} %get-tuple-element.51), channel_id=1, source_target_pairs={{0,1},{1,0},{2,3},{3,2},{4,5},{5,4},{6,7},{7,6},{8,9},{9,8},{10,11... | collective-permute-start | bytes 1179656 | tf_op jit(solution)/shard_map/ppermute | solution.py:296
  60.1 19.5 %copy-start.5 = (f32[2,32,3072]{2,1,0:T(8,128)}, f32[2,32,3072]{2,1,0:T(8,128)S(1)}, u32[]{:S(2)}) copy-start(f32[2,32,3072]{2,1,0:T(8,128)S(1)} %convert_add_fusion.3) | copy-start | bytes 2359300
  60.2 7.1 %collective-permute-start.14 = (bf16[1,32,64]{2,1,0:T(8,128)(2,1)S(1)}, bf16[1,32,64]{2,1,0:T(8,128)(2,1)S(1)}, u32[]{:S(2)}, u32[]{:S(2)}) collective-permute-start(bf16[1,32,64]{2,1,0:T(8,128)(2,1)S(1)} %bitcast.151), channel_id=1, source_target_pairs={{0,3},{1,2},{2,1},{3,0},{4,7},{5,6},{6,5},{7,4},{8,11},{9,10},{10,... | collective-permute-start | bytes 12296 | tf_op jit(solution)/shard_map/ppermute | solution.py:296
  64.3 5.2 %collective-permute-start.13 = (bf16[1,32,64]{2,1,0:T(8,128)(2,1)S(1)}, bf16[1,32,64]{2,1,0:T(8,128)(2,1)S(1)}, u32[]{:S(2)}, u32[]{:S(2)}) collective-permute-start(bf16[1,32,64]{2,1,0:T(8,128)(2,1)S(1)} %bitcast.152), channel_id=1, source_target_pairs={{0,2},{1,3},{2,0},{3,1},{4,6},{5,7},{6,4},{7,5},{8,10},{9,11},{10,... | collective-permute-start | bytes 12296 | tf_op jit(solution)/shard_map/ppermute | solution.py:296
  64.3 5.2 %collective-permute-start.12 = (bf16[1,32,64]{2,1,0:T(8,128)(2,1)S(1)}, bf16[1,32,64]{2,1,0:T(8,128)(2,1)S(1)}, u32[]{:S(2)}, u32[]{:S(2)}) collective-permute-start(bf16[1,32,64]{2,1,0:T(8,128)(2,1)S(1)} %bitcast.153), channel_id=1, source_target_pairs={{0,1},{1,0},{2,3},{3,2},{4,5},{5,4},{6,7},{7,6},{8,9},{9,8},{10,11... | collective-permute-start | bytes 12296 | tf_op jit(solution)/shard_map/ppermute | solution.py:296
  65.0 26.2 %collective-permute-start.15 = (bf16[1,32,3072]{2,1,0:T(8,128)(2,1)S(1)}, bf16[1,32,3072]{2,1,0:T(8,128)(2,1)S(1)}, u32[]{:S(2)}, u32[]{:S(2)}) collective-permute-start(bf16[1,32,3072]{2,1,0:T(8,128)(2,1)S(1)} %slice.172), channel_id=1, source_target_pairs={{0,2},{1,3},{2,0},{3,1},{4,6},{5,7},{6,4},{7,5},{8,10},{9,11},{10,... | collective-permute-start | bytes 589832 | tf_op jit(solution)/shard_map/ppermute | solution.py:296
  69.6 10.0 %collective-permute-start.16 = (bf16[4,1,32,64]{3,2,1,0:T(8,128)(2,1)S(1)}, bf16[4,1,32,64]{3,2,1,0:T(8,128)(2,1)S(1)}, u32[]{:S(2)}, u32[]{:S(2)}) collective-permute-start(bf16[4,1,32,64]{3,2,1,0:T(8,128)(2,1)S(1)} %get-tuple-element.72.query_ref), channel_id=1, source_target_pairs={{0,4},{4,0},{8,12},{12,8},{16,20},{20,16},{24,28},{28,24},{1,5},{5... | collective-permute-start | bytes 49160 | tf_op jit(solution)/shard_map/ppermute | solution.py:296
  79.7 11.4 %collective-permute-start.22 = (bf16[2,4,1,32,64]{4,3,1,2,0:T(8,128)(2,1)S(1)}, bf16[2,4,1,32,64]{4,3,1,2,0:T(8,128)(2,1)S(1)}, u32[]{:S(2)}, u32[]{:S(2)}) collective-permute-start(bf16[2,4,1,32,64]{4,3,1,2,0:T(8,128)(2,1)S(1)} %pad_maximum_fusion.6), channel_id=1, source_target_pairs={{0,24},{4,28},{8,16},{12,20},{16,8},{20,12},{24,0},{28,4},{1,25},{... | collective-permute-start | bytes 98312 | tf_op jit(solution)/shard_map/ppermute | solution.py:296
  82.8 8.3 %collective-permute-start.21 = (bf16[2,4,1,32,64]{4,3,1,0,2:T(8,128)(2,1)S(1)}, bf16[2,4,1,32,64]{4,3,1,0,2:T(8,128)(2,1)S(1)}, u32[]{:S(2)}, u32[]{:S(2)}) collective-permute-start(bf16[2,4,1,32,64]{4,3,1,0,2:T(8,128)(2,1)S(1)} %bitcast.137), channel_id=1, source_target_pairs={{0,16},{4,20},{8,24},{12,28},{16,0},{20,4},{24,8},{28,12},{1,17},{... | collective-permute-start | bytes 98312 | tf_op jit(solution)/shard_map/ppermute | solution.py:296
  83.2 7.9 %collective-permute-start.20 = (bf16[2,4,1,32,64]{4,3,1,0,2:T(8,128)(2,1)S(1)}, bf16[2,4,1,32,64]{4,3,1,0,2:T(8,128)(2,1)S(1)}, u32[]{:S(2)}, u32[]{:S(2)}) collective-permute-start(bf16[2,4,1,32,64]{4,3,1,0,2:T(8,128)(2,1)S(1)} %bitcast.138), channel_id=1, source_target_pairs={{0,8},{4,12},{8,0},{12,4},{16,24},{20,28},{24,16},{28,20},{1,9},{5... | collective-permute-start | bytes 98312 | tf_op jit(solution)/shard_map/ppermute | solution.py:296
  83.5 11.0 %collective-permute-start.17 = (bf16[2,32,3072]{2,1,0:T(8,128)(2,1)S(1)}, bf16[2,32,3072]{2,1,0:T(8,128)(2,1)S(1)}, u32[]{:S(2)}, u32[]{:S(2)}) collective-permute-start(bf16[2,32,3072]{2,1,0:T(8,128)(2,1)S(1)} %get-tuple-element.59), channel_id=1, source_target_pairs={{0,1},{1,0},{2,3},{3,2},{4,5},{5,4},{6,7},{7,6},{8,9},{9,8},{10,11... | collective-permute-start | bytes 1179656 | tf_op jit(solution)/shard_map/ppermute | solution.py:296
  94.6 11.2 %collective-permute-start.18 = (bf16[1,32,3072]{2,1,0:T(8,128)(2,1)S(1)}, bf16[1,32,3072]{2,1,0:T(8,128)(2,1)S(1)}, u32[]{:S(2)}, u32[]{:S(2)}) collective-permute-start(bf16[1,32,3072]{2,1,0:T(8,128)(2,1)S(1)} %slice.171), channel_id=1, source_target_pairs={{0,2},{1,3},{2,0},{3,1},{4,6},{5,7},{6,4},{7,5},{8,10},{9,11},{10,... | collective-permute-start | bytes 589832 | tf_op jit(solution)/shard_map/ppermute | solution.py:296
  95.5 13.7 %collective-permute-start.19 = (bf16[2,32,3072]{2,1,0:T(8,128)(2,1)S(1)}, bf16[2,32,3072]{2,1,0:T(8,128)(2,1)S(1)}, u32[]{:S(2)}, u32[]{:S(2)}) collective-permute-start(bf16[2,32,3072]{2,1,0:T(8,128)(2,1)S(1)} %get-tuple-element.70), channel_id=1, source_target_pairs={{0,1},{1,0},{2,3},{3,2},{4,5},{5,4},{6,7},{7,6},{8,9},{9,8},{10,11... | collective-permute-start | bytes 1179656 | tf_op jit(solution)/shard_map/ppermute | solution.py:296
  109.3 13.0 %collective-permute-start.23 = (bf16[2,32,3072]{2,1,0:T(8,128)(2,1)S(1)}, bf16[2,32,3072]{2,1,0:T(8,128)(2,1)S(1)}, u32[]{:S(2)}, u32[]{:S(2)}) collective-permute-start(bf16[2,32,3072]{2,1,0:T(8,128)(2,1)S(1)} %get-tuple-element.76), channel_id=1, source_target_pairs={{0,1},{1,0},{2,3},{3,2},{4,5},{5,4},{6,7},{7,6},{8,9},{9,8},{10,11... | collective-permute-start | bytes 1179656 | tf_op jit(solution)/shard_map/ppermute | solution.py:296
  111.0 11.7 %collective-permute-start.25 = (bf16[1,32,3072]{2,1,0:T(8,128)(2,1)S(1)}, bf16[1,32,3072]{2,1,0:T(8,128)(2,1)S(1)}, u32[]{:S(2)}, u32[]{:S(2)}) collective-permute-start(bf16[1,32,3072]{2,1,0:T(8,128)(2,1)S(1)} %slice.170), channel_id=1, source_target_pairs={{0,2},{1,3},{2,0},{3,1},{4,6},{5,7},{6,4},{7,5},{8,10},{9,11},{10,... | collective-permute-start | bytes 589832 | tf_op jit(solution)/shard_map/ppermute | solution.py:296
  122.4 9.9 %collective-permute-start.24 = (bf16[1,32,3072]{2,1,0:T(8,128)(2,1)S(1)}, bf16[1,32,3072]{2,1,0:T(8,128)(2,1)S(1)}, u32[]{:S(2)}, u32[]{:S(2)}) collective-permute-start(bf16[1,32,3072]{2,1,0:T(8,128)(2,1)S(1)} %slice.169), channel_id=1, source_target_pairs={{0,2},{1,3},{2,0},{3,1},{4,6},{5,7},{6,4},{7,5},{8,10},{9,11},{10,... | collective-permute-start | bytes 589832 | tf_op jit(solution)/shard_map/ppermute | solution.py:296
  (15 other events, 122.8 us)

commit v3 on v2

--- a/solution.py
+++ b/solution.py
@@ -163,7 +163,7 @@
             pltpu.VMEM((3, wide, rows, channels), bf16),
             pltpu.VMEM((wide - 2, rows, channels), f32),
         ],
-        compiler_params=pltpu.CompilerParams(vmem_limit_bytes=40 * 2**20),
+        compiler_params=pltpu.CompilerParams(vmem_limit_bytes=20 * 2**20),
         cost_estimate=pl.CostEstimate(
             flops=2 * 9 * wide * rows * channels * (2 * hidden + latents),
             bytes_accessed=9 * channels * 2 * (2 * hidden + 128),
@@ -186,15 +186,36 @@
 
 
 def attend_kernel(
-    hp, head_dim, slot, slots, key_ref, query_ref, gram_ref, m_ref, bias_ref, gain_ref,
-    wo_ref, keep_ref, send_ref, kaug_ref, qaug_ref, acc_ref,
+    hp, head_dim, slot, slots, groups, *refs
+):
+    key_refs = refs[:groups]
+    attend_body(hp, head_dim, slot, slots, key_refs, *refs[groups:])
+
+
+def attend_body(
+    hp, head_dim, slot, slots, key_refs, query_ref, gram_ref, m_ref, bias_ref, gain_ref,
+    wo_ref, keep_ref, send_ref, kaug_ref, qaug_ref, att_ref, wo_vmem, sems,
 ):
     step = pl.program_id(0)
-    width = key_ref.shape[-1]
+    width = query_ref.shape[-1]
+    count = sems.shape[0]
+    rows = wo_ref.shape[0] // count
+    copies = [
+        pltpu.make_async_copy(
+            wo_ref.at[i * rows : (i + 1) * rows], wo_vmem.at[i * rows : (i + 1) * rows], sems.at[i]
+        )
+        for i in range(count)
+    ]
 
     @pl.when(step == 0)
     def _():
-        kaug_ref[...] = widen(key_ref[...].reshape(-1, width), gram_ref)
+        for copy in copies:
+            copy.start()
+        part = kaug_ref.shape[0] // len(key_refs)
+        for i, key_ref in enumerate(key_refs):
+            kaug_ref[i * part : (i + 1) * part] = widen(
+                key_ref[...].reshape(-1, width), gram_ref
+            )
         qaug_ref[...] = widen(query_ref[...].reshape(-1, width), gram_ref)
 
     kaug = kaug_ref[...]
@@ -226,27 +247,23 @@
         total = jnp.sum(e, axis=1, keepdims=True)
         o = jnp.dot(e.astype(bf16), v, preferred_element_type=f32)
         outs.append((o / total).astype(bf16))
-    att = outs[0] if hp == 1 else jnp.concatenate(outs, axis=1)
-    part = jnp.dot(att, wo_ref[...], preferred_element_type=f32)
-
-    @pl.when(step == 0)
-    def _():
-        acc_ref[...] = part
-
-    @pl.when(step > 0)
-    def _():
-        acc_ref[...] += part
+    att_ref[step] = outs[0] if hp == 1 else jnp.concatenate(outs, axis=1)
 
     @pl.when(step == pl.num_programs(0) - 1)
     def _():
+        for copy in copies:
+            copy.wait()
+        att = jnp.concatenate([att_ref[i] for i in range(att_ref.shape[0])], axis=1)
+        part = jnp.dot(att, wo_vmem[...], preferred_element_type=f32)
         tok = keep_ref.shape[1]
         for i in range(keep_ref.shape[0]):
-            keep_ref[i] = acc_ref[2 * i * tok : (2 * i + 1) * tok, :]
-            send_ref[i] = acc_ref[(2 * i + 1) * tok : (2 * i + 2) * tok, :].astype(bf16)
+            keep_ref[i] = part[2 * i * tok : (2 * i + 1) * tok, :]
+            send_ref[i] = part[(2 * i + 1) * tok : (2 * i + 2) * tok, :].astype(bf16)
 
 
 def attend(keys, queries, slot, at, gram, folded, gain, out_weight):
-    nr, nc, _, tok, width = keys.shape
+    each, nc, _, tok, width = keys[0].shape
+    nr = each * len(keys)
     slots = folded.shape[0] // width
     head_dim = gain.shape[1]
     heads = folded.shape[1] // (3 * head_dim)
@@ -257,16 +274,16 @@
     spare = folded.shape[0] - slots * width
     out_spec = pl.BlockSpec((half, tok, depth), lambda h: (0, 0, 0))
     return pl.pallas_call(
-        functools.partial(attend_kernel, hp, head_dim, slot, slots),
+        functools.partial(attend_kernel, hp, head_dim, slot, slots, len(keys)),
         grid=(heads // hp,),
         in_specs=[
-            pl.BlockSpec((nr, nc, None, tok, width), lambda h: (0, 0, at, 0, 0)),
+            *[pl.BlockSpec((each, nc, None, tok, width), lambda h: (0, 0, at, 0, 0))] * len(keys),
             pl.BlockSpec((nc, None, tok, width), lambda h: (0, at, 0, 0)),
             pl.BlockSpec((2, width, width), lambda h: (0, 0, 0)),
             pl.BlockSpec((width, hp * 3 * head_dim), lambda h: (slot, h)),
             pl.BlockSpec((spare, hp * 3 * head_dim), lambda h: (slots * width // spare, h)),
             pl.BlockSpec((1, head_dim), lambda h: (0, 0)),
-            pl.BlockSpec((hp * head_dim, depth), lambda h: (h, 0)),
+            pl.BlockSpec(memory_space=pltpu.HBM),
         ],
         out_specs=[out_spec, out_spec],
         out_shape=[
@@ -276,15 +293,17 @@
         scratch_shapes=[
             pltpu.VMEM((nk, 4 * width), bf16),
             pltpu.VMEM((nq, 4 * width), bf16),
-            pltpu.VMEM((nq, depth), f32),
+            pltpu.VMEM((heads // hp, nq, hp * head_dim), bf16),
+            pltpu.VMEM(out_weight.shape, bf16),
+            pltpu.SemaphoreType.DMA((3,)),
         ],
-        compiler_params=pltpu.CompilerParams(vmem_limit_bytes=40 * 2**20),
+        compiler_params=pltpu.CompilerParams(vmem_limit_bytes=16 * 2**20 + 24 * nq * nk),
         cost_estimate=pl.CostEstimate(
             flops=2 * heads * (nk * 256 * 256 + 2 * nq * nk * head_dim * 2 + nq * head_dim * depth),
             bytes_accessed=heads * head_dim * depth * 2 + nq * depth * 3,
             transcendentals=heads * nq * nk,
         ),
-    )(keys, queries, gram, folded, folded, gain, out_weight)
+    )(*keys, queries, gram, folded, folded, gain, out_weight)
 
 
 def heads_per_step(heads):
@@ -296,11 +315,15 @@
     return lax.ppermute(value, axis, [(i, i ^ bit) for i in range(count)])
 
 
-def spread(value, axis, bits):
+def reached(value, axis, bits):
     masks = [0]
     for bit in bits:
         masks += [mask | bit for mask in masks]
-    return jnp.stack([value] + [exchange(value, axis, mask) for mask in masks[1:]])
+    return [value] + [exchange(value, axis, mask) for mask in masks[1:]]
+
+
+def spread(value, axis, bits):
+    return jnp.stack(reached(value, axis, bits))
 
 
 def bits_of(axis):
@@ -309,10 +332,10 @@
 
 def finish_row(keys, shape):
     rest = bits_of("row")[1:]
-    while rest:
-        keys = spread(keys, "row", rest[:2]).reshape(-1, *shape)
-        rest = rest[2:]
-    return keys
+    while len(rest) > 2:
+        keys = spread(keys, "row", rest[:1]).reshape(-1, *shape)
+        rest = rest[1:]
+    return reached(keys, "row", rest)
 
 
 def fold_inputs(embed_weight, scale, shift):
@@ -359,10 +382,10 @@
         for k in range(step_total)
     )
     head_dim = q_gain.shape[0]
-    lhs, gram = fold_inputs(embed_weight, mods[:, 1, :], mods[:, 0, :])
+    pair = spread(queries, "row", bits_of("row")[:1])
+    pair, early_weight, early_mods = tie((pair, embed_weight, mods))
+    lhs, gram = fold_inputs(early_weight, early_mods[:, 1, :], early_mods[:, 0, :])
     gain = (q_gain * k_gain * (math.log2(math.e) / math.sqrt(head_dim)))[None]
-    pair = spread(queries, "row", bits_of("row")[:1])
-    pair, lhs = tie((pair, lhs))
     keys = finish_row(pair, queries.shape)
     folded = jnp.dot(lhs, qkv_weight, preferred_element_type=f32)
 
@@ -387,8 +410,7 @@
             bit *= 2
         sums[slot] = total[0]
 
-    parts[1] = attended(1, keys, queries, 0)
-    mid, left, right, parts[1] = tie((mid, left, right, parts[1]))
+    mid, left, right, folded = tie((mid, left, right, folded))
     latent = encode(left, mid, right, tile_rows, conv_first, conv_second, conv_last)
     channels = latent.shape[-1]
     tok = tile_rows // 2 * (tile_cols // 2)
@@ -399,22 +421,25 @@
     )
     sigma = (step_total - step_index.astype(f32)) / (step_total + 1.0)
     fresh = ((1.0 - sigma[0]) * patch + sigma[0] * noise.astype(f32)).astype(bf16)
+    arrived = reached(fresh[None], "col", bits_of("col"))
+    fresh, queries = tie((fresh, queries))
+    parts[1] = attended(1, keys, queries, 0)
+    arrived, queries, parts[1] = tie((arrived, queries, parts[1]))
+    fresh_queries = jnp.stack(arrived)
+    fresh_pair = spread(fresh_queries, "row", bits_of("row")[:1])
+    parts[2] = attended(2, keys, queries, 1)
     first(1)
-    fresh, queries, parts[1] = tie((fresh, queries, parts[1]))
-    fresh_queries = spread(fresh[None], "col", bits_of("col"))
-    parts[2] = attended(2, keys, queries, 1)
-    fresh_pair = spread(fresh_queries, "row", bits_of("row")[:1])
-    fresh_pair, queries, parts[2] = tie((fresh_pair, queries, parts[2]))
+    fresh_pair, queries, parts[1], parts[2] = tie((fresh_pair, queries, parts[1], parts[2]))
     fresh_keys = finish_row(fresh_pair, fresh_queries.shape)
     parts[3] = attended(3, keys, queries, 2)
-    rest(1)
     first(2)
-    sums[1], parts[2], parts[3] = tie((sums[1], parts[2], parts[3]))
     fresh_queries, parts[2], parts[3] = tie((fresh_queries, parts[2], parts[3]))
     parts[0] = attended(0, fresh_keys, fresh_queries, 0)
+    rest(1)
+    first(3)
+    sums[1], parts[3], parts[0] = tie((sums[1], parts[3], parts[0]))
     rest(2)
-    first(3)
-    sums[2], parts[3], parts[0] = tie((sums[2], parts[3], parts[0]))
+    sums[2], parts[3] = tie((sums[2], parts[3]))
     first(0)
     rest(3)
     rest(0)

time: 134 us -> 125 us (0.933)
  waiting for transfers between devices: 33.9 us -> 25.3 us
  other arithmetic: 7.75 us -> 5.28 us
  starting transfers between devices: 37.2 us -> 38.9 us
    ppermute x22, waiting for transfers between devices: 33.9 us -> 25.3 us  [exchange(): return lax.ppermute(value, axis, [(i, i ^ bit) for i in range(count)])]
    ppermute x22, starting transfers between devices: 29.8 us -> 31.9 us  [exchange(): return lax.ppermute(value, axis, [(i, i ^ bit) for i in range(count)])]
    concatenate x1 -> x0, other arithmetic: 1.68 us -> none  [fold_inputs(): jnp.concatenate([scaled, shift_hi, shift_lo, jnp.zeros((spare, depth), bf...]
    unnamed x45 -> x37, local copies, waits for them, and re-layouts: 3.5 us -> 3.48 us
  transfers between devices with their start and end apart: 26 -> 26, of which waited for: 8 -> 4; matrix products, arithmetic and copies ran while one was open for 14% -> 14% of each run, Pallas kernels for 28% -> 29%
where the time goes in v3:
time: 125 us; the launch traced here: 124 us
  starting transfers between devices  38.9 us (31%)
  Pallas kernels  35.9 us (29%)
  waiting for transfers between devices  25.3 us (20%)
  matrix products  9.3 us (7%)
  local copies, waits for them, and re-layouts  8.74 us (7%)
  other arithmetic  5.28 us (4%)
    ppermute x22, starting transfers between devices, exchange(): return lax.ppermute(value, axis, [(i, i ^ bit) for i in range(count)])  31.9 us
    pallas_call x4, Pallas kernels, attend(): pl.pallas_call(functools.partial(attend_kernel, hp, head_dim, slot, slots...  29.8 us
    ppermute x22, waiting for transfers between devices, exchange(): return lax.ppermute(value, axis, [(i, i ^ bit) for i in range(count)])  25.3 us
    dot_general x1, matrix products, on_device(): folded = jnp.dot(lhs, qkv_weight, preferred_element_type=f32)  8.02 us
    pallas_call x1, Pallas kernels, encode(): pl.pallas_call(encode_kernel, grid=(6,), in_specs=[pl.BlockSpec(memory_sp...  6.02 us
    unnamed x37, local copies, waits for them, and re-layouts  3.48 us
    ppermute x1, starting transfers between devices, sides(): left = lax.ppermute(mid[-3:], 'col', [(i, i + 1) for i in range(nc - 1)])  3.15 us
  transfers between devices with their start and end apart: 26, of which 4 were waited for; matrix products, arithmetic and copies ran while one was open for 14% of the time, Pallas kernels for 29%

profile of v3, /device:TPU:0, one launch (start us, length us, event | category | flops | bytes accessed | tf_op | source)
XLA Modules:
  0.0 124.1 jit_solution(14776029215118569218)
XLA Ops:
  0.0 5.0 %collective-permute-start.6 = (bf16[3,32,64]{2,1,0:T(8,128)(2,1)}, bf16[3,32,64]{2,1,0:T(8,128)(2,1)S(1)}, u32[]{:S(2)}, u32[]{:S(2)}) collective-permute-start(bf16[3,32,64]{2,1,0:T(8,128)(2,1)} %bitcast.126), channel_id=1, source_target_pairs={{0,3},{1,2},{2,1},{3,0},{4,7},{5,6},{6,5},{7,4},{8,11},{9,10},{10,... | collective-permute-start | bytes 36872 | tf_op jit(solution)/shard_map/ppermute | solution.py:315
  5.7 1.0 copy.45
  6.7 1.3 %collective-permute-start.1 = (bf16[16,3,512]{2,1,0:T(4,128)(2,1)S(1)}, bf16[16,3,512]{2,1,0:T(4,128)(2,1)S(1)}, u32[]{:S(2)}, u32[]{:S(2)}) collective-permute-start(bf16[16,3,512]{2,1,0:T(4,128)(2,1)S(1)} %get-tuple-element.108), channel_id=1, source_target_pairs={{0,4},{4,8},{8,12},{12,16},{16,20},{20,24},{24,28},{1,5},{5,9},{9,... | collective-permute-start | bytes 147464 | tf_op jit(solution)/shard_map/ppermute | solution.py:104
  8.0 1.3 %collective-permute-start = (bf16[16,3,512]{2,1,0:T(4,128)(2,1)S(1)}, bf16[16,3,512]{2,1,0:T(4,128)(2,1)S(1)}, u32[]{:S(2)}, u32[]{:S(2)}) collective-permute-start(bf16[16,3,512]{2,1,0:T(4,128)(2,1)S(1)} %get-tuple-element.107), channel_id=1, source_target_pairs={{4,0},{8,4},{12,8},{16,12},{20,16},{24,20},{28,24},{5,1},{9,5},{13... | collective-permute-start | bytes 147464 | tf_op jit(solution)/shard_map/ppermute | solution.py:105
  10.6 1.4 %fusion.29 = (f32[1,3,3072]{2,0,1:T(1,128)S(1)}, f32[1,3,3072]{2,0,1:T(1,128)S(1)}, f32[1,3,3072]{2,0,1:T(1,128)S(1)}, f32[1,3,3072]{2,0,1:T(1,128)S(1)}) fusion(f32[4,3,3072]{2,0,1:T(4,128)} %param.20), kind=kLoop, calls=%fused_computation.83 | loop fusion | bytes 294912 | tf_op jit(solution)/shard_map/slice | solution.py:381
  14.7 3.1 %collective-permute-start.7 = (bf16[4,3,32,64]{3,2,1,0:T(8,128)(2,1)S(1)}, bf16[4,3,32,64]{3,2,1,0:T(8,128)(2,1)S(1)}, u32[]{:S(2)}, u32[]{:S(2)}) collective-permute-start(bf16[4,3,32,64]{3,2,1,0:T(8,128)(2,1)S(1)} %get-tuple-element.72.refs_4_), channel_id=1, source_target_pairs={{0,4},{4,0},{8,12},{12,8},{16,20},{20,16},{24,28},{28,24},{1,5},{5... | collective-permute-start | bytes 147464 | tf_op jit(solution)/shard_map/ppermute | solution.py:315
  17.9 3.1 %collective-permute-start.2 = (bf16[3,16,512]{2,1,0:T(8,128)(2,1)S(1)}, bf16[3,16,512]{2,1,0:T(8,128)(2,1)S(1)}, u32[]{:S(2)}, u32[]{:S(2)}) collective-permute-start(bf16[3,16,512]{2,1,0:T(8,128)(2,1)S(1)} %get-tuple-element.96), channel_id=1, source_target_pairs={{0,1},{1,2},{2,3},{4,5},{5,6},{6,7},{8,9},{9,10},{10,11},{12,13},{... | collective-permute-start | bytes 147464 | tf_op jit(solution)/shard_map/ppermute | solution.py:113
  21.1 1.3 %collective-permute-start.3 = (bf16[3,16,512]{2,1,0:T(8,128)(2,1)S(1)}, bf16[3,16,512]{2,1,0:T(8,128)(2,1)S(1)}, u32[]{:S(2)}, u32[]{:S(2)}) collective-permute-start(bf16[3,16,512]{2,1,0:T(8,128)(2,1)S(1)} %get-tuple-element.95), channel_id=1, source_target_pairs={{1,0},{2,1},{3,2},{5,4},{6,5},{7,6},{9,8},{10,9},{11,10},{13,12},{... | collective-permute-start | bytes 147464 | tf_op jit(solution)/shard_map/ppermute | solution.py:114
  22.6 1.7 %collective-permute-start.11 = (bf16[2,4,3,32,64]{4,3,2,1,0:T(8,128)(2,1)S(1)}, bf16[2,4,3,32,64]{4,3,2,1,0:T(8,128)(2,1)S(1)}, u32[]{:S(2)}, u32[]{:S(2)}) collective-permute-start(bf16[2,4,3,32,64]{4,3,2,1,0:T(8,128)(2,1)S(1)} %pad_maximum_fusion.2.refs_0_), channel_id=1, source_target_pairs={{0,8},{4,12},{8,0},{12,4},{16,24},{20,28},{24,16},{28,20},{1,9},{5... | collective-permute-start | bytes 294920 | tf_op jit(solution)/shard_map/ppermute | solution.py:315
  24.3 1.5 %collective-permute-start.12 = (bf16[2,4,3,32,64]{4,3,2,1,0:T(8,128)(2,1)S(1)}, bf16[2,4,3,32,64]{4,3,2,1,0:T(8,128)(2,1)S(1)}, u32[]{:S(2)}, u32[]{:S(2)}) collective-permute-start(bf16[2,4,3,32,64]{4,3,2,1,0:T(8,128)(2,1)S(1)} %pad_maximum_fusion.2.refs_0_), channel_id=1, source_target_pairs={{0,16},{4,20},{8,24},{12,28},{16,0},{20,4},{24,8},{28,12},{1,17},{... | collective-permute-start | bytes 294920 | tf_op jit(solution)/shard_map/ppermute | solution.py:315
  25.8 0.9 collective-permute-start.13
  27.0 0.9 convert_bitcast_fusion
  28.3 8.0 %fusion.refs_6_.refs_7_ = f32[272,2304]{1,0:T(8,128)S(1)} fusion(bf16[3072,2304]{1,0:T(8,128)(2,1)} %param.22, bf16[4,3072]{1,0:T(4,128)(2,1)S(1)} %fusion.18, bf16[4,3072]{1,0:T(4,128)(2,1)S(1)} %bitcast.144, bf16[256,3072]{1,0:T(8,128)(2,1)S(1)} %bitcast.119, bf16[272]{0:T(512)(128)(2,1)S(1)} %pad.17.clone), kind=kOutput, calls=%fused_computation.2 | convolution fusion | flops 3857055744 | bytes 18285088 | tf_op jit(solution)/shard_map/dot_general | solution.py:390
  36.4 6.0 %shard_map.127 = f32[16,8,16]{2,1,0:T(8,128)S(1)} custom-call(s32[4]{0:T(128)S(1)} %pad_add_fusion.place_ref, bf16[3,16,512]{2,1,0:T(8,128)(2,1)S(1)} %collective-permute-done.2.left_ref, bf16[16,16,512]{2,1,0:T(8,128)(2,1)S(1)} %pad_maximum_fusion.1.mid_ref, bf16[3,16,512]{2,1,0:T(8,128)(2,1)S(1)} %collective-permute-done.3.right_ref, ...), custom_call_target="tpu_custom_call" | custom-call | flops 3373793280 | bytes 10616832 | tf_op jit(solution)/shard_map/pallas_call | solution.py:137
  43.3 2.7 %collective-permute-start.8 = (bf16[1,32,64]{2,1,0:T(8,128)(2,1)S(1)}, bf16[1,32,64]{2,1,0:T(8,128)(2,1)S(1)}, u32[]{:S(2)}, u32[]{:S(2)}) collective-permute-start(bf16[1,32,64]{2,1,0:T(8,128)(2,1)S(1)} %bitcast.131), channel_id=1, source_target_pairs={{0,1},{1,0},{2,3},{3,2},{4,5},{5,4},{6,7},{7,6},{8,9},{9,8},{10,11... | collective-permute-start | bytes 12296 | tf_op jit(solution)/shard_map/ppermute | solution.py:315
  45.9 3.0 %collective-permute-start.9 = (bf16[1,32,64]{2,1,0:T(8,128)(2,1)S(1)}, bf16[1,32,64]{2,1,0:T(8,128)(2,1)S(1)}, u32[]{:S(2)}, u32[]{:S(2)}) collective-permute-start(bf16[1,32,64]{2,1,0:T(8,128)(2,1)S(1)} %bitcast.132), channel_id=1, source_target_pairs={{0,2},{1,3},{2,0},{3,1},{4,6},{5,7},{6,4},{7,5},{8,10},{9,11},{10,... | collective-permute-start | bytes 12296 | tf_op jit(solution)/shard_map/ppermute | solution.py:315
  48.9 2.3 %copy-done = bf16[768,3072]{1,0:T(8,128)(2,1)S(1)} copy-done((bf16[768,3072]{1,0:T(8,128)(2,1)S(1)}, bf16[768,3072]{1,0:T(8,128)(2,1)}, u32[]{:S(2)}) %copy-start) | copy-done | bytes 4718616
  51.2 7.4 %shard_map.128 = (f32[2,32,3072]{2,1,0:T(8,128)S(1)}, bf16[2,32,3072]{2,1,0:T(8,128)(2,1)S(1)}) custom-call(bf16[2,4,3,32,64]{4,3,2,1,0:T(8,128)(2,1)S(1)} %pad_maximum_fusion.2.refs_0_, bf16[2,4,3,32,64]{4,3,2,1,0:T(8,128)(2,1)S(1)} %collective-permute-done.11.refs_1_, bf16[2,4,3,32,64]{4,3,2,1,0:T(8,128)(2,1)S(1)} %collective-permute-done.12.refs_2_, ...), custom_call_target="tpu_custom_call" | custom-call | flops 2214592512 | bytes 5898240 | tf_op jit(solution)/shard_map/pallas_call | solution.py:276
  59.4 7.6 %shard_map.129 = (f32[2,32,3072]{2,1,0:T(8,128)S(1)}, bf16[2,32,3072]{2,1,0:T(8,128)(2,1)S(1)}) custom-call(bf16[2,4,3,32,64]{4,3,2,1,0:T(8,128)(2,1)S(1)} %pad_maximum_fusion.2.refs_0_, bf16[2,4,3,32,64]{4,3,2,1,0:T(8,128)(2,1)S(1)} %collective-permute-done.11.refs_1_, bf16[2,4,3,32,64]{4,3,2,1,0:T(8,128)(2,1)S(1)} %collective-permute-done.12.refs_2_, ...), custom_call_target="tpu_custom_call" | custom-call | flops 2214592512 | bytes 5898240 | tf_op jit(solution)/shard_map/pallas_call | solution.py:276
  67.1 1.5 %collective-permute-done.15 = bf16[2,32,3072]{2,1,0:T(8,128)(2,1)S(1)} collective-permute-done((bf16[2,32,3072]{2,1,0:T(8,128)(2,1)S(1)}, bf16[2,32,3072]{2,1,0:T(8,128)(2,1)S(1)}, u32[]{:S(2)}, u32[]{:S(2)}) %collective-permute-start.15) | collective-permute-done | bytes 393248 | tf_op jit(solution)/shard_map/ppermute | solution.py:315
  69.7 0.9 collective-permute-start.19
  70.6 1.5 %collective-permute-start.20 = (bf16[2,4,1,32,64]{4,3,1,2,0:T(8,128)(2,1)S(1)}, bf16[2,4,1,32,64]{4,3,1,2,0:T(8,128)(2,1)S(1)}, u32[]{:S(2)}, u32[]{:S(2)}) collective-permute-start(bf16[2,4,1,32,64]{4,3,1,2,0:T(8,128)(2,1)S(1)} %pad_maximum_fusion.4), channel_id=1, source_target_pairs={{0,16},{4,20},{8,24},{12,28},{16,0},{20,4},{24,8},{28,12},{1,17},{... | collective-permute-start | bytes 98312 | tf_op jit(solution)/shard_map/ppermute | solution.py:315
  72.1 1.2 collective-permute-start.21
  73.3 3.5 %collective-permute-start.16 = (bf16[1,32,3072]{2,1,0:T(8,128)(2,1)S(1)}, bf16[1,32,3072]{2,1,0:T(8,128)(2,1)S(1)}, u32[]{:S(2)}, u32[]{:S(2)}) collective-permute-start(bf16[1,32,3072]{2,1,0:T(8,128)(2,1)S(1)} %slice.170), channel_id=1, source_target_pairs={{0,2},{1,3},{2,0},{3,1},{4,6},{5,7},{6,4},{7,5},{8,10},{9,11},{10,... | collective-permute-start | bytes 589832 | tf_op jit(solution)/shard_map/ppermute | solution.py:315
  76.8 7.4 %shard_map.130 = (f32[2,32,3072]{2,1,0:T(8,128)S(1)}, bf16[2,32,3072]{2,1,0:T(8,128)(2,1)S(1)}) custom-call(bf16[2,4,3,32,64]{4,3,2,1,0:T(8,128)(2,1)S(1)} %pad_maximum_fusion.2.refs_0_, bf16[2,4,3,32,64]{4,3,2,1,0:T(8,128)(2,1)S(1)} %collective-permute-done.11.refs_1_, bf16[2,4,3,32,64]{4,3,2,1,0:T(8,128)(2,1)S(1)} %collective-permute-done.12.refs_2_, ...), custom_call_target="tpu_custom_call" | custom-call | flops 2214592512 | bytes 5898240 | tf_op jit(solution)/shard_map/pallas_call | solution.py:276
  85.6 7.4 %shard_map.131 = (f32[2,32,3072]{2,1,0:T(8,128)S(1)}, bf16[2,32,3072]{2,1,0:T(8,128)(2,1)S(1)}) custom-call(bf16[2,4,1,32,64]{4,3,2,1,0:T(8,128)(2,1)S(1)} %bitcast.114, bf16[2,4,1,32,64]{4,3,2,1,0:T(8,128)(2,1)S(1)} %bitcast.116, bf16[2,4,1,32,64]{4,3,2,1,0:T(8,128)(2,1)S(1)} %bitcast.117, bf16[2,4,1,32,64]{4,3,2,1,0:T(8,128)(2,1)S(1)} %bitcast.118, ...), custom_call_target="tpu_custom_call" | custom-call | flops 2214592512 | bytes 5898240 | tf_op jit(solution)/shard_map/pallas_call | solution.py:276
  93.0 5.2 %collective-permute-done.18 = bf16[2,32,3072]{2,1,0:T(8,128)(2,1)S(1)} collective-permute-done((bf16[2,32,3072]{2,1,0:T(8,128)(2,1)S(1)}, bf16[2,32,3072]{2,1,0:T(8,128)(2,1)S(1)}, u32[]{:S(2)}, u32[]{:S(2)}) %collective-permute-start.18) | collective-permute-done | bytes 393248 | tf_op jit(solution)/shard_map/ppermute | solution.py:315
  99.2 2.3 %collective-permute-start.25 = (bf16[1,32,3072]{2,1,0:T(8,128)(2,1)S(1)}, bf16[1,32,3072]{2,1,0:T(8,128)(2,1)S(1)}, u32[]{:S(2)}, u32[]{:S(2)}) collective-permute-start(bf16[1,32,3072]{2,1,0:T(8,128)(2,1)S(1)} %slice.168), channel_id=1, source_target_pairs={{0,2},{1,3},{2,0},{3,1},{4,6},{5,7},{6,4},{7,5},{8,10},{9,11},{10,... | collective-permute-start | bytes 589832 | tf_op jit(solution)/shard_map/ppermute | solution.py:315
  101.5 10.3 %collective-permute-done.22 = bf16[2,32,3072]{2,1,0:T(8,128)(2,1)S(1)} collective-permute-done((bf16[2,32,3072]{2,1,0:T(8,128)(2,1)S(1)}, bf16[2,32,3072]{2,1,0:T(8,128)(2,1)S(1)}, u32[]{:S(2)}, u32[]{:S(2)}) %collective-permute-start.22) | collective-permute-done | bytes 393248 | tf_op jit(solution)/shard_map/ppermute | solution.py:315
  111.9 2.0 %collective-permute-start.23 = (bf16[1,32,3072]{2,1,0:T(8,128)(2,1)S(1)}, bf16[1,32,3072]{2,1,0:T(8,128)(2,1)S(1)}, u32[]{:S(2)}, u32[]{:S(2)}) collective-permute-start(bf16[1,32,3072]{2,1,0:T(8,128)(2,1)S(1)} %slice.167), channel_id=1, source_target_pairs={{0,2},{1,3},{2,0},{3,1},{4,6},{5,7},{6,4},{7,5},{8,10},{9,11},{10,... | collective-permute-start | bytes 589832 | tf_op jit(solution)/shard_map/ppermute | solution.py:315
  114.0 8.3 %collective-permute-done.23 = bf16[1,32,3072]{2,1,0:T(8,128)(2,1)S(1)} collective-permute-done((bf16[1,32,3072]{2,1,0:T(8,128)(2,1)S(1)}, bf16[1,32,3072]{2,1,0:T(8,128)(2,1)S(1)}, u32[]{:S(2)}, u32[]{:S(2)}) %collective-permute-start.23) | collective-permute-done | bytes 196640 | tf_op jit(solution)/shard_map/ppermute | solution.py:315
  122.6 1.5 %copy.27 = bf16[32,4,3072]{2,1,0:T(4,128)(2,1)} copy(bf16[32,4,3072]{2,0,1:T(8,128)(2,1)S(1)} %pad_maximum_fusion) | data formatting | bytes 1572864 | tf_op jit(solution)/shard_map/stack | solution.py:454
  (117 shorter events, 10.9 us)
Async XLA Ops:
  0.0 26.7 %copy-start.2 = (bf16[64,3072]{1,0:T(8,128)(2,1)S(1)}, bf16[64,3072]{1,0:T(8,128)(2,1)}, u32[]{:S(2)}) copy-start(bf16[64,3072]{1,0:T(8,128)(2,1)} %param.21) | copy-start | bytes 1179652
  0.0 13.9 %collective-permute-start.6 = (bf16[3,32,64]{2,1,0:T(8,128)(2,1)}, bf16[3,32,64]{2,1,0:T(8,128)(2,1)S(1)}, u32[]{:S(2)}, u32[]{:S(2)}) collective-permute-start(bf16[3,32,64]{2,1,0:T(8,128)(2,1)} %bitcast.126), channel_id=1, source_target_pairs={{0,3},{1,2},{2,1},{3,0},{4,7},{5,6},{6,5},{7,4},{8,11},{9,10},{10,... | collective-permute-start | bytes 36872 | tf_op jit(solution)/shard_map/ppermute | solution.py:315
  5.1 8.8 %collective-permute-start.5 = (bf16[3,32,64]{2,1,0:T(8,128)(2,1)}, bf16[3,32,64]{2,1,0:T(8,128)(2,1)S(1)}, u32[]{:S(2)}, u32[]{:S(2)}) collective-permute-start(bf16[3,32,64]{2,1,0:T(8,128)(2,1)} %bitcast.127), channel_id=1, source_target_pairs={{0,2},{1,3},{2,0},{3,1},{4,6},{5,7},{6,4},{7,5},{8,10},{9,11},{10,... | collective-permute-start | bytes 36872 | tf_op jit(solution)/shard_map/ppermute | solution.py:315
  5.1 8.8 %collective-permute-start.4 = (bf16[3,32,64]{2,1,0:T(8,128)(2,1)}, bf16[3,32,64]{2,1,0:T(8,128)(2,1)S(1)}, u32[]{:S(2)}, u32[]{:S(2)}) collective-permute-start(bf16[3,32,64]{2,1,0:T(8,128)(2,1)} %bitcast.128), channel_id=1, source_target_pairs={{0,1},{1,0},{2,3},{3,2},{4,5},{5,4},{6,7},{7,6},{8,9},{9,8},{10,11... | collective-permute-start | bytes 36872 | tf_op jit(solution)/shard_map/ppermute | solution.py:315
  6.7 11.0 %collective-permute-start.1 = (bf16[16,3,512]{2,1,0:T(4,128)(2,1)S(1)}, bf16[16,3,512]{2,1,0:T(4,128)(2,1)S(1)}, u32[]{:S(2)}, u32[]{:S(2)}) collective-permute-start(bf16[16,3,512]{2,1,0:T(4,128)(2,1)S(1)} %get-tuple-element.108), channel_id=1, source_target_pairs={{0,4},{4,8},{8,12},{12,16},{16,20},{20,24},{24,28},{1,5},{5,9},{9,... | collective-permute-start | bytes 147464 | tf_op jit(solution)/shard_map/ppermute | solution.py:104
  8.0 9.7 %collective-permute-start = (bf16[16,3,512]{2,1,0:T(4,128)(2,1)S(1)}, bf16[16,3,512]{2,1,0:T(4,128)(2,1)S(1)}, u32[]{:S(2)}, u32[]{:S(2)}) collective-permute-start(bf16[16,3,512]{2,1,0:T(4,128)(2,1)S(1)} %get-tuple-element.107), channel_id=1, source_target_pairs={{4,0},{8,4},{12,8},{16,12},{20,16},{24,20},{28,24},{5,1},{9,5},{13... | collective-permute-start | bytes 147464 | tf_op jit(solution)/shard_map/ppermute | solution.py:105
  14.7 7.7 %collective-permute-start.7 = (bf16[4,3,32,64]{3,2,1,0:T(8,128)(2,1)S(1)}, bf16[4,3,32,64]{3,2,1,0:T(8,128)(2,1)S(1)}, u32[]{:S(2)}, u32[]{:S(2)}) collective-permute-start(bf16[4,3,32,64]{3,2,1,0:T(8,128)(2,1)S(1)} %get-tuple-element.72.refs_4_), channel_id=1, source_target_pairs={{0,4},{4,0},{8,12},{12,8},{16,20},{20,16},{24,28},{28,24},{1,5},{5... | collective-permute-start | bytes 147464 | tf_op jit(solution)/shard_map/ppermute | solution.py:315
  17.9 18.4 %collective-permute-start.2 = (bf16[3,16,512]{2,1,0:T(8,128)(2,1)S(1)}, bf16[3,16,512]{2,1,0:T(8,128)(2,1)S(1)}, u32[]{:S(2)}, u32[]{:S(2)}) collective-permute-start(bf16[3,16,512]{2,1,0:T(8,128)(2,1)S(1)} %get-tuple-element.96), channel_id=1, source_target_pairs={{0,1},{1,2},{2,3},{4,5},{5,6},{6,7},{8,9},{9,10},{10,11},{12,13},{... | collective-permute-start | bytes 147464 | tf_op jit(solution)/shard_map/ppermute | solution.py:113
  21.1 15.2 %collective-permute-start.3 = (bf16[3,16,512]{2,1,0:T(8,128)(2,1)S(1)}, bf16[3,16,512]{2,1,0:T(8,128)(2,1)S(1)}, u32[]{:S(2)}, u32[]{:S(2)}) collective-permute-start(bf16[3,16,512]{2,1,0:T(8,128)(2,1)S(1)} %get-tuple-element.95), channel_id=1, source_target_pairs={{1,0},{2,1},{3,2},{5,4},{6,5},{7,6},{9,8},{10,9},{11,10},{13,12},{... | collective-permute-start | bytes 147464 | tf_op jit(solution)/shard_map/ppermute | solution.py:114
  22.6 26.3 %collective-permute-start.11 = (bf16[2,4,3,32,64]{4,3,2,1,0:T(8,128)(2,1)S(1)}, bf16[2,4,3,32,64]{4,3,2,1,0:T(8,128)(2,1)S(1)}, u32[]{:S(2)}, u32[]{:S(2)}) collective-permute-start(bf16[2,4,3,32,64]{4,3,2,1,0:T(8,128)(2,1)S(1)} %pad_maximum_fusion.2.refs_0_), channel_id=1, source_target_pairs={{0,8},{4,12},{8,0},{12,4},{16,24},{20,28},{24,16},{28,20},{1,9},{5... | collective-permute-start | bytes 294920 | tf_op jit(solution)/shard_map/ppermute | solution.py:315
  24.3 24.6 %collective-permute-start.12 = (bf16[2,4,3,32,64]{4,3,2,1,0:T(8,128)(2,1)S(1)}, bf16[2,4,3,32,64]{4,3,2,1,0:T(8,128)(2,1)S(1)}, u32[]{:S(2)}, u32[]{:S(2)}) collective-permute-start(bf16[2,4,3,32,64]{4,3,2,1,0:T(8,128)(2,1)S(1)} %pad_maximum_fusion.2.refs_0_), channel_id=1, source_target_pairs={{0,16},{4,20},{8,24},{12,28},{16,0},{20,4},{24,8},{28,12},{1,17},{... | collective-permute-start | bytes 294920 | tf_op jit(solution)/shard_map/ppermute | solution.py:315
  25.8 23.1 %collective-permute-start.13 = (bf16[2,4,3,32,64]{4,3,2,1,0:T(8,128)(2,1)S(1)}, bf16[2,4,3,32,64]{4,3,2,1,0:T(8,128)(2,1)S(1)}, u32[]{:S(2)}, u32[]{:S(2)}) collective-permute-start(bf16[2,4,3,32,64]{4,3,2,1,0:T(8,128)(2,1)S(1)} %pad_maximum_fusion.2.refs_0_), channel_id=1, source_target_pairs={{0,24},{4,28},{8,16},{12,20},{16,8},{20,12},{24,0},{28,4},{1,25},{... | collective-permute-start | bytes 294920 | tf_op jit(solution)/shard_map/ppermute | solution.py:315
  43.3 15.4 %collective-permute-start.8 = (bf16[1,32,64]{2,1,0:T(8,128)(2,1)S(1)}, bf16[1,32,64]{2,1,0:T(8,128)(2,1)S(1)}, u32[]{:S(2)}, u32[]{:S(2)}) collective-permute-start(bf16[1,32,64]{2,1,0:T(8,128)(2,1)S(1)} %bitcast.131), channel_id=1, source_target_pairs={{0,1},{1,0},{2,3},{3,2},{4,5},{5,4},{6,7},{7,6},{8,9},{9,8},{10,11... | collective-permute-start | bytes 12296 | tf_op jit(solution)/shard_map/ppermute | solution.py:315
  45.9 12.8 %collective-permute-start.9 = (bf16[1,32,64]{2,1,0:T(8,128)(2,1)S(1)}, bf16[1,32,64]{2,1,0:T(8,128)(2,1)S(1)}, u32[]{:S(2)}, u32[]{:S(2)}) collective-permute-start(bf16[1,32,64]{2,1,0:T(8,128)(2,1)S(1)} %bitcast.132), channel_id=1, source_target_pairs={{0,2},{1,3},{2,0},{3,1},{4,6},{5,7},{6,4},{7,5},{8,10},{9,11},{10,... | collective-permute-start | bytes 12296 | tf_op jit(solution)/shard_map/ppermute | solution.py:315
  48.9 9.8 %collective-permute-start.10 = (bf16[1,32,64]{2,1,0:T(8,128)(2,1)S(1)}, bf16[1,32,64]{2,1,0:T(8,128)(2,1)S(1)}, u32[]{:S(2)}, u32[]{:S(2)}) collective-permute-start(bf16[1,32,64]{2,1,0:T(8,128)(2,1)S(1)} %bitcast.133), channel_id=1, source_target_pairs={{0,3},{1,2},{2,1},{3,0},{4,7},{5,6},{6,5},{7,4},{8,11},{9,10},{10,... | collective-permute-start | bytes 12296 | tf_op jit(solution)/shard_map/ppermute | solution.py:315
  58.7 9.9 %collective-permute-start.15 = (bf16[2,32,3072]{2,1,0:T(8,128)(2,1)S(1)}, bf16[2,32,3072]{2,1,0:T(8,128)(2,1)S(1)}, u32[]{:S(2)}, u32[]{:S(2)}) collective-permute-start(bf16[2,32,3072]{2,1,0:T(8,128)(2,1)S(1)} %get-tuple-element.65), channel_id=1, source_target_pairs={{0,1},{1,0},{2,3},{3,2},{4,5},{5,4},{6,7},{7,6},{8,9},{9,8},{10,11... | collective-permute-start | bytes 1179656 | tf_op jit(solution)/shard_map/ppermute | solution.py:315
  59.3 7.7 %collective-permute-start.14 = (bf16[4,1,32,64]{3,2,1,0:T(8,128)(2,1)S(1)}, bf16[4,1,32,64]{3,2,1,0:T(8,128)(2,1)S(1)}, u32[]{:S(2)}, u32[]{:S(2)}) collective-permute-start(bf16[4,1,32,64]{3,2,1,0:T(8,128)(2,1)S(1)} %get-tuple-element.78.refs_4_), channel_id=1, source_target_pairs={{0,4},{4,0},{8,12},{12,8},{16,20},{20,16},{24,28},{28,24},{1,5},{5... | collective-permute-start | bytes 49160 | tf_op jit(solution)/shard_map/ppermute | solution.py:315
  68.7 15.6 %copy-start.4 = (f32[2,32,3072]{2,1,0:T(8,128)}, f32[2,32,3072]{2,1,0:T(8,128)S(1)}, u32[]{:S(2)}) copy-start(f32[2,32,3072]{2,1,0:T(8,128)S(1)} %convert_add_fusion.3) | copy-start | bytes 2359300
  68.7 15.5 %collective-permute-start.17 = (bf16[2,32,3072]{2,1,0:T(8,128)(2,1)S(1)}, bf16[2,32,3072]{2,1,0:T(8,128)(2,1)S(1)}, u32[]{:S(2)}, u32[]{:S(2)}) collective-permute-start(bf16[2,32,3072]{2,1,0:T(8,128)(2,1)S(1)} %get-tuple-element.71), channel_id=1, source_target_pairs={{0,1},{1,0},{2,3},{3,2},{4,5},{5,4},{6,7},{7,6},{8,9},{9,8},{10,11... | collective-permute-start | bytes 1179656 | tf_op jit(solution)/shard_map/ppermute | solution.py:315
  69.4 16.2 %slice-start = ((s8[4718592]{0:T(1024)(128)(4,1)}), s8[4194304]{0:T(1024)(128)(4,1)S(1)}, s32[]{:S(2)}) async-start(s8[4718592]{0:T(1024)(128)(4,1)} %bitcast.108), calls=%async_computation | async-start | bytes 8388608
  69.7 15.8 %slice-start.1 = ((s8[4718592]{0:T(1024)(128)(4,1)}), s8[524288]{0:T(1024)(128)(4,1)S(1)}, s32[]{:S(2)}) async-start(s8[4718592]{0:T(1024)(128)(4,1)} %bitcast.108), calls=%async_computation.1 | async-start | bytes 1048576
  69.7 15.8 %collective-permute-start.19 = (bf16[2,4,1,32,64]{4,3,1,2,0:T(8,128)(2,1)S(1)}, bf16[2,4,1,32,64]{4,3,1,2,0:T(8,128)(2,1)S(1)}, u32[]{:S(2)}, u32[]{:S(2)}) collective-permute-start(bf16[2,4,1,32,64]{4,3,1,2,0:T(8,128)(2,1)S(1)} %pad_maximum_fusion.4), channel_id=1, source_target_pairs={{0,8},{4,12},{8,0},{12,4},{16,24},{20,28},{24,16},{28,20},{1,9},{5... | collective-permute-start | bytes 98312 | tf_op jit(solution)/shard_map/ppermute | solution.py:315
  70.6 14.9 %collective-permute-start.20 = (bf16[2,4,1,32,64]{4,3,1,2,0:T(8,128)(2,1)S(1)}, bf16[2,4,1,32,64]{4,3,1,2,0:T(8,128)(2,1)S(1)}, u32[]{:S(2)}, u32[]{:S(2)}) collective-permute-start(bf16[2,4,1,32,64]{4,3,1,2,0:T(8,128)(2,1)S(1)} %pad_maximum_fusion.4), channel_id=1, source_target_pairs={{0,16},{4,20},{8,24},{12,28},{16,0},{20,4},{24,8},{28,12},{1,17},{... | collective-permute-start | bytes 98312 | tf_op jit(solution)/shard_map/ppermute | solution.py:315
  72.1 13.5 %collective-permute-start.21 = (bf16[2,4,1,32,64]{4,3,1,2,0:T(8,128)(2,1)S(1)}, bf16[2,4,1,32,64]{4,3,1,2,0:T(8,128)(2,1)S(1)}, u32[]{:S(2)}, u32[]{:S(2)}) collective-permute-start(bf16[2,4,1,32,64]{4,3,1,2,0:T(8,128)(2,1)S(1)} %pad_maximum_fusion.4), channel_id=1, source_target_pairs={{0,24},{4,28},{8,16},{12,20},{16,8},{20,12},{24,0},{28,4},{1,25},{... | collective-permute-start | bytes 98312 | tf_op jit(solution)/shard_map/ppermute | solution.py:315
  73.3 11.5 %collective-permute-start.16 = (bf16[1,32,3072]{2,1,0:T(8,128)(2,1)S(1)}, bf16[1,32,3072]{2,1,0:T(8,128)(2,1)S(1)}, u32[]{:S(2)}, u32[]{:S(2)}) collective-permute-start(bf16[1,32,3072]{2,1,0:T(8,128)(2,1)S(1)} %slice.170), channel_id=1, source_target_pairs={{0,2},{1,3},{2,0},{3,1},{4,6},{5,7},{6,4},{7,5},{8,10},{9,11},{10,... | collective-permute-start | bytes 589832 | tf_op jit(solution)/shard_map/ppermute | solution.py:315
  84.4 8.6 %copy-start.5 = (f32[2,32,3072]{2,1,0:T(8,128)}, f32[2,32,3072]{2,1,0:T(8,128)S(1)}, u32[]{:S(2)}) copy-start(f32[2,32,3072]{2,1,0:T(8,128)S(1)} %convert_add_fusion.2) | copy-start | bytes 2359300
  84.4 13.8 %collective-permute-start.18 = (bf16[2,32,3072]{2,1,0:T(8,128)(2,1)S(1)}, bf16[2,32,3072]{2,1,0:T(8,128)(2,1)S(1)}, u32[]{:S(2)}, u32[]{:S(2)}) collective-permute-start(bf16[2,32,3072]{2,1,0:T(8,128)(2,1)S(1)} %get-tuple-element.76), channel_id=1, source_target_pairs={{0,1},{1,0},{2,3},{3,2},{4,5},{5,4},{6,7},{7,6},{8,9},{9,8},{10,11... | collective-permute-start | bytes 1179656 | tf_op jit(solution)/shard_map/ppermute | solution.py:315
  85.3 13.1 %collective-permute-start.24 = (bf16[1,32,3072]{2,1,0:T(8,128)(2,1)S(1)}, bf16[1,32,3072]{2,1,0:T(8,128)(2,1)S(1)}, u32[]{:S(2)}, u32[]{:S(2)}) collective-permute-start(bf16[1,32,3072]{2,1,0:T(8,128)(2,1)S(1)} %slice.169), channel_id=1, source_target_pairs={{0,2},{1,3},{2,0},{3,1},{4,6},{5,7},{6,4},{7,5},{8,10},{9,11},{10,... | collective-permute-start | bytes 589832 | tf_op jit(solution)/shard_map/ppermute | solution.py:315
  93.0 20.9 %copy-start.7 = (f32[1,1,3072]{2,1,0:T(1,128)S(1)}, f32[1,1,3072]{2,1,0:T(1,128)}, u32[]{:S(2)}) copy-start(f32[1,1,3072]{2,1,0:T(1,128)} %get-tuple-element.100) | copy-start | bytes 36868
  98.3 13.5 %collective-permute-start.22 = (bf16[2,32,3072]{2,1,0:T(8,128)(2,1)S(1)}, bf16[2,32,3072]{2,1,0:T(8,128)(2,1)S(1)}, u32[]{:S(2)}, u32[]{:S(2)}) collective-permute-start(bf16[2,32,3072]{2,1,0:T(8,128)(2,1)S(1)} %get-tuple-element.82), channel_id=1, source_target_pairs={{0,1},{1,0},{2,3},{3,2},{4,5},{5,4},{6,7},{7,6},{8,9},{9,8},{10,11... | collective-permute-start | bytes 1179656 | tf_op jit(solution)/shard_map/ppermute | solution.py:315
  99.2 14.8 %collective-permute-start.25 = (bf16[1,32,3072]{2,1,0:T(8,128)(2,1)S(1)}, bf16[1,32,3072]{2,1,0:T(8,128)(2,1)S(1)}, u32[]{:S(2)}, u32[]{:S(2)}) collective-permute-start(bf16[1,32,3072]{2,1,0:T(8,128)(2,1)S(1)} %slice.168), channel_id=1, source_target_pairs={{0,2},{1,3},{2,0},{3,1},{4,6},{5,7},{6,4},{7,5},{8,10},{9,11},{10,... | collective-permute-start | bytes 589832 | tf_op jit(solution)/shard_map/ppermute | solution.py:315
  111.9 10.5 %collective-permute-start.23 = (bf16[1,32,3072]{2,1,0:T(8,128)(2,1)S(1)}, bf16[1,32,3072]{2,1,0:T(8,128)(2,1)S(1)}, u32[]{:S(2)}, u32[]{:S(2)}) collective-permute-start(bf16[1,32,3072]{2,1,0:T(8,128)(2,1)S(1)} %slice.167), channel_id=1, source_target_pairs={{0,2},{1,3},{2,0},{3,1},{4,6},{5,7},{6,4},{7,5},{8,10},{9,11},{10,... | collective-permute-start | bytes 589832 | tf_op jit(solution)/shard_map/ppermute | solution.py:315
  (12 other events, 62.9 us)

commit v4 on v3

--- a/solution.py
+++ b/solution.py
@@ -297,7 +297,7 @@
             pltpu.VMEM(out_weight.shape, bf16),
             pltpu.SemaphoreType.DMA((3,)),
         ],
-        compiler_params=pltpu.CompilerParams(vmem_limit_bytes=16 * 2**20 + 24 * nq * nk),
+        compiler_params=pltpu.CompilerParams(vmem_limit_bytes=46 * 2**20),
         cost_estimate=pl.CostEstimate(
             flops=2 * heads * (nk * 256 * 256 + 2 * nq * nk * head_dim * 2 + nq * head_dim * depth),
             bytes_accessed=heads * head_dim * depth * 2 + nq * depth * 3,

time: 125 us -> 120 us (0.960)
  local copies, waits for them, and re-layouts: 8.74 us -> 6.41 us
  Pallas kernels: 35.9 us -> 34.6 us
    unnamed x37 -> x31, local copies, waits for them, and re-layouts: 3.48 us -> 1.14 us
  transfers between devices with their start and end apart: 26 -> 26, of which waited for: 4 -> 4; matrix products, arithmetic and copies ran while one was open for 14% -> 15% of each run, Pallas kernels for 29% -> 29%
where the time goes in v4:
time: 120 us
  starting transfers between devices  38.4 us (32%)
  Pallas kernels  34.6 us (29%)
  waiting for transfers between devices  25.5 us (21%)
  matrix products  9.29 us (8%)
  local copies, waits for them, and re-layouts  6.41 us (5%)
  other arithmetic  5.22 us (4%)
    ppermute x22, starting transfers between devices, exchange(): return lax.ppermute(value, axis, [(i, i ^ bit) for i in range(count)])  31.3 us
    pallas_call x4, Pallas kernels, attend(): pl.pallas_call(functools.partial(attend_kernel, hp, head_dim, slot, slots...  28.6 us
    ppermute x22, waiting for transfers between devices, exchange(): return lax.ppermute(value, axis, [(i, i ^ bit) for i in range(count)])  25.5 us
    dot_general x1, matrix products, on_device(): folded = jnp.dot(lhs, qkv_weight, preferred_element_type=f32)  8.01 us
    pallas_call x1, Pallas kernels, encode(): pl.pallas_call(encode_kernel, grid=(6,), in_specs=[pl.BlockSpec(memory_sp...  6.02 us
    ppermute x1, starting transfers between devices, sides(): left = lax.ppermute(mid[-3:], 'col', [(i, i + 1) for i in range(nc - 1)])  3.15 us
  transfers between devices with their start and end apart: 26, of which 4 were waited for; matrix products, arithmetic and copies ran while one was open for 15% of the time, Pallas kernels for 29%

profile of v4, /device:TPU:0, one launch (start us, length us, event | category | flops | bytes accessed | tf_op | source)
XLA Modules:
  0.0 120.1 jit_solution(16231046312770404792)
XLA Ops:
  0.0 5.0 %collective-permute-start.6 = (bf16[3,32,64]{2,1,0:T(8,128)(2,1)}, bf16[3,32,64]{2,1,0:T(8,128)(2,1)S(1)}, u32[]{:S(2)}, u32[]{:S(2)}) collective-permute-start(bf16[3,32,64]{2,1,0:T(8,128)(2,1)} %bitcast.124), channel_id=1, source_target_pairs={{0,3},{1,2},{2,1},{3,0},{4,7},{5,6},{6,5},{7,4},{8,11},{9,10},{10,... | collective-permute-start | bytes 36872 | tf_op jit(solution)/shard_map/ppermute | solution.py:315
  5.7 1.0 copy.45
  6.7 1.3 %collective-permute-start.1 = (bf16[16,3,512]{2,1,0:T(4,128)(2,1)S(1)}, bf16[16,3,512]{2,1,0:T(4,128)(2,1)S(1)}, u32[]{:S(2)}, u32[]{:S(2)}) collective-permute-start(bf16[16,3,512]{2,1,0:T(4,128)(2,1)S(1)} %get-tuple-element.108), channel_id=1, source_target_pairs={{0,4},{4,8},{8,12},{12,16},{16,20},{20,24},{24,28},{1,5},{5,9},{9,... | collective-permute-start | bytes 147464 | tf_op jit(solution)/shard_map/ppermute | solution.py:104
  8.0 1.3 %collective-permute-start = (bf16[16,3,512]{2,1,0:T(4,128)(2,1)S(1)}, bf16[16,3,512]{2,1,0:T(4,128)(2,1)S(1)}, u32[]{:S(2)}, u32[]{:S(2)}) collective-permute-start(bf16[16,3,512]{2,1,0:T(4,128)(2,1)S(1)} %get-tuple-element.107), channel_id=1, source_target_pairs={{4,0},{8,4},{12,8},{16,12},{20,16},{24,20},{28,24},{5,1},{9,5},{13... | collective-permute-start | bytes 147464 | tf_op jit(solution)/shard_map/ppermute | solution.py:105
  10.6 1.4 %fusion.29 = (f32[1,3,3072]{2,0,1:T(1,128)S(1)}, f32[1,3,3072]{2,0,1:T(1,128)S(1)}, f32[1,3,3072]{2,0,1:T(1,128)S(1)}, f32[1,3,3072]{2,0,1:T(1,128)S(1)}) fusion(f32[4,3,3072]{2,0,1:T(4,128)} %param.20), kind=kLoop, calls=%fused_computation.83 | loop fusion | bytes 294912 | tf_op jit(solution)/shard_map/slice | solution.py:381
  13.9 0.8 fusion.26
  14.7 3.1 %collective-permute-start.7 = (bf16[4,3,32,64]{3,2,1,0:T(8,128)(2,1)S(1)}, bf16[4,3,32,64]{3,2,1,0:T(8,128)(2,1)S(1)}, u32[]{:S(2)}, u32[]{:S(2)}) collective-permute-start(bf16[4,3,32,64]{3,2,1,0:T(8,128)(2,1)S(1)} %get-tuple-element.72.refs_4_), channel_id=1, source_target_pairs={{0,4},{4,0},{8,12},{12,8},{16,20},{20,16},{24,28},{28,24},{1,5},{5... | collective-permute-start | bytes 147464 | tf_op jit(solution)/shard_map/ppermute | solution.py:315
  17.9 3.1 %collective-permute-start.2 = (bf16[3,16,512]{2,1,0:T(8,128)(2,1)S(1)}, bf16[3,16,512]{2,1,0:T(8,128)(2,1)S(1)}, u32[]{:S(2)}, u32[]{:S(2)}) collective-permute-start(bf16[3,16,512]{2,1,0:T(8,128)(2,1)S(1)} %get-tuple-element.96), channel_id=1, source_target_pairs={{0,1},{1,2},{2,3},{4,5},{5,6},{6,7},{8,9},{9,10},{10,11},{12,13},{... | collective-permute-start | bytes 147464 | tf_op jit(solution)/shard_map/ppermute | solution.py:113
  21.1 1.3 %collective-permute-start.3 = (bf16[3,16,512]{2,1,0:T(8,128)(2,1)S(1)}, bf16[3,16,512]{2,1,0:T(8,128)(2,1)S(1)}, u32[]{:S(2)}, u32[]{:S(2)}) collective-permute-start(bf16[3,16,512]{2,1,0:T(8,128)(2,1)S(1)} %get-tuple-element.95), channel_id=1, source_target_pairs={{1,0},{2,1},{3,2},{5,4},{6,5},{7,6},{9,8},{10,9},{11,10},{13,12},{... | collective-permute-start | bytes 147464 | tf_op jit(solution)/shard_map/ppermute | solution.py:114
  22.6 1.7 %collective-permute-start.11 = (bf16[2,4,3,32,64]{4,3,2,1,0:T(8,128)(2,1)S(1)}, bf16[2,4,3,32,64]{4,3,2,1,0:T(8,128)(2,1)S(1)}, u32[]{:S(2)}, u32[]{:S(2)}) collective-permute-start(bf16[2,4,3,32,64]{4,3,2,1,0:T(8,128)(2,1)S(1)} %pad_maximum_fusion.2.refs_0_), channel_id=1, source_target_pairs={{0,8},{4,12},{8,0},{12,4},{16,24},{20,28},{24,16},{28,20},{1,9},{5... | collective-permute-start | bytes 294920 | tf_op jit(solution)/shard_map/ppermute | solution.py:315
  24.3 1.5 %collective-permute-start.12 = (bf16[2,4,3,32,64]{4,3,2,1,0:T(8,128)(2,1)S(1)}, bf16[2,4,3,32,64]{4,3,2,1,0:T(8,128)(2,1)S(1)}, u32[]{:S(2)}, u32[]{:S(2)}) collective-permute-start(bf16[2,4,3,32,64]{4,3,2,1,0:T(8,128)(2,1)S(1)} %pad_maximum_fusion.2.refs_0_), channel_id=1, source_target_pairs={{0,16},{4,20},{8,24},{12,28},{16,0},{20,4},{24,8},{28,12},{1,17},{... | collective-permute-start | bytes 294920 | tf_op jit(solution)/shard_map/ppermute | solution.py:315
  25.8 0.9 collective-permute-start.13
  27.0 0.9 convert_bitcast_fusion
  28.3 8.0 %fusion.refs_6_.refs_7_ = f32[272,2304]{1,0:T(8,128)S(1)} fusion(bf16[3072,2304]{1,0:T(8,128)(2,1)} %param.22, bf16[4,3072]{1,0:T(4,128)(2,1)S(1)} %fusion.18, bf16[4,3072]{1,0:T(4,128)(2,1)S(1)} %bitcast.142, bf16[256,3072]{1,0:T(8,128)(2,1)S(1)} %bitcast.117, bf16[272]{0:T(512)(128)(2,1)S(1)} %pad.17.clone), kind=kOutput, calls=%fused_computation.2 | convolution fusion | flops 3857055744 | bytes 18285088 | tf_op jit(solution)/shard_map/dot_general | solution.py:390
  36.4 6.0 %shard_map.127 = f32[16,8,16]{2,1,0:T(8,128)S(1)} custom-call(s32[4]{0:T(128)S(1)} %pad_add_fusion.place_ref, bf16[3,16,512]{2,1,0:T(8,128)(2,1)S(1)} %collective-permute-done.2.left_ref, bf16[16,16,512]{2,1,0:T(8,128)(2,1)S(1)} %pad_maximum_fusion.1.mid_ref, bf16[3,16,512]{2,1,0:T(8,128)(2,1)S(1)} %collective-permute-done.3.right_ref, ...), custom_call_target="tpu_custom_call" | custom-call | flops 3373793280 | bytes 10616832 | tf_op jit(solution)/shard_map/pallas_call | solution.py:137
  43.2 2.7 %collective-permute-start.8 = (bf16[1,32,64]{2,1,0:T(8,128)(2,1)S(1)}, bf16[1,32,64]{2,1,0:T(8,128)(2,1)S(1)}, u32[]{:S(2)}, u32[]{:S(2)}) collective-permute-start(bf16[1,32,64]{2,1,0:T(8,128)(2,1)S(1)} %bitcast.129), channel_id=1, source_target_pairs={{0,1},{1,0},{2,3},{3,2},{4,5},{5,4},{6,7},{7,6},{8,9},{9,8},{10,11... | collective-permute-start | bytes 12296 | tf_op jit(solution)/shard_map/ppermute | solution.py:315
  45.8 3.0 %collective-permute-start.9 = (bf16[1,32,64]{2,1,0:T(8,128)(2,1)S(1)}, bf16[1,32,64]{2,1,0:T(8,128)(2,1)S(1)}, u32[]{:S(2)}, u32[]{:S(2)}) collective-permute-start(bf16[1,32,64]{2,1,0:T(8,128)(2,1)S(1)} %bitcast.130), channel_id=1, source_target_pairs={{0,2},{1,3},{2,0},{3,1},{4,6},{5,7},{6,4},{7,5},{8,10},{9,11},{10,... | collective-permute-start | bytes 12296 | tf_op jit(solution)/shard_map/ppermute | solution.py:315
  48.8 7.1 %shard_map.128 = (f32[2,32,3072]{2,1,0:T(8,128)S(1)}, bf16[2,32,3072]{2,1,0:T(8,128)(2,1)S(1)}) custom-call(bf16[2,4,3,32,64]{4,3,2,1,0:T(8,128)(2,1)S(1)} %pad_maximum_fusion.2.refs_0_, bf16[2,4,3,32,64]{4,3,2,1,0:T(8,128)(2,1)S(1)} %collective-permute-done.11.refs_1_, bf16[2,4,3,32,64]{4,3,2,1,0:T(8,128)(2,1)S(1)} %collective-permute-done.12.refs_2_, ...), custom_call_target="tpu_custom_call" | custom-call | flops 2214592512 | bytes 5898240 | tf_op jit(solution)/shard_map/pallas_call | solution.py:276
  56.7 7.3 %shard_map.129 = (f32[2,32,3072]{2,1,0:T(8,128)S(1)}, bf16[2,32,3072]{2,1,0:T(8,128)(2,1)S(1)}) custom-call(bf16[2,4,3,32,64]{4,3,2,1,0:T(8,128)(2,1)S(1)} %pad_maximum_fusion.2.refs_0_, bf16[2,4,3,32,64]{4,3,2,1,0:T(8,128)(2,1)S(1)} %collective-permute-done.11.refs_1_, bf16[2,4,3,32,64]{4,3,2,1,0:T(8,128)(2,1)S(1)} %collective-permute-done.12.refs_2_, ...), custom_call_target="tpu_custom_call" | custom-call | flops 2214592512 | bytes 5898240 | tf_op jit(solution)/shard_map/pallas_call | solution.py:276
  64.0 1.8 %collective-permute-done.15 = bf16[2,32,3072]{2,1,0:T(8,128)(2,1)S(1)} collective-permute-done((bf16[2,32,3072]{2,1,0:T(8,128)(2,1)S(1)}, bf16[2,32,3072]{2,1,0:T(8,128)(2,1)S(1)}, u32[]{:S(2)}, u32[]{:S(2)}) %collective-permute-start.15) | collective-permute-done | bytes 393248 | tf_op jit(solution)/shard_map/ppermute | solution.py:315
  67.0 0.9 collective-permute-start.19
  67.9 1.5 %collective-permute-start.20 = (bf16[2,4,1,32,64]{4,3,1,2,0:T(8,128)(2,1)S(1)}, bf16[2,4,1,32,64]{4,3,1,2,0:T(8,128)(2,1)S(1)}, u32[]{:S(2)}, u32[]{:S(2)}) collective-permute-start(bf16[2,4,1,32,64]{4,3,1,2,0:T(8,128)(2,1)S(1)} %pad_maximum_fusion.4), channel_id=1, source_target_pairs={{0,16},{4,20},{8,24},{12,28},{16,0},{20,4},{24,8},{28,12},{1,17},{... | collective-permute-start | bytes 98312 | tf_op jit(solution)/shard_map/ppermute | solution.py:315
  69.4 1.2 collective-permute-start.21
  70.5 3.6 %collective-permute-start.16 = (bf16[1,32,3072]{2,1,0:T(8,128)(2,1)S(1)}, bf16[1,32,3072]{2,1,0:T(8,128)(2,1)S(1)}, u32[]{:S(2)}, u32[]{:S(2)}) collective-permute-start(bf16[1,32,3072]{2,1,0:T(8,128)(2,1)S(1)} %slice.170), channel_id=1, source_target_pairs={{0,2},{1,3},{2,0},{3,1},{4,6},{5,7},{6,4},{7,5},{8,10},{9,11},{10,... | collective-permute-start | bytes 589832 | tf_op jit(solution)/shard_map/ppermute | solution.py:315
  74.1 7.1 %shard_map.130 = (f32[2,32,3072]{2,1,0:T(8,128)S(1)}, bf16[2,32,3072]{2,1,0:T(8,128)(2,1)S(1)}) custom-call(bf16[2,4,3,32,64]{4,3,2,1,0:T(8,128)(2,1)S(1)} %pad_maximum_fusion.2.refs_0_, bf16[2,4,3,32,64]{4,3,2,1,0:T(8,128)(2,1)S(1)} %collective-permute-done.11.refs_1_, bf16[2,4,3,32,64]{4,3,2,1,0:T(8,128)(2,1)S(1)} %collective-permute-done.12.refs_2_, ...), custom_call_target="tpu_custom_call" | custom-call | flops 2214592512 | bytes 5898240 | tf_op jit(solution)/shard_map/pallas_call | solution.py:276
  82.6 7.1 %shard_map.131 = (f32[2,32,3072]{2,1,0:T(8,128)S(1)}, bf16[2,32,3072]{2,1,0:T(8,128)(2,1)S(1)}) custom-call(bf16[2,4,1,32,64]{4,3,2,1,0:T(8,128)(2,1)S(1)} %bitcast.112, bf16[2,4,1,32,64]{4,3,2,1,0:T(8,128)(2,1)S(1)} %bitcast.114, bf16[2,4,1,32,64]{4,3,2,1,0:T(8,128)(2,1)S(1)} %bitcast.115, bf16[2,4,1,32,64]{4,3,2,1,0:T(8,128)(2,1)S(1)} %bitcast.116, ...), custom_call_target="tpu_custom_call" | custom-call | flops 2214592512 | bytes 5898240 | tf_op jit(solution)/shard_map/pallas_call | solution.py:276
  89.7 5.1 %collective-permute-done.18 = bf16[2,32,3072]{2,1,0:T(8,128)(2,1)S(1)} collective-permute-done((bf16[2,32,3072]{2,1,0:T(8,128)(2,1)S(1)}, bf16[2,32,3072]{2,1,0:T(8,128)(2,1)S(1)}, u32[]{:S(2)}, u32[]{:S(2)}) %collective-permute-start.18) | collective-permute-done | bytes 393248 | tf_op jit(solution)/shard_map/ppermute | solution.py:315
  95.8 2.2 %collective-permute-start.25 = (bf16[1,32,3072]{2,1,0:T(8,128)(2,1)S(1)}, bf16[1,32,3072]{2,1,0:T(8,128)(2,1)S(1)}, u32[]{:S(2)}, u32[]{:S(2)}) collective-permute-start(bf16[1,32,3072]{2,1,0:T(8,128)(2,1)S(1)} %slice.168), channel_id=1, source_target_pairs={{0,2},{1,3},{2,0},{3,1},{4,6},{5,7},{6,4},{7,5},{8,10},{9,11},{10,... | collective-permute-start | bytes 589832 | tf_op jit(solution)/shard_map/ppermute | solution.py:315
  98.0 10.3 %collective-permute-done.22 = bf16[2,32,3072]{2,1,0:T(8,128)(2,1)S(1)} collective-permute-done((bf16[2,32,3072]{2,1,0:T(8,128)(2,1)S(1)}, bf16[2,32,3072]{2,1,0:T(8,128)(2,1)S(1)}, u32[]{:S(2)}, u32[]{:S(2)}) %collective-permute-start.22) | collective-permute-done | bytes 393248 | tf_op jit(solution)/shard_map/ppermute | solution.py:315
  108.4 1.5 %collective-permute-start.23 = (bf16[1,32,3072]{2,1,0:T(8,128)(2,1)S(1)}, bf16[1,32,3072]{2,1,0:T(8,128)(2,1)S(1)}, u32[]{:S(2)}, u32[]{:S(2)}) collective-permute-start(bf16[1,32,3072]{2,1,0:T(8,128)(2,1)S(1)} %slice.167), channel_id=1, source_target_pairs={{0,2},{1,3},{2,0},{3,1},{4,6},{5,7},{6,4},{7,5},{8,10},{9,11},{10,... | collective-permute-start | bytes 589832 | tf_op jit(solution)/shard_map/ppermute | solution.py:315
  110.0 8.3 %collective-permute-done.23 = bf16[1,32,3072]{2,1,0:T(8,128)(2,1)S(1)} collective-permute-done((bf16[1,32,3072]{2,1,0:T(8,128)(2,1)S(1)}, bf16[1,32,3072]{2,1,0:T(8,128)(2,1)S(1)}, u32[]{:S(2)}, u32[]{:S(2)}) %collective-permute-start.23) | collective-permute-done | bytes 196640 | tf_op jit(solution)/shard_map/ppermute | solution.py:315
  118.6 1.5 %copy.27 = bf16[32,4,3072]{2,1,0:T(4,128)(2,1)} copy(bf16[32,4,3072]{2,0,1:T(8,128)(2,1)S(1)} %pad_maximum_fusion) | data formatting | bytes 1572864 | tf_op jit(solution)/shard_map/stack | solution.py:454
  (110 shorter events, 10.0 us)
Async XLA Ops:
  0.0 26.7 %copy-start.1 = (bf16[64,3072]{1,0:T(8,128)(2,1)S(1)}, bf16[64,3072]{1,0:T(8,128)(2,1)}, u32[]{:S(2)}) copy-start(bf16[64,3072]{1,0:T(8,128)(2,1)} %param.21) | copy-start | bytes 1179652
  0.0 13.9 %collective-permute-start.6 = (bf16[3,32,64]{2,1,0:T(8,128)(2,1)}, bf16[3,32,64]{2,1,0:T(8,128)(2,1)S(1)}, u32[]{:S(2)}, u32[]{:S(2)}) collective-permute-start(bf16[3,32,64]{2,1,0:T(8,128)(2,1)} %bitcast.124), channel_id=1, source_target_pairs={{0,3},{1,2},{2,1},{3,0},{4,7},{5,6},{6,5},{7,4},{8,11},{9,10},{10,... | collective-permute-start | bytes 36872 | tf_op jit(solution)/shard_map/ppermute | solution.py:315
  5.1 8.8 %collective-permute-start.5 = (bf16[3,32,64]{2,1,0:T(8,128)(2,1)}, bf16[3,32,64]{2,1,0:T(8,128)(2,1)S(1)}, u32[]{:S(2)}, u32[]{:S(2)}) collective-permute-start(bf16[3,32,64]{2,1,0:T(8,128)(2,1)} %bitcast.125), channel_id=1, source_target_pairs={{0,2},{1,3},{2,0},{3,1},{4,6},{5,7},{6,4},{7,5},{8,10},{9,11},{10,... | collective-permute-start | bytes 36872 | tf_op jit(solution)/shard_map/ppermute | solution.py:315
  5.1 8.9 %collective-permute-start.4 = (bf16[3,32,64]{2,1,0:T(8,128)(2,1)}, bf16[3,32,64]{2,1,0:T(8,128)(2,1)S(1)}, u32[]{:S(2)}, u32[]{:S(2)}) collective-permute-start(bf16[3,32,64]{2,1,0:T(8,128)(2,1)} %bitcast.126), channel_id=1, source_target_pairs={{0,1},{1,0},{2,3},{3,2},{4,5},{5,4},{6,7},{7,6},{8,9},{9,8},{10,11... | collective-permute-start | bytes 36872 | tf_op jit(solution)/shard_map/ppermute | solution.py:315
  6.7 11.0 %collective-permute-start.1 = (bf16[16,3,512]{2,1,0:T(4,128)(2,1)S(1)}, bf16[16,3,512]{2,1,0:T(4,128)(2,1)S(1)}, u32[]{:S(2)}, u32[]{:S(2)}) collective-permute-start(bf16[16,3,512]{2,1,0:T(4,128)(2,1)S(1)} %get-tuple-element.108), channel_id=1, source_target_pairs={{0,4},{4,8},{8,12},{12,16},{16,20},{20,24},{24,28},{1,5},{5,9},{9,... | collective-permute-start | bytes 147464 | tf_op jit(solution)/shard_map/ppermute | solution.py:104
  8.0 9.8 %collective-permute-start = (bf16[16,3,512]{2,1,0:T(4,128)(2,1)S(1)}, bf16[16,3,512]{2,1,0:T(4,128)(2,1)S(1)}, u32[]{:S(2)}, u32[]{:S(2)}) collective-permute-start(bf16[16,3,512]{2,1,0:T(4,128)(2,1)S(1)} %get-tuple-element.107), channel_id=1, source_target_pairs={{4,0},{8,4},{12,8},{16,12},{20,16},{24,20},{28,24},{5,1},{9,5},{13... | collective-permute-start | bytes 147464 | tf_op jit(solution)/shard_map/ppermute | solution.py:105
  14.7 7.7 %collective-permute-start.7 = (bf16[4,3,32,64]{3,2,1,0:T(8,128)(2,1)S(1)}, bf16[4,3,32,64]{3,2,1,0:T(8,128)(2,1)S(1)}, u32[]{:S(2)}, u32[]{:S(2)}) collective-permute-start(bf16[4,3,32,64]{3,2,1,0:T(8,128)(2,1)S(1)} %get-tuple-element.72.refs_4_), channel_id=1, source_target_pairs={{0,4},{4,0},{8,12},{12,8},{16,20},{20,16},{24,28},{28,24},{1,5},{5... | collective-permute-start | bytes 147464 | tf_op jit(solution)/shard_map/ppermute | solution.py:315
  17.9 18.4 %collective-permute-start.2 = (bf16[3,16,512]{2,1,0:T(8,128)(2,1)S(1)}, bf16[3,16,512]{2,1,0:T(8,128)(2,1)S(1)}, u32[]{:S(2)}, u32[]{:S(2)}) collective-permute-start(bf16[3,16,512]{2,1,0:T(8,128)(2,1)S(1)} %get-tuple-element.96), channel_id=1, source_target_pairs={{0,1},{1,2},{2,3},{4,5},{5,6},{6,7},{8,9},{9,10},{10,11},{12,13},{... | collective-permute-start | bytes 147464 | tf_op jit(solution)/shard_map/ppermute | solution.py:113
  21.1 15.2 %collective-permute-start.3 = (bf16[3,16,512]{2,1,0:T(8,128)(2,1)S(1)}, bf16[3,16,512]{2,1,0:T(8,128)(2,1)S(1)}, u32[]{:S(2)}, u32[]{:S(2)}) collective-permute-start(bf16[3,16,512]{2,1,0:T(8,128)(2,1)S(1)} %get-tuple-element.95), channel_id=1, source_target_pairs={{1,0},{2,1},{3,2},{5,4},{6,5},{7,6},{9,8},{10,9},{11,10},{13,12},{... | collective-permute-start | bytes 147464 | tf_op jit(solution)/shard_map/ppermute | solution.py:114
  22.6 26.2 %collective-permute-start.11 = (bf16[2,4,3,32,64]{4,3,2,1,0:T(8,128)(2,1)S(1)}, bf16[2,4,3,32,64]{4,3,2,1,0:T(8,128)(2,1)S(1)}, u32[]{:S(2)}, u32[]{:S(2)}) collective-permute-start(bf16[2,4,3,32,64]{4,3,2,1,0:T(8,128)(2,1)S(1)} %pad_maximum_fusion.2.refs_0_), channel_id=1, source_target_pairs={{0,8},{4,12},{8,0},{12,4},{16,24},{20,28},{24,16},{28,20},{1,9},{5... | collective-permute-start | bytes 294920 | tf_op jit(solution)/shard_map/ppermute | solution.py:315
  24.3 24.5 %collective-permute-start.12 = (bf16[2,4,3,32,64]{4,3,2,1,0:T(8,128)(2,1)S(1)}, bf16[2,4,3,32,64]{4,3,2,1,0:T(8,128)(2,1)S(1)}, u32[]{:S(2)}, u32[]{:S(2)}) collective-permute-start(bf16[2,4,3,32,64]{4,3,2,1,0:T(8,128)(2,1)S(1)} %pad_maximum_fusion.2.refs_0_), channel_id=1, source_target_pairs={{0,16},{4,20},{8,24},{12,28},{16,0},{20,4},{24,8},{28,12},{1,17},{... | collective-permute-start | bytes 294920 | tf_op jit(solution)/shard_map/ppermute | solution.py:315
  25.8 23.0 %collective-permute-start.13 = (bf16[2,4,3,32,64]{4,3,2,1,0:T(8,128)(2,1)S(1)}, bf16[2,4,3,32,64]{4,3,2,1,0:T(8,128)(2,1)S(1)}, u32[]{:S(2)}, u32[]{:S(2)}) collective-permute-start(bf16[2,4,3,32,64]{4,3,2,1,0:T(8,128)(2,1)S(1)} %pad_maximum_fusion.2.refs_0_), channel_id=1, source_target_pairs={{0,24},{4,28},{8,16},{12,20},{16,8},{20,12},{24,0},{28,4},{1,25},{... | collective-permute-start | bytes 294920 | tf_op jit(solution)/shard_map/ppermute | solution.py:315
  28.2 8.1 %slice-start = ((s8[4718592]{0:T(1024)(128)(4,1)}), s8[4194304]{0:T(1024)(128)(4,1)S(1)}, s32[]{:S(2)}) async-start(s8[4718592]{0:T(1024)(128)(4,1)} %bitcast.108), calls=%async_computation | async-start | bytes 8388608
  28.2 8.1 %slice-start.2 = ((s8[4718592]{0:T(1024)(128)(4,1)}), s8[4194304]{0:T(1024)(128)(4,1)S(1)}, s32[]{:S(2)}) async-start(s8[4718592]{0:T(1024)(128)(4,1)} %bitcast.110), calls=%async_computation.2 | async-start | bytes 8388608
  43.2 12.8 %collective-permute-start.8 = (bf16[1,32,64]{2,1,0:T(8,128)(2,1)S(1)}, bf16[1,32,64]{2,1,0:T(8,128)(2,1)S(1)}, u32[]{:S(2)}, u32[]{:S(2)}) collective-permute-start(bf16[1,32,64]{2,1,0:T(8,128)(2,1)S(1)} %bitcast.129), channel_id=1, source_target_pairs={{0,1},{1,0},{2,3},{3,2},{4,5},{5,4},{6,7},{7,6},{8,9},{9,8},{10,11... | collective-permute-start | bytes 12296 | tf_op jit(solution)/shard_map/ppermute | solution.py:315
  45.8 10.1 %collective-permute-start.9 = (bf16[1,32,64]{2,1,0:T(8,128)(2,1)S(1)}, bf16[1,32,64]{2,1,0:T(8,128)(2,1)S(1)}, u32[]{:S(2)}, u32[]{:S(2)}) collective-permute-start(bf16[1,32,64]{2,1,0:T(8,128)(2,1)S(1)} %bitcast.130), channel_id=1, source_target_pairs={{0,2},{1,3},{2,0},{3,1},{4,6},{5,7},{6,4},{7,5},{8,10},{9,11},{10,... | collective-permute-start | bytes 12296 | tf_op jit(solution)/shard_map/ppermute | solution.py:315
  48.8 7.2 %collective-permute-start.10 = (bf16[1,32,64]{2,1,0:T(8,128)(2,1)S(1)}, bf16[1,32,64]{2,1,0:T(8,128)(2,1)S(1)}, u32[]{:S(2)}, u32[]{:S(2)}) collective-permute-start(bf16[1,32,64]{2,1,0:T(8,128)(2,1)S(1)} %bitcast.131), channel_id=1, source_target_pairs={{0,3},{1,2},{2,1},{3,0},{4,7},{5,6},{6,5},{7,4},{8,11},{9,10},{10,... | collective-permute-start | bytes 12296 | tf_op jit(solution)/shard_map/ppermute | solution.py:315
  56.0 9.9 %collective-permute-start.15 = (bf16[2,32,3072]{2,1,0:T(8,128)(2,1)S(1)}, bf16[2,32,3072]{2,1,0:T(8,128)(2,1)S(1)}, u32[]{:S(2)}, u32[]{:S(2)}) collective-permute-start(bf16[2,32,3072]{2,1,0:T(8,128)(2,1)S(1)} %get-tuple-element.65), channel_id=1, source_target_pairs={{0,1},{1,0},{2,3},{3,2},{4,5},{5,4},{6,7},{7,6},{8,9},{9,8},{10,11... | collective-permute-start | bytes 1179656 | tf_op jit(solution)/shard_map/ppermute | solution.py:315
  56.6 7.4 %collective-permute-start.14 = (bf16[4,1,32,64]{3,2,1,0:T(8,128)(2,1)S(1)}, bf16[4,1,32,64]{3,2,1,0:T(8,128)(2,1)S(1)}, u32[]{:S(2)}, u32[]{:S(2)}) collective-permute-start(bf16[4,1,32,64]{3,2,1,0:T(8,128)(2,1)S(1)} %get-tuple-element.78.refs_4_), channel_id=1, source_target_pairs={{0,4},{4,0},{8,12},{12,8},{16,20},{20,16},{24,28},{28,24},{1,5},{5... | collective-permute-start | bytes 49160 | tf_op jit(solution)/shard_map/ppermute | solution.py:315
  66.0 15.2 %copy-start.3 = (f32[2,32,3072]{2,1,0:T(8,128)}, f32[2,32,3072]{2,1,0:T(8,128)S(1)}, u32[]{:S(2)}) copy-start(f32[2,32,3072]{2,1,0:T(8,128)S(1)} %convert_add_fusion.3) | copy-start | bytes 2359300
  66.0 15.2 %collective-permute-start.17 = (bf16[2,32,3072]{2,1,0:T(8,128)(2,1)S(1)}, bf16[2,32,3072]{2,1,0:T(8,128)(2,1)S(1)}, u32[]{:S(2)}, u32[]{:S(2)}) collective-permute-start(bf16[2,32,3072]{2,1,0:T(8,128)(2,1)S(1)} %get-tuple-element.71), channel_id=1, source_target_pairs={{0,1},{1,0},{2,3},{3,2},{4,5},{5,4},{6,7},{7,6},{8,9},{9,8},{10,11... | collective-permute-start | bytes 1179656 | tf_op jit(solution)/shard_map/ppermute | solution.py:315
  67.0 15.6 %collective-permute-start.19 = (bf16[2,4,1,32,64]{4,3,1,2,0:T(8,128)(2,1)S(1)}, bf16[2,4,1,32,64]{4,3,1,2,0:T(8,128)(2,1)S(1)}, u32[]{:S(2)}, u32[]{:S(2)}) collective-permute-start(bf16[2,4,1,32,64]{4,3,1,2,0:T(8,128)(2,1)S(1)} %pad_maximum_fusion.4), channel_id=1, source_target_pairs={{0,8},{4,12},{8,0},{12,4},{16,24},{20,28},{24,16},{28,20},{1,9},{5... | collective-permute-start | bytes 98312 | tf_op jit(solution)/shard_map/ppermute | solution.py:315
  67.9 14.7 %collective-permute-start.20 = (bf16[2,4,1,32,64]{4,3,1,2,0:T(8,128)(2,1)S(1)}, bf16[2,4,1,32,64]{4,3,1,2,0:T(8,128)(2,1)S(1)}, u32[]{:S(2)}, u32[]{:S(2)}) collective-permute-start(bf16[2,4,1,32,64]{4,3,1,2,0:T(8,128)(2,1)S(1)} %pad_maximum_fusion.4), channel_id=1, source_target_pairs={{0,16},{4,20},{8,24},{12,28},{16,0},{20,4},{24,8},{28,12},{1,17},{... | collective-permute-start | bytes 98312 | tf_op jit(solution)/shard_map/ppermute | solution.py:315
  69.4 13.2 %collective-permute-start.21 = (bf16[2,4,1,32,64]{4,3,1,2,0:T(8,128)(2,1)S(1)}, bf16[2,4,1,32,64]{4,3,1,2,0:T(8,128)(2,1)S(1)}, u32[]{:S(2)}, u32[]{:S(2)}) collective-permute-start(bf16[2,4,1,32,64]{4,3,1,2,0:T(8,128)(2,1)S(1)} %pad_maximum_fusion.4), channel_id=1, source_target_pairs={{0,24},{4,28},{8,16},{12,20},{16,8},{20,12},{24,0},{28,4},{1,25},{... | collective-permute-start | bytes 98312 | tf_op jit(solution)/shard_map/ppermute | solution.py:315
  70.5 11.2 %collective-permute-start.16 = (bf16[1,32,3072]{2,1,0:T(8,128)(2,1)S(1)}, bf16[1,32,3072]{2,1,0:T(8,128)(2,1)S(1)}, u32[]{:S(2)}, u32[]{:S(2)}) collective-permute-start(bf16[1,32,3072]{2,1,0:T(8,128)(2,1)S(1)} %slice.170), channel_id=1, source_target_pairs={{0,2},{1,3},{2,0},{3,1},{4,6},{5,7},{6,4},{7,5},{8,10},{9,11},{10,... | collective-permute-start | bytes 589832 | tf_op jit(solution)/shard_map/ppermute | solution.py:315
  81.3 8.3 %copy-start.4 = (f32[2,32,3072]{2,1,0:T(8,128)}, f32[2,32,3072]{2,1,0:T(8,128)S(1)}, u32[]{:S(2)}) copy-start(f32[2,32,3072]{2,1,0:T(8,128)S(1)} %convert_add_fusion.2) | copy-start | bytes 2359300
  81.4 13.4 %collective-permute-start.18 = (bf16[2,32,3072]{2,1,0:T(8,128)(2,1)S(1)}, bf16[2,32,3072]{2,1,0:T(8,128)(2,1)S(1)}, u32[]{:S(2)}, u32[]{:S(2)}) collective-permute-start(bf16[2,32,3072]{2,1,0:T(8,128)(2,1)S(1)} %get-tuple-element.76), channel_id=1, source_target_pairs={{0,1},{1,0},{2,3},{3,2},{4,5},{5,4},{6,7},{7,6},{8,9},{9,8},{10,11... | collective-permute-start | bytes 1179656 | tf_op jit(solution)/shard_map/ppermute | solution.py:315
  82.3 12.7 %collective-permute-start.24 = (bf16[1,32,3072]{2,1,0:T(8,128)(2,1)S(1)}, bf16[1,32,3072]{2,1,0:T(8,128)(2,1)S(1)}, u32[]{:S(2)}, u32[]{:S(2)}) collective-permute-start(bf16[1,32,3072]{2,1,0:T(8,128)(2,1)S(1)} %slice.169), channel_id=1, source_target_pairs={{0,2},{1,3},{2,0},{3,1},{4,6},{5,7},{6,4},{7,5},{8,10},{9,11},{10,... | collective-permute-start | bytes 589832 | tf_op jit(solution)/shard_map/ppermute | solution.py:315
  89.7 20.2 %copy-start.6 = (f32[1,1,3072]{2,1,0:T(1,128)S(1)}, f32[1,1,3072]{2,1,0:T(1,128)}, u32[]{:S(2)}) copy-start(f32[1,1,3072]{2,1,0:T(1,128)} %get-tuple-element.100) | copy-start | bytes 36868
  94.9 13.4 %collective-permute-start.22 = (bf16[2,32,3072]{2,1,0:T(8,128)(2,1)S(1)}, bf16[2,32,3072]{2,1,0:T(8,128)(2,1)S(1)}, u32[]{:S(2)}, u32[]{:S(2)}) collective-permute-start(bf16[2,32,3072]{2,1,0:T(8,128)(2,1)S(1)} %get-tuple-element.82), channel_id=1, source_target_pairs={{0,1},{1,0},{2,3},{3,2},{4,5},{5,4},{6,7},{7,6},{8,9},{9,8},{10,11... | collective-permute-start | bytes 1179656 | tf_op jit(solution)/shard_map/ppermute | solution.py:315
  95.8 14.2 %collective-permute-start.25 = (bf16[1,32,3072]{2,1,0:T(8,128)(2,1)S(1)}, bf16[1,32,3072]{2,1,0:T(8,128)(2,1)S(1)}, u32[]{:S(2)}, u32[]{:S(2)}) collective-permute-start(bf16[1,32,3072]{2,1,0:T(8,128)(2,1)S(1)} %slice.168), channel_id=1, source_target_pairs={{0,2},{1,3},{2,0},{3,1},{4,6},{5,7},{6,4},{7,5},{8,10},{9,11},{10,... | collective-permute-start | bytes 589832 | tf_op jit(solution)/shard_map/ppermute | solution.py:315
  108.4 9.9 %collective-permute-start.23 = (bf16[1,32,3072]{2,1,0:T(8,128)(2,1)S(1)}, bf16[1,32,3072]{2,1,0:T(8,128)(2,1)S(1)}, u32[]{:S(2)}, u32[]{:S(2)}) collective-permute-start(bf16[1,32,3072]{2,1,0:T(8,128)(2,1)S(1)} %slice.167), channel_id=1, source_target_pairs={{0,2},{1,3},{2,0},{3,1},{4,6},{5,7},{6,4},{7,5},{8,10},{9,11},{10,... | collective-permute-start | bytes 589832 | tf_op jit(solution)/shard_map/ppermute | solution.py:315
  (9 other events, 44.9 us)
